TPU v7x, 128 devices: a whole 4x4x4 slice. The times are simulated.
128 devices in a mesh: row: 16 (over y, x), col: 8 (over z, core).
Axes of the slice: x: 4, y: 4, z: 4, core: 2. Of those that a mesh axis runs over, the one named last changes fastest.
Arguments:
- noise: float32 [512, 18, 2048], P('col', None, 'row'), may hold values from -6 to 6
- factor: bfloat16 [13, 2048, 3, 10240], P(None, 'row', None, 'col'), may hold values from -0.03125 to 0.03125
- dinv: bfloat16 [3, 10240, 5, 2048], P(None, 'col', None, 'row'), as said below
Outputs:
- solved: bfloat16 [3, 10240, 512], P(None, 'col')
- remaining: float32 [512, 18, 2048], P('col', None, 'row')
Inputs may be any that keep to these rules, and one draw needn't show every extreme that they name: dinv[s], read as a 10240 x 10240 matrix, is lower triangular with a positive diagonal.
All inputs are finite; a program needn't handle non-finite values.
Results may differ from a plain program's by a relative error of at most 0.007.
Values may be sent and summed in bfloat16 or wider, within the bound.
No kernel may reach another device: no remote copies, remote signals or barrier semaphores. Data moves between devices by JAX's collectives and lax.ppermute only.
A program may use at most 128 MiB of HBM per device.

v0:
```python
import jax
import jax.numpy as jnp
from jax import lax
from jax.sharding import PartitionSpec as P


def local(noise, factor, dinv):
    step_count = dinv.shape[0]
    rounds = dinv.shape[2]
    work = noise
    solved_list = []
    for step_idx in range(step_count):
        current = work[:, step_idx * rounds : (step_idx + 1) * rounds, :].astype(jnp.bfloat16)
        gathered = lax.all_gather(current, "col", axis=0, tiled=True).astype(jnp.float32)
        inverse = dinv[step_idx].astype(jnp.float32)
        partial_sum = lax.dot_general(inverse, gathered, (((1, 2), (1, 2)), ((), ())))
        solution = lax.psum(partial_sum, "row").astype(jnp.bfloat16)
        solved_list.append(solution)
        solution_wide = solution.astype(jnp.float32)
        panel_rows = factor[step_idx * rounds :, :, step_idx, :].astype(jnp.float32)
        reduced = lax.psum_scatter(
            lax.dot_general(solution_wide, panel_rows, (((0,), (2,)), ((), ()))),
            "col",
            scatter_dimension=0,
            tiled=True,
        )
        work = work.at[:, (step_idx + 1) * rounds :, :].add(-reduced)
    return (jnp.stack(solved_list), work)


def solution(mesh):
    placed = (P("col", None, "row"), P(None, "row", None, "col"), P(None, "col", None, "row"))
    return jax.shard_map(
        local,
        mesh=mesh,
        in_specs=placed,
        out_specs=(P(None, "col", None), P("col", None, "row")),
        check_vma=False,
    )
```

profile of v0, /device:TPU:1, one launch (start us, length us, event | category | flops | bytes accessed | tf_op | source)
XLA Modules:
  0.0 460.4 jit_solution(17969831107973538819)
XLA Ops:
  7.2 0.0 reduce-scatter.4.cloned.1.call-start
  7.2 1.1 copy.36
  8.3 15.8 %all_gather.9 = bf16[512,5,128]{2,0,1:T(8,128)(2,1)S(1)} all-gather(bf16[64,5,128]{2,0,1:T(8,128)(2,1)S(1)} %slice.157), channel_id=1, replica_groups=mesh['row'=16,'col'=8] {'col'}, dimensions={0}, use_global_device_ids=true | all-gather | bytes 737280 | tf_op jit(solution)/shard_map/all_gather | solution.py:14
  24.1 4.1 convolution_bitcast_fusion.2
  28.2 84.4 %all-reduce.3 = bf16[1280,512]{1,0:T(8,128)(2,1)S(1)} all-reduce(f32[1280,512]{1,0:T(8,128)} %convolution_bitcast_fusion.2), channel_id=1, replica_groups=mesh['row'=16,'col'=8] {'row'}, use_global_device_ids=true, to_apply=%region_0.0 | all-reduce | flops 655360 | bytes 3932160 | tf_op jit(solution)/shard_map/psum | solution.py:17
  112.6 6.5 %fusion = f32[512,13,128]{2,0,1:T(8,128)} fusion(bf16[13,128,3,1280]{3,1,2,0:T(8,128)(2,1)} %param.10, bf16[1280,512]{1,0:T(8,128)(2,1)S(1)} %all-reduce.3), kind=kOutput, calls=%fused_computation | convolution fusion | flops 2181038080 | bytes 8978432 | tf_op jit(solution)/shard_map/dot_general | solution.py:22
  119.1 0.0 reduce-scatter.4.cloned.1.call-update
  119.1 0.0 reduce-scatter.6.cloned.1.call-start
  119.2 40.8 %reduce-scatter.4.cloned.1.call-done = f32[64,13,128]{2,0,1:T(8,128)} async-done(((f32[512,13,128]{2,0,1:T(8,128)}), f32[64,13,128]{2,0,1:T(8,128)}) %reduce-scatter.4.cloned.1.call-update) | async-done | bytes 426000 | tf_op jit(solution)/shard_map/reduce_scatter | solution.py:21
  160.0 1.2 constant_dynamic-update-slice_fusion.1
  161.1 0.0 copy-start.1
  161.2 16.8 %all_gather.10 = bf16[512,5,128]{2,0,1:T(8,128)(2,1)S(1)} all-gather(bf16[64,5,128]{2,0,1:T(8,128)(2,1)S(1)} %slice.156), channel_id=1, replica_groups=mesh['row'=16,'col'=8] {'col'}, dimensions={0}, use_global_device_ids=true | all-gather | bytes 737280 | tf_op jit(solution)/shard_map/all_gather | solution.py:14
  178.0 0.0 copy-done.1
  178.0 4.1 convolution_bitcast_fusion.1
  182.1 84.0 %all-reduce.4 = bf16[1280,512]{1,0:T(8,128)(2,1)S(1)} all-reduce(f32[1280,512]{1,0:T(8,128)} %convolution_bitcast_fusion.1), channel_id=1, replica_groups=mesh['row'=16,'col'=8] {'row'}, use_global_device_ids=true, to_apply=%region_2.0 | all-reduce | flops 655360 | bytes 3932160 | tf_op jit(solution)/shard_map/psum | solution.py:17
  266.2 4.6 %fusion.3 = f32[512,8,128]{2,0,1:T(8,128)} fusion(bf16[13,128,3,1280]{3,1,2,0:T(8,128)(2,1)} %param.10, bf16[1280,512]{1,0:T(8,128)(2,1)S(1)} %all-reduce.4), kind=kOutput, calls=%fused_computation.7 | convolution fusion | flops 1342177280 | bytes 6029312 | tf_op jit(solution)/shard_map/dot_general | solution.py:22
  270.8 0.0 reduce-scatter.6.cloned.1.call-update
  270.8 0.0 reduce-scatter.8.cloned.1.call-start
  270.9 36.6 %reduce-scatter.6.cloned.1.call-done = f32[64,8,128]{2,0,1:T(8,128)} async-done(((f32[512,8,128]{2,0,1:T(8,128)}), f32[64,8,128]{2,0,1:T(8,128)}) %reduce-scatter.6.cloned.1.call-update) | async-done | bytes 262160 | tf_op jit(solution)/shard_map/reduce_scatter | solution.py:21
  307.5 1.1 constant_dynamic-update-slice_fusion
  308.6 16.9 %all_gather.11 = bf16[512,5,128]{2,0,1:T(8,128)(2,1)S(1)} all-gather(bf16[64,5,128]{2,0,1:T(8,128)(2,1)S(1)} %slice.155), channel_id=1, replica_groups=mesh['row'=16,'col'=8] {'col'}, dimensions={0}, use_global_device_ids=true | all-gather | bytes 737280 | tf_op jit(solution)/shard_map/all_gather | solution.py:14
  325.5 4.1 convolution_bitcast_fusion
  329.7 84.5 %all-reduce.5 = bf16[1280,512]{1,0:T(8,128)(2,1)} all-reduce(f32[1280,512]{1,0:T(8,128)} %convolution_bitcast_fusion), channel_id=1, replica_groups=mesh['row'=16,'col'=8] {'row'}, use_global_device_ids=true, to_apply=%region_4.0 | all-reduce | flops 655360 | bytes 3932160 | tf_op jit(solution)/shard_map/psum | solution.py:17
  414.2 3.4 fusion.12
  417.6 0.0 reduce-scatter.8.cloned.1.call-update
  417.6 3.2 pad_maximum_fusion
  420.8 31.3 %reduce-scatter.8.cloned.1.call-done = f32[64,3,128]{2,0,1:T(8,128)} async-done(((f32[512,3,128]{2,0,1:T(8,128)}), f32[64,3,128]{2,0,1:T(8,128)}) %reduce-scatter.8.cloned.1.call-update) | async-done | bytes 98320 | tf_op jit(solution)/shard_map/reduce_scatter | solution.py:21
  452.2 0.9 fusion.21
  453.1 0.0 copy-start
  453.1 0.8 copy-done
  (3 shorter events, 0.0 us)
Async XLA Ops:
  7.2 152.8 %reduce-scatter.4.cloned.1.call-start = ((), (), s32[]{:S(2)}) async-start(), calls=%async_computation.3 | async-start | bytes 3833856 | tf_op jit(solution)/shard_map/reduce_scatter | solution.py:21
  119.1 188.4 %reduce-scatter.6.cloned.1.call-start = ((), (), s32[]{:S(2)}) async-start(), calls=%async_computation.4 | async-start | bytes 2359296 | tf_op jit(solution)/shard_map/reduce_scatter | solution.py:21
  161.1 16.8 %copy-start.1 = (f32[64,13,128]{2,0,1:T(8,128)}, f32[64,13,128]{2,0,1:T(8,128)S(1)}, u32[]{:S(2)}) copy-start(f32[64,13,128]{2,0,1:T(8,128)S(1)} %get-tuple-element.41) | copy-start | bytes 1277956
  270.8 181.4 %reduce-scatter.8.cloned.1.call-start = ((), (), s32[]{:S(2)}) async-start(), calls=%async_computation.5 | async-start | bytes 884736 | tf_op jit(solution)/shard_map/reduce_scatter | solution.py:21
  453.1 0.8 copy-start
Sparse Core Ops, SparseCore 0:
  119.3 40.6 reduce-scatter.3
  270.9 36.5 reduce-scatter.5
  417.7 34.4 reduce-scatter.7
where the time goes:
time: 463 us; the launch traced here: 460 us
  blocking collectives  302 us (65%)
  waiting for transfers between devices  109 us (24%)
  matrix products  27 us (6%)
  between operations  13.8 us (3%)
  other arithmetic  6.37 us (1%)
    psum x3, blocking collectives, local(): solution = lax.psum(partial_sum, 'row').astype(jnp.bfloat16)  253 us
    reduce_scatter x3, waiting for transfers between devices, local(): lax.psum_scatter(lax.dot_general(solution_wide, panel_rows, (((0,), (2,))...  109 us
    all_gather x3, blocking collectives, local(): lax.all_gather(current, 'col', axis=0, tiled=True).astype(jnp.float32)  49.5 us
    dot_general x3, matrix products, local(): lax.dot_general(solution_wide, panel_rows, (((0,), (2,)), ((), ())))  14.6 us
    dot_general x3, matrix products, local(): lax.dot_general(inverse, gathered, (((1, 2), (1, 2)), ((), ())))  12.4 us
  transfers between devices with their start and end apart: 3, of which 3 were waited for; matrix products, arithmetic and copies ran while one was open for 1% of the time, Pallas kernels for 0%

commit v1 on v0

v1 whole, which is shorter than its diff:
```python
import jax
import jax.numpy as jnp
from jax import lax
from jax.sharding import PartitionSpec as P

BF16 = jnp.bfloat16
F32 = jnp.float32


def gather(block, axis, size):
    copies = jnp.broadcast_to(block[None], (size,) + block.shape)
    return lax.all_to_all(copies, axis, 0, 0, tiled=True)


def reduce_parts(parts, axis):
    received = lax.all_to_all(parts.astype(BF16), axis, 0, 0, tiled=True)
    return jnp.sum(received.astype(F32), axis=0)


def local(noise, factor, dinv):
    steps, width, rounds, lanes = dinv.shape
    n_row = lax.axis_size("row")
    n_col = lax.axis_size("col")
    total = noise.shape[1]
    vecs = noise.shape[0] * n_col
    solved_list = []
    done = [noise[:, :rounds, :]]
    current = noise[:, :rounds, :]
    for s in range(steps):
        everyone = lax.all_gather(current.astype(BF16), "col", axis=0, tiled=True)
        partial = lax.dot_general(
            dinv[s], everyone, (((1, 2), (1, 2)), ((), ())), preferred_element_type=F32
        )
        own = reduce_parts(partial.reshape(n_row, width // n_row, vecs), "row")
        solved = gather(own.astype(BF16), "row", n_row).reshape(width, vecs)
        solved_list.append(solved)
        first = (s + 1) * rounds
        last = min(first + rounds, total)
        update = 0.0
        for t in range(s + 1):
            update = update + lax.dot_general(
                solved_list[t],
                factor[first - rounds : last - rounds, :, t, :],
                (((0,), (2,)), ((), ())),
                preferred_element_type=F32,
            )
        reduced = reduce_parts(update.reshape(n_col, vecs // n_col, last - first, lanes), "col")
        current = noise[:, first:last, :] - reduced
        done.append(current)
    return jnp.stack(solved_list), jnp.concatenate(done, axis=1)


def solution(mesh):
    placed = (P("col", None, "row"), P(None, "row", None, "col"), P(None, "col", None, "row"))
    return jax.shard_map(
        local,
        mesh=mesh,
        in_specs=placed,
        out_specs=(P(None, "col", None), P("col", None, "row")),
        check_vma=False,
    )
```

time: 463 us -> 259 us (0.56)
  blocking collectives: 302 us -> 192 us
  waiting for transfers between devices: 109 us -> 17.9 us
  between operations: 13.8 us -> 0.83 us
  starting transfers between devices: 0.12 us -> 11.1 us
  matrix products: 27 us -> 21.4 us
  local copies, waits for them, and re-layouts: 1.92 us -> 7.04 us
    psum x3 -> x0, blocking collectives: 253 us -> none  [local(): solution = lax.psum(partial_sum, 'row').astype(jnp.bfloat16)]
    all_to_all x0 -> x7, blocking collectives: none -> 149 us  [the longest x5 105 us: reduce_parts(): received = lax.all_to_all(parts.astype(BF16), axis, 0, 0, tiled=True)]
    reduce_scatter x3 -> x0, waiting for transfers between devices: 109 us -> none  [local(): lax.psum_scatter(lax.dot_general(solution_wide, panel_rows, (((0,), (2,))...]
    all_to_all x0 -> x2, waiting for transfers between devices: none -> 17.9 us  [the longest x1 13.1 us: gather(): return lax.all_to_all(copies, axis, 0, 0, tiled=True)]
    all_to_all x0 -> x2, starting transfers between devices: none -> 11.1 us  [the longest x1 6.57 us: reduce_parts(): received = lax.all_to_all(parts.astype(BF16), axis, 0, 0, tiled=True)]
    all_gather x3, blocking collectives: 49.5 us -> 43.7 us  [local(): everyone = lax.all_gather(current.astype(BF16), 'col', axis=0, tiled=True)]
    dot_general x6 -> x9, matrix products: 27 us -> 21.4 us  [the longest x6 16.7 us: local(): lax.dot_general(solved_list[t], factor[first - rounds:last - rounds, :, t...]
  transfers between devices with their start and end apart: 3 -> 2, of which waited for: 3 -> 2; matrix products, arithmetic and copies ran while one was open for 1% -> 3% of each run, Pallas kernels for 0% -> 0%
where the time goes in v1:
time: 259 us
  blocking collectives  192 us (74%)
  matrix products  21.4 us (8%)
  waiting for transfers between devices  17.9 us (7%)
  starting transfers between devices  11.1 us (4%)
  other arithmetic  7.88 us (3%)
  local copies, waits for them, and re-layouts  7.04 us (3%)
    all_to_all x5, blocking collectives, reduce_parts(): received = lax.all_to_all(parts.astype(BF16), axis, 0, 0, tiled=True)  105 us
    all_gather x3, blocking collectives, local(): everyone = lax.all_gather(current.astype(BF16), 'col', axis=0, tiled=True)  43.7 us
    all_to_all x2, blocking collectives, gather(): return lax.all_to_all(copies, axis, 0, 0, tiled=True)  43.3 us
    dot_general x6, matrix products, local(): lax.dot_general(solved_list[t], factor[first - rounds:last - rounds, :, t...  16.7 us
    all_to_all x1, waiting for transfers between devices, gather(): return lax.all_to_all(copies, axis, 0, 0, tiled=True)  13.1 us
    all_to_all x1, starting transfers between devices, reduce_parts(): received = lax.all_to_all(parts.astype(BF16), axis, 0, 0, tiled=True)  6.57 us
  transfers between devices with their start and end apart: 2, of which 2 were waited for; matrix products, arithmetic and copies ran while one was open for 3% of the time, Pallas kernels for 0%

profile of v1, /device:TPU:1, one launch (start us, length us, event | category | flops | bytes accessed | tf_op | source)
XLA Modules:
  0.0 258.5 jit_solution(16801590991782297439)
XLA Ops:
  0.6 0.0 slice-start.4
  0.6 1.1 slice.95
  1.7 15.8 %all_gather.9 = bf16[512,5,128]{2,0,1:T(8,128)(2,1)S(1)} all-gather(bf16[64,5,128]{2,0,1:T(8,128)(2,1)S(1)} %slice.95), channel_id=1, replica_groups=mesh['row'=16,'col'=8] {'col'}, dimensions={0}, use_global_device_ids=true | all-gather | bytes 737280 | tf_op jit(solution)/shard_map/all_gather | solution.py:30
  17.5 0.0 slice-done.4
  17.5 1.2 bitcast_convert_fusion
  18.7 26.2 %all_to_all.45 = bf16[16,80,512]{2,1,0:T(8,128)(2,1)S(1)} all-to-all(bf16[16,80,512]{2,1,0:T(8,128)(2,1)S(1)} %bitcast_convert_fusion), channel_id=1, replica_groups=mesh['row'=16,'col'=8] {'row'}, dimensions={0} | all-to-all | bytes 2621440 | tf_op jit(solution)/shard_map/all_to_all | solution.py:16
  44.9 0.2 reduce_sum.63
  45.1 0.1 broadcast_in_dim.6
  45.2 21.7 %all_to_all.46 = bf16[16,80,512]{2,1,0:T(8,128)(2,1)S(1)} all-to-all(bf16[16,80,512]{2,1,0:T(8,128)(2,1)S(1)} %broadcast_in_dim.6), channel_id=1, replica_groups=mesh['row'=16,'col'=8] {'row'}, dimensions={0} | all-to-all | bytes 2621440 | tf_op jit(solution)/shard_map/all_to_all | solution.py:12
  66.9 0.0 slice-start
  66.9 0.6 copy.29
  67.5 0.0 slice-start.1
  67.6 2.8 %fusion.23 = bf16[8,64,5,128]{3,1,2,0:T(8,128)(2,1)S(1)} fusion(bf16[8,64,1280,1]{2,1,3,0:T(8,128)(2,1)S(1)} %bitcast.115, bf16[13,128,3,1280]{3,1,2,0:T(8,128)(2,1)} %param.4), kind=kOutput, calls=%fused_computation.23 | convolution fusion | flops 839188480 | bytes 3604480 | tf_op jit(solution)/shard_map/dot_general | solution.py:41
  70.4 0.0 copy-start.2
  70.4 17.1 %all_to_all.47 = bf16[8,64,5,128]{3,1,2,0:T(8,128)(2,1)S(1)} all-to-all(bf16[8,64,5,128]{3,1,2,0:T(8,128)(2,1)S(1)} %fusion.23), channel_id=1, replica_groups=mesh['row'=16,'col'=8] {'col'}, dimensions={0} | all-to-all | bytes 1310720 | tf_op jit(solution)/shard_map/all_to_all | solution.py:16
  87.5 0.1 convert_reduce_fusion.1
  87.6 0.0 copy-done.2
  87.7 13.9 %all_gather.10 = bf16[512,5,128]{2,0,1:T(8,128)(2,1)S(1)} all-gather(bf16[64,5,128]{2,0,1:T(8,128)(2,1)S(1)} %get-tuple-element.4), channel_id=1, replica_groups=mesh['row'=16,'col'=8] {'col'}, dimensions={0}, use_global_device_ids=true | all-gather | bytes 737280 | tf_op jit(solution)/shard_map/all_gather | solution.py:30
  101.6 0.0 slice-done
  101.6 0.0 slice-done.1
  101.6 2.3 fusion.3
  103.9 1.6 copy.31
  105.5 23.0 %all_to_all.48 = bf16[16,80,512]{2,1,0:T(8,128)(2,1)} all-to-all(bf16[16,80,512]{2,1,0:T(8,128)(2,1)S(1)} %bitcast.105), channel_id=1, replica_groups=mesh['row'=16,'col'=8] {'row'}, dimensions={0} | all-to-all | bytes 2621440 | tf_op jit(solution)/shard_map/all_to_all | solution.py:16
  128.5 1.5 reduce_sum.65
  130.0 0.1 broadcast_in_dim.7
  130.2 21.6 %all_to_all.49 = bf16[16,80,512]{2,1,0:T(8,128)(2,1)S(1)} all-to-all(bf16[16,80,512]{2,1,0:T(8,128)(2,1)S(1)} %broadcast_in_dim.7), channel_id=1, replica_groups=mesh['row'=16,'col'=8] {'row'}, dimensions={0} | all-to-all | bytes 2621440 | tf_op jit(solution)/shard_map/all_to_all | solution.py:12
  151.8 0.0 copy-start
  151.8 0.0 slice-start.2
  151.8 3.2 %fusion.4 = f32[512,5,128]{2,0,1:T(8,128)S(1)} fusion(bf16[1280,512,1]{1,0,2:T(8,128)(2,1)S(1)} %bitcast.107, bf16[13,128,3,1280]{3,1,2,0:T(8,128)(2,1)} %param.4), kind=kOutput, calls=%fused_computation.8 | convolution fusion | flops 838860800 | bytes 4259840 | tf_op jit(solution)/shard_map/dot_general | solution.py:41
  155.0 0.0 copy-done
  155.0 0.0 slice-start.3
  155.0 2.7 %fusion.20 = bf16[512,5,128]{2,0,1:T(8,128)(2,1)S(1)} fusion(f32[512,5,128]{2,0,1:T(8,128)S(1)} %fusion.4, bf16[1280,512,1]{1,0,2:T(8,128)(2,1)S(1)} %bitcast.102, bf16[13,128,3,1280]{3,1,2,0:T(8,128)(2,1)} %param.4), kind=kOutput, calls=%fused_computation.22 | convolution fusion | flops 839516160 | bytes 4915200 | tf_op jit(solution)/shard_map/dot_general | solution.py:41
  157.8 15.6 %all_to_all.50 = bf16[8,64,5,128]{3,1,2,0:T(8,128)(2,1)S(1)} all-to-all(bf16[8,64,5,128]{3,1,2,0:T(8,128)(2,1)S(1)} %copy.36), channel_id=1, replica_groups=mesh['row'=16,'col'=8] {'col'}, dimensions={0} | all-to-all | bytes 1310720 | tf_op jit(solution)/shard_map/all_to_all | solution.py:16
  173.4 0.1 convert_reduce_fusion
  173.5 0.7 fusion.35
  174.2 13.9 %all_gather.11 = bf16[512,5,128]{2,0,1:T(8,128)(2,1)S(1)} all-gather(bf16[64,5,128]{2,0,1:T(8,128)(2,1)S(1)} %get-tuple-element.2), channel_id=1, replica_groups=mesh['row'=16,'col'=8] {'col'}, dimensions={0}, use_global_device_ids=true | all-gather | bytes 737280 | tf_op jit(solution)/shard_map/all_gather | solution.py:30
  188.2 0.0 slice-done.2
  188.2 0.0 slice-done.3
  188.2 1.2 fusion.2
  189.4 1.5 copy.37
  190.9 23.4 %all_to_all.51 = bf16[16,80,512]{2,1,0:T(8,128)(2,1)S(1)} all-to-all(bf16[16,80,512]{2,1,0:T(8,128)(2,1)} %bitcast.106), channel_id=1, replica_groups=mesh['row'=16,'col'=8] {'row'}, dimensions={0} | all-to-all | bytes 2621440 | tf_op jit(solution)/shard_map/all_to_all | solution.py:16
  214.2 0.2 reduce_sum.67
  214.4 1.2 broadcast_in_dim.8
  215.6 4.6 %all-to-all-start.7 = ((bf16[16,80,512]{2,1,0:T(8,128)(2,1)}), bf16[16,80,512]{2,1,0:T(8,128)(2,1)}, u32[]{:S(2)}, u32[]{:S(2)}) async-start(bf16[16,80,512]{2,1,0:T(8,128)(2,1)} %broadcast_in_dim.8), calls=%async_computation.7 | async-start | bytes 2621440 | tf_op jit(solution)/shard_map/all_to_all | solution.py:12
  220.2 0.0 copy-start.1
  220.2 2.2 fusion.29
  222.4 0.0 copy-done.1
  222.4 3.0 %convolution_add_fusion.1 = f32[512,3,128]{2,0,1:T(8,128)} fusion(f32[512,3,128]{2,0,1:T(8,128)S(1)} %fusion.29, bf16[1280,512,1]{1,0,2:T(8,128)(2,1)S(1)} %bitcast.108, bf16[13,128,3,1280]{3,1,2,0:T(8,128)(2,1)} %param.4), kind=kOutput, calls=%fused_computation.27 | convolution fusion | flops 503513088 | bytes 3866624 | tf_op jit(solution)/shard_map/dot_general | solution.py:41
  225.4 13.1 %all-to-all-done.7 = bf16[16,80,512]{2,1,0:T(8,128)(2,1)} async-done(((bf16[16,80,512]{2,1,0:T(8,128)(2,1)}), bf16[16,80,512]{2,1,0:T(8,128)(2,1)}, u32[]{:S(2)}, u32[]{:S(2)}) %all-to-all-start.7) | async-done | bytes 1310752 | tf_op jit(solution)/shard_map/all_to_all | solution.py:12
  238.5 2.7 %fusion.26 = bf16[512,3,128]{2,0,1:T(8,128)(2,1)S(1)} fusion(f32[512,3,128]{2,0,1:T(8,128)} %convolution_add_fusion.1, bf16[1280,512,1]{1,0,2:T(8,128)(2,1)} %bitcast.33, bf16[13,128,3,1280]{3,1,2,0:T(8,128)(2,1)} %param.4), kind=kOutput, calls=%fused_computation.28 | convolution fusion | flops 503709696 | bytes 3473408 | tf_op jit(solution)/shard_map/dot_general | solution.py:41
  241.3 0.8 copy.44
  242.0 6.6 %all-to-all-start.8 = ((bf16[8,64,3,128]{3,1,2,0:T(8,128)(2,1)}), bf16[8,64,3,128]{3,1,2,0:T(8,128)(2,1)S(1)}, u32[]{:S(2)}, u32[]{:S(2)}) async-start(bf16[8,64,3,128]{3,1,2,0:T(8,128)(2,1)} %copy.44), calls=%async_computation.8 | async-start | bytes 786432 | tf_op jit(solution)/shard_map/all_to_all | solution.py:16
  248.6 0.0 copy-start.3
  248.6 3.3 %pad_maximum_fusion = bf16[3,1280,512]{2,1,0:T(8,128)(2,1)} fusion(bf16[1,1280,512]{2,1,0:T(8,128)(2,1)} %bitcast.27, bf16[1,1280,512]{2,1,0:T(8,128)(2,1)S(1)} %bitcast.109, bf16[1,1280,512]{2,1,0:T(8,128)(2,1)S(1)} %bitcast.104), kind=kLoop, calls=%fused_computation | loop fusion | flops 3932160 | bytes 7864320 | tf_op jit(solution)/shard_map/stack | solution.py:50
  251.9 4.8 %all-to-all-done.8 = bf16[8,64,3,128]{3,1,2,0:T(8,128)(2,1)S(1)} async-done(((bf16[8,64,3,128]{3,1,2,0:T(8,128)(2,1)}), bf16[8,64,3,128]{3,1,2,0:T(8,128)(2,1)S(1)}, u32[]{:S(2)}, u32[]{:S(2)}) %all-to-all-start.8) | async-done | bytes 393248 | tf_op jit(solution)/shard_map/all_to_all | solution.py:16
  256.7 0.1 convert_reduce_fusion.2
  256.8 0.9 slice_subtract_fusion.2
  257.7 0.0 copy-done.3
  257.7 0.9 pad_maximum_fusion.1
  (4 shorter events, 0.1 us)
Async XLA Ops:
  0.6 16.9 %slice-start.4 = ((bf16[3,1280,5,128]{3,1,2,0:T(8,128)(2,1)}), bf16[1,1280,5,128]{3,1,2,0:T(8,128)(2,1)S(1)}, s32[]{:S(2)}) async-start(bf16[3,1280,5,128]{3,1,2,0:T(8,128)(2,1)} %param.5), calls=%async_computation.13 | async-start | bytes 3276800 | tf_op jit(solution)/shard_map/slice | solution.py:32
  66.9 34.7 %slice-start = ((s8[4915200]{0:T(1024)(128)(4,1)}), s8[720896]{0:T(1024)(128)(4,1)S(1)}, s32[]{:S(2)}) async-start(s8[4915200]{0:T(1024)(128)(4,1)} %bitcast.110), calls=%async_computation.9 | async-start | bytes 1441792
  67.5 34.1 %slice-start.1 = ((s8[4915200]{0:T(1024)(128)(4,1)}), s8[4194304]{0:T(1024)(128)(4,1)S(1)}, s32[]{:S(2)}) async-start(s8[4915200]{0:T(1024)(128)(4,1)} %bitcast.110), calls=%async_computation.10 | async-start | bytes 8388608
  70.4 17.2 %copy-start.2 = (f32[64,18,128]{2,0,1:T(8,128)S(1)}, f32[64,18,128]{2,0,1:T(8,128)}, u32[]{:S(2)}) copy-start(f32[64,18,128]{2,0,1:T(8,128)} %param.3) | copy-start | bytes 1769476
  151.8 3.2 %copy-start = (bf16[16,80,512]{2,1,0:T(8,128)(2,1)}, bf16[16,80,512]{2,1,0:T(8,128)(2,1)S(1)}, u32[]{:S(2)}) copy-start(bf16[16,80,512]{2,1,0:T(8,128)(2,1)S(1)} %all_to_all.49) | copy-start | bytes 3932164
  151.8 36.4 %slice-start.2 = ((s8[4915200]{0:T(1024)(128)(4,1)}), s8[4194304]{0:T(1024)(128)(4,1)S(1)}, s32[]{:S(2)}) async-start(s8[4915200]{0:T(1024)(128)(4,1)} %bitcast.112), calls=%async_computation.11 | async-start | bytes 8388608
  155.0 33.2 %slice-start.3 = ((s8[4915200]{0:T(1024)(128)(4,1)}), s8[720896]{0:T(1024)(128)(4,1)S(1)}, s32[]{:S(2)}) async-start(s8[4915200]{0:T(1024)(128)(4,1)} %bitcast.112), calls=%async_computation.12 | async-start | bytes 1441792
  215.6 22.9 %all-to-all-start.7 = ((bf16[16,80,512]{2,1,0:T(8,128)(2,1)}), bf16[16,80,512]{2,1,0:T(8,128)(2,1)}, u32[]{:S(2)}, u32[]{:S(2)}) async-start(bf16[16,80,512]{2,1,0:T(8,128)(2,1)} %broadcast_in_dim.8), calls=%async_computation.7 | async-start | bytes 2621440 | tf_op jit(solution)/shard_map/all_to_all | solution.py:12
  220.2 2.2 copy-start.1
  242.0 14.7 %all-to-all-start.8 = ((bf16[8,64,3,128]{3,1,2,0:T(8,128)(2,1)}), bf16[8,64,3,128]{3,1,2,0:T(8,128)(2,1)S(1)}, u32[]{:S(2)}, u32[]{:S(2)}) async-start(bf16[8,64,3,128]{3,1,2,0:T(8,128)(2,1)} %copy.44), calls=%async_computation.8 | async-start | bytes 786432 | tf_op jit(solution)/shard_map/all_to_all | solution.py:16
  248.6 9.1 %copy-start.3 = (f32[64,5,128]{2,0,1:T(8,128)S(1)}, f32[64,5,128]{2,0,1:T(8,128)}, u32[]{:S(2)}) copy-start(f32[64,5,128]{2,0,1:T(8,128)} %get-tuple-element.3) | copy-start | bytes 491524

commit v2 on v0

v2 whole, which is shorter than its diff:
```python
import jax
import jax.numpy as jnp
from jax import lax
from jax.sharding import PartitionSpec as P

BF16 = jnp.bfloat16
F32 = jnp.float32


def swap(block, n_col, mask):
    return lax.ppermute(block, "col", [(c, c ^ mask) for c in range(n_col)])


def same_core(n_col):
    return [[2 * z + k for z in range(n_col // 2)] for k in range(2)]


def tied(first, *others):
    return lax.optimization_barrier((first,) + others)


def product(solved, block):
    out = lax.dot_general(solved, block, (((1,), (2,)), ((), ())), preferred_element_type=F32)
    return out.transpose(1, 0, 2)


def local(noise, factor, dinv):
    steps, width, rounds, lanes = dinv.shape
    n_row = lax.axis_size("row")
    n_col = lax.axis_size("col")
    n_z = n_col // 2
    chunk, total, _ = noise.shape
    vecs = chunk * n_col
    half = vecs // 2
    my_z = lax.axis_index("col") // 2
    my_core = lax.axis_index("col") % 2
    noise = noise.transpose(1, 0, 2)
    bounds = [(s * rounds, min((s + 1) * rounds, total)) for s in range(steps + 1)]

    first = noise[:rounds].astype(BF16)
    copies = jnp.broadcast_to(first[None], (n_z,) + first.shape)
    own = lax.all_to_all(copies, "col", 0, 0, tiled=True, axis_index_groups=same_core(n_col))
    own = own.transpose(1, 0, 2, 3).reshape(rounds, half, lanes)
    done = [noise[:rounds]]
    solved_list = []
    later = {}
    for s in range(steps):
        other = swap(own, n_col, 1)
        everyone = jnp.concatenate([own, other], axis=1)
        partial = lax.dot_general(
            everyone, dinv[s], (((0, 2), (1, 2)), ((), ())), preferred_element_type=F32
        ).astype(BF16)
        parts = partial.reshape(n_row, vecs // n_row, width)
        received = lax.all_to_all(parts, "row", 0, 0, tiled=True)
        if s > 0:
            for n in range(s + 1, steps + 1):
                lo, hi = bounds[n]
                block = factor[lo - rounds : hi - rounds, :, s - 1, :]
                more = product(solved_list[s - 1], block)
                later[n] = more if n not in later else later[n] + more
            received, *held = tied(received, *[later[n] for n in range(s + 1, steps + 1)])
            later.update(zip(range(s + 1, steps + 1), held))
        mine = jnp.sum(received.astype(F32), axis=0).astype(BF16)
        copies = jnp.broadcast_to(mine[None], (n_row,) + mine.shape)
        solved = lax.all_to_all(copies, "row", 0, 0, tiled=True).reshape(vecs, width)
        solved_list.append(solved)

        lo, hi = bounds[s + 1]
        block = factor[lo - rounds : hi - rounds, :, s, :]
        update_other = product(solved[half:], block)
        if s > 0:
            update_other = update_other + later[s + 1][:, half:]
        arrived = swap(update_other.astype(BF16), n_col, 1)
        update = product(solved[:half], block)
        if s > 0:
            update = update + later[s + 1][:, :half]
        update = update + arrived.astype(F32)
        if s + 1 < steps:
            spread = update.reshape(hi - lo, n_z, chunk, lanes)
            here = (lax.iota(jnp.int32, n_z) == my_z)[None, :, None, None]
            work = (jnp.where(here, noise[lo:hi][:, None], 0.0) - spread).reshape(hi - lo, half, lanes)
            work = work + swap(work.astype(BF16), n_col, 2).astype(F32)
            work = work + swap(work.astype(BF16), n_col, n_col - 2).astype(F32)
            done.append(lax.dynamic_slice_in_dim(work, my_z * chunk, chunk, axis=1))
            own = work.astype(BF16)
        else:
            parts = update.astype(BF16).reshape(hi - lo, n_z, chunk, lanes).transpose(1, 0, 2, 3)
            got = lax.all_to_all(parts, "col", 0, 0, tiled=True, axis_index_groups=same_core(n_col))
            done.append(noise[lo:hi] - jnp.sum(got.astype(F32), axis=0))

    outs = []
    for solved in solved_list:
        halves = solved.reshape(2, n_z, chunk, width)
        ordered = jnp.where(my_core == 0, halves, halves[::-1])
        outs.append(ordered.transpose(3, 1, 0, 2).reshape(width, vecs))
    return jnp.stack(outs), jnp.concatenate(done, axis=0).transpose(1, 0, 2)


def solution(mesh):
    placed = (P("col", None, "row"), P(None, "row", None, "col"), P(None, "col", None, "row"))
    return jax.shard_map(
        local,
        mesh=mesh,
        in_specs=placed,
        out_specs=(P(None, "col", None), P("col", None, "row")),
        check_vma=False,
    )
```

time: 463 us -> 267 us (0.58)
  blocking collectives: 302 us -> 60.4 us
  starting transfers between devices: 0.12 us -> 37 us
  local copies, waits for them, and re-layouts: 1.92 us -> 17.8 us
  between operations: 13.8 us -> 0.93 us
  matrix products: 27 us -> 32.2 us
  other arithmetic: 6.37 us -> 11 us
    psum x3 -> x0, blocking collectives: 253 us -> none  [local(): solution = lax.psum(partial_sum, 'row').astype(jnp.bfloat16)]
    reduce_scatter x3 -> x0, waiting for transfers between devices: 109 us -> none  [local(): lax.psum_scatter(lax.dot_general(solution_wide, panel_rows, (((0,), (2,))...]
    all_to_all x0 -> x5, waiting for transfers between devices: none -> 66.7 us  [the longest x2 34 us: local(): lax.all_to_all(copies, 'row', 0, 0, tiled=True).reshape(vecs, width)]
    all_to_all x0 -> x3, blocking collectives: none -> 60.4 us  [the longest x1 26 us: local(): received = lax.all_to_all(parts, 'row', 0, 0, tiled=True)]
    all_gather x3 -> x0, blocking collectives: 49.5 us -> none  [local(): lax.all_gather(current, 'col', axis=0, tiled=True).astype(jnp.float32)]
    ppermute x0 -> x10, waiting for transfers between devices: none -> 39.7 us  [swap(): return lax.ppermute(block, 'col', [(c, c ^ mask) for c in range(n_col)])]
    all_to_all x0 -> x5, starting transfers between devices: none -> 19.7 us  [the longest x2 8.28 us: local(): received = lax.all_to_all(parts, 'row', 0, 0, tiled=True)]
    ppermute x0 -> x10, starting transfers between devices: none -> 17.3 us  [swap(): return lax.ppermute(block, 'col', [(c, c ^ mask) for c in range(n_col)])]
  transfers between devices with their start and end apart: 3 -> 15, of which waited for: 3 -> 13; matrix products, arithmetic and copies ran while one was open for 1% -> 10% of each run, Pallas kernels for 0% -> 0%
where the time goes in v2:
time: 267 us; the launch traced here: 266 us
  waiting for transfers between devices  106 us (40%)
  blocking collectives  60.4 us (23%)
  starting transfers between devices  37 us (14%)
  matrix products  32.2 us (12%)
  local copies, waits for them, and re-layouts  17.8 us (7%)
  other arithmetic  11 us (4%)
    ppermute x10, waiting for transfers between devices, swap(): return lax.ppermute(block, 'col', [(c, c ^ mask) for c in range(n_col)])  39.7 us
    all_to_all x2, waiting for transfers between devices, local(): lax.all_to_all(copies, 'row', 0, 0, tiled=True).reshape(vecs, width)  34 us
    all_to_all x2, waiting for transfers between devices, local(): received = lax.all_to_all(parts, 'row', 0, 0, tiled=True)  32.7 us
    all_to_all x1, blocking collectives, local(): received = lax.all_to_all(parts, 'row', 0, 0, tiled=True)  26 us
    all_to_all x1, blocking collectives, local(): lax.all_to_all(copies, 'row', 0, 0, tiled=True).reshape(vecs, width)  22.6 us
    dot_general x9, matrix products, product(): lax.dot_general(solved, block, (((1,), (2,)), ((), ())), preferred_elemen...  22.1 us
    ppermute x10, starting transfers between devices, swap(): return lax.ppermute(block, 'col', [(c, c ^ mask) for c in range(n_col)])  17.3 us
    all_to_all x1, blocking collectives, local(): lax.all_to_all(copies, 'col', 0, 0, tiled=True, axis_index_groups=same_co...  11.8 us
  transfers between devices with their start and end apart: 15, of which 13 were waited for; matrix products, arithmetic and copies ran while one was open for 10% of the time, Pallas kernels for 0%

profile of v2, /device:TPU:1, one launch (start us, length us, event | category | flops | bytes accessed | tf_op | source)
XLA Modules:
  0.0 265.8 jit_solution(9024273863274108205)
XLA Ops:
  0.6 0.9 slice.207
  1.6 11.8 %all_to_all.40 = bf16[4,5,64,128]{3,2,1,0:T(8,128)(2,1)S(1)} all-to-all(bf16[4,5,64,128]{3,2,1,0:T(8,128)(2,1)S(1)} %broadcast_in_dim.65), channel_id=1, replica_groups={{0,2,4,6},{1,3,5,7},{8,10,12,14},{9,11,13,15},{16,18,20,22},{17,19,21,2..., dimensions={0} | all-to-all | bytes 655360 | tf_op jit(solution)/shard_map/all_to_all | solution.py:42
  13.5 2.2 collective-permute-start
  15.7 1.3 collective-permute-done
  17.0 2.6 fusion
  19.6 26.0 %all_to_all.41 = bf16[16,32,1280]{2,1,0:T(8,128)(2,1)S(1)} all-to-all(bf16[16,32,1280]{2,1,0:T(8,128)(2,1)S(1)} %bitcast.203), channel_id=1, replica_groups=mesh['row'=16,'col'=8] {'row'}, dimensions={0} | all-to-all | bytes 2621440 | tf_op jit(solution)/shard_map/all_to_all | solution.py:54
  45.6 0.2 reduce_sum.45
  45.8 1.2 broadcast_in_dim.66
  47.0 3.7 %all-to-all-start.2 = ((bf16[16,32,1280]{2,1,0:T(8,128)(2,1)}), bf16[16,32,1280]{2,1,0:T(8,128)(2,1)S(1)}, u32[]{:S(2)}, u32[]{:S(2)}) async-start(bf16[16,32,1280]{2,1,0:T(8,128)(2,1)} %broadcast_in_dim.66), calls=%async_computation.2 | async-start | bytes 2621440 | tf_op jit(solution)/shard_map/all_to_all | solution.py:65
  50.7 18.2 %all-to-all-done.2 = bf16[16,32,1280]{2,1,0:T(8,128)(2,1)S(1)} async-done(((bf16[16,32,1280]{2,1,0:T(8,128)(2,1)}), bf16[16,32,1280]{2,1,0:T(8,128)(2,1)S(1)}, u32[]{:S(2)}, u32[]{:S(2)}) %all-to-all-start.2) | async-done | bytes 1310752 | tf_op jit(solution)/shard_map/all_to_all | solution.py:65
  69.0 2.2 fusion.54
  71.2 3.5 %collective-permute-start.1 = (bf16[5,256,128]{2,1,0:T(8,128)(2,1)S(1)}, bf16[5,256,128]{2,1,0:T(8,128)(2,1)S(1)}, u32[]{:S(2)}, u32[]{:S(2)}) collective-permute-start(bf16[5,256,128]{2,1,0:T(8,128)(2,1)S(1)} %fusion.54), channel_id=1, source_target_pairs={{0,1},{1,0},{2,3},{3,2},{4,5},{5,4},{6,7},{7,6},{8,9},{9,8},{10,11... | collective-permute-start | bytes 983048 | tf_op jit(solution)/shard_map/ppermute | solution.py:11
  74.9 0.7 fusion.92
  75.6 0.4 collective-permute-done.1
  76.0 2.1 fusion.86
  78.2 0.3 collective-permute-start.2
  78.5 8.7 %collective-permute-done.2 = bf16[5,256,128]{2,1,0:T(8,128)(2,1)S(1)} collective-permute-done((bf16[5,256,128]{2,1,0:T(8,128)(2,1)S(1)}, bf16[5,256,128]{2,1,0:T(8,128)(2,1)S(1)}, u32[]{:S(2)}, u32[]{:S(2)}) %collective-permute-start.2) | collective-permute-done | bytes 327712 | tf_op jit(solution)/shard_map/ppermute | solution.py:11
  87.2 0.2 fusion.79
  87.4 0.9 collective-permute-start.3
  88.4 8.4 %collective-permute-done.3 = bf16[5,256,128]{2,1,0:T(8,128)(2,1)S(1)} collective-permute-done((bf16[5,256,128]{2,1,0:T(8,128)(2,1)S(1)}, bf16[5,256,128]{2,1,0:T(8,128)(2,1)S(1)}, u32[]{:S(2)}, u32[]{:S(2)}) %collective-permute-start.3) | collective-permute-done | bytes 327712 | tf_op jit(solution)/shard_map/ppermute | solution.py:11
  96.7 0.3 fusion.88
  97.0 2.2 collective-permute-start.4
  99.2 1.3 collective-permute-done.4
  100.5 3.7 %fusion.1 = bf16[512,1280]{1,0:T(8,128)(2,1)} fusion(bf16[3,1280,5,128]{3,1,2,0:T(8,128)(2,1)} %param.5, bf16[5,256,128]{2,1,0:T(8,128)(2,1)S(1)} %collective-permute-done.4, bf16[5,256,128]{2,1,0:T(8,128)(2,1)S(1)} %get-tuple-element.20), kind=kOutput, calls=%fused_computation.5 | convolution fusion | flops 840826880 | bytes 3604480 | tf_op jit(solution)/shard_map/dot_general | solution.py:50
  104.2 3.7 %all-to-all-start.3 = ((bf16[16,32,1280]{2,1,0:T(8,128)(2,1)}), bf16[16,32,1280]{2,1,0:T(8,128)(2,1)S(1)}, u32[]{:S(2)}, u32[]{:S(2)}) async-start(bf16[16,32,1280]{2,1,0:T(8,128)(2,1)} %bitcast.201), calls=%async_computation.3 | async-start | bytes 2621440 | tf_op jit(solution)/shard_map/all_to_all | solution.py:54
  107.9 3.0 %convolution_bitcast_fusion.4 = f32[3,512,128]{2,1,0:T(8,128)} fusion(bf16[512,1280,1]{1,0,2:T(8,128)(2,1)S(1)} %bitcast.191, bf16[13,128,3,1280]{3,1,2,0:T(8,128)(2,1)} %param.4), kind=kOutput, calls=%fused_computation.37 | convolution fusion | flops 503316480 | bytes 3080192 | tf_op jit(solution)/shard_map/dot_general | solution.py:23
  110.8 3.7 %fusion.24 = f32[5,512,128]{2,1,0:T(8,128)} fusion(bf16[512,1280,1]{1,0,2:T(8,128)(2,1)S(1)} %bitcast.192, bf16[13,128,3,1280]{3,1,2,0:T(8,128)(2,1)} %param.4), kind=kOutput, calls=%fused_computation.31 | convolution fusion | flops 838860800 | bytes 4259840 | tf_op jit(solution)/shard_map/dot_general | solution.py:23
  114.6 14.7 %all-to-all-done.3 = bf16[16,32,1280]{2,1,0:T(8,128)(2,1)S(1)} async-done(((bf16[16,32,1280]{2,1,0:T(8,128)(2,1)}), bf16[16,32,1280]{2,1,0:T(8,128)(2,1)S(1)}, u32[]{:S(2)}, u32[]{:S(2)}) %all-to-all-start.3) | async-done | bytes 1310752 | tf_op jit(solution)/shard_map/all_to_all | solution.py:54
  129.6 22.6 %all_to_all.42 = bf16[16,32,1280]{2,1,0:T(8,128)(2,1)S(1)} all-to-all(bf16[16,32,1280]{2,1,0:T(8,128)(2,1)S(1)} %broadcast_in_dim.73), channel_id=1, replica_groups=mesh['row'=16,'col'=8] {'row'}, dimensions={0} | all-to-all | bytes 2621440 | tf_op jit(solution)/shard_map/all_to_all | solution.py:65
  152.3 1.2 copy-done.3
  153.5 2.1 fusion.46
  155.6 1.7 collective-permute-start.5
  157.3 1.3 collective-permute-done.5
  158.6 2.2 fusion.93
  160.9 8.9 %collective-permute-done.6 = bf16[5,256,128]{2,1,0:T(8,128)(2,1)S(1)} collective-permute-done((bf16[5,256,128]{2,1,0:T(8,128)(2,1)S(1)}, bf16[5,256,128]{2,1,0:T(8,128)(2,1)S(1)}, u32[]{:S(2)}, u32[]{:S(2)}) %collective-permute-start.6) | collective-permute-done | bytes 327712 | tf_op jit(solution)/shard_map/ppermute | solution.py:11
  169.9 0.9 collective-permute-start.7
  170.8 8.4 %collective-permute-done.7 = bf16[5,256,128]{2,1,0:T(8,128)(2,1)S(1)} collective-permute-done((bf16[5,256,128]{2,1,0:T(8,128)(2,1)S(1)}, bf16[5,256,128]{2,1,0:T(8,128)(2,1)S(1)}, u32[]{:S(2)}, u32[]{:S(2)}) %collective-permute-start.7) | collective-permute-done | bytes 327712 | tf_op jit(solution)/shard_map/ppermute | solution.py:11
  179.2 1.0 fusion.87
  180.1 2.1 collective-permute-start.8
  182.2 1.3 collective-permute-done.8
  183.5 3.7 %fusion.2 = bf16[512,1280]{1,0:T(8,128)(2,1)} fusion(bf16[3,1280,5,128]{3,1,2,0:T(8,128)(2,1)} %param.5, bf16[5,256,128]{2,1,0:T(8,128)(2,1)S(1)} %collective-permute-done.8, bf16[5,256,128]{2,1,0:T(8,128)(2,1)S(1)} %get-tuple-element.18), kind=kOutput, calls=%fused_computation.6 | convolution fusion | flops 840826880 | bytes 3604480 | tf_op jit(solution)/shard_map/dot_general | solution.py:50
  187.2 4.6 %all-to-all-start.5 = ((bf16[16,32,1280]{2,1,0:T(8,128)(2,1)}), bf16[16,32,1280]{2,1,0:T(8,128)(2,1)}, u32[]{:S(2)}, u32[]{:S(2)}) async-start(bf16[16,32,1280]{2,1,0:T(8,128)(2,1)} %bitcast.202), calls=%async_computation.5 | async-start | bytes 2621440 | tf_op jit(solution)/shard_map/all_to_all | solution.py:54
  191.8 3.2 %fusion.30 = f32[3,512,128]{2,1,0:T(8,128)} fusion(f32[3,512,128]{2,1,0:T(8,128)} %convolution_bitcast_fusion.4, bf16[512,1280,1]{1,0,2:T(8,128)(2,1)S(1)} %bitcast.194, bf16[13,128,3,1280]{3,1,2,0:T(8,128)(2,1)} %param.4), kind=kOutput, calls=%fused_computation.36 | convolution fusion | flops 503513088 | bytes 3866624 | tf_op jit(solution)/shard_map/dot_general | solution.py:23
  195.0 18.0 %all-to-all-done.5 = bf16[16,32,1280]{2,1,0:T(8,128)(2,1)} async-done(((bf16[16,32,1280]{2,1,0:T(8,128)(2,1)}), bf16[16,32,1280]{2,1,0:T(8,128)(2,1)}, u32[]{:S(2)}, u32[]{:S(2)}) %all-to-all-start.5) | async-done | bytes 1310752 | tf_op jit(solution)/shard_map/all_to_all | solution.py:54
  213.0 1.5 reduce_sum.47
  214.5 1.2 broadcast_in_dim.76
  215.7 4.4 %all-to-all-start.6 = ((bf16[16,32,1280]{2,1,0:T(8,128)(2,1)}), bf16[16,32,1280]{2,1,0:T(8,128)(2,1)}, u32[]{:S(2)}, u32[]{:S(2)}) async-start(bf16[16,32,1280]{2,1,0:T(8,128)(2,1)} %broadcast_in_dim.76), calls=%async_computation.6 | async-start | bytes 2621440 | tf_op jit(solution)/shard_map/all_to_all | solution.py:65
  220.2 0.5 fusion.27
  220.8 1.2 copy.35
  221.9 0.9 constant_dynamic-slice_fusion
  222.9 15.8 %all-to-all-done.6 = bf16[16,32,1280]{2,1,0:T(8,128)(2,1)} async-done(((bf16[16,32,1280]{2,1,0:T(8,128)(2,1)}), bf16[16,32,1280]{2,1,0:T(8,128)(2,1)}, u32[]{:S(2)}, u32[]{:S(2)}) %all-to-all-start.6) | async-done | bytes 1310752 | tf_op jit(solution)/shard_map/all_to_all | solution.py:65
  238.7 1.4 fusion.89
  240.0 1.7 fusion.57
  241.8 3.3 %collective-permute-start.9 = (bf16[3,256,128]{2,1,0:T(8,128)(2,1)S(1)}, bf16[3,256,128]{2,1,0:T(8,128)(2,1)S(1)}, u32[]{:S(2)}, u32[]{:S(2)}) collective-permute-start(bf16[3,256,128]{2,1,0:T(8,128)(2,1)S(1)} %fusion.57), channel_id=1, source_target_pairs={{0,1},{1,0},{2,3},{3,2},{4,5},{5,4},{6,7},{7,6},{8,9},{9,8},{10,11... | collective-permute-start | bytes 589832 | tf_op jit(solution)/shard_map/ppermute | solution.py:11
  245.1 2.0 fusion.29
  247.1 1.1 copy.42
  248.2 0.3 copy-done.5
  248.5 1.8 add_convert_fusion
  250.4 0.7 copy.53
  251.1 3.4 %all-to-all-start.7 = ((bf16[4,3,64,128]{3,2,1,0:T(8,128)(2,1)}), bf16[4,3,64,128]{3,2,1,0:T(8,128)(2,1)S(1)}, u32[]{:S(2)}, u32[]{:S(2)}) async-start(bf16[4,3,64,128]{3,2,1,0:T(8,128)(2,1)} %bitcast.190), calls=%async_computation.7 | async-start | bytes 393216 | tf_op jit(solution)/shard_map/all_to_all | solution.py:88
  254.5 3.2 %pad_maximum_fusion = bf16[3,1280,512]{1,2,0:T(8,128)(2,1)} fusion(bf16[1,1280,512]{1,2,0:T(8,128)(2,1)} %bitcast.198, bf16[1,1280,512]{1,2,0:T(8,128)(2,1)S(1)} %bitcast.196, bf16[1,1280,512]{1,2,0:T(8,128)(2,1)S(1)} %bitcast.197), kind=kLoop, calls=%fused_computation | loop fusion | flops 3932160 | bytes 7864320 | tf_op jit(solution)/shard_map/stack | solution.py:96
  257.6 6.3 %copy.45 = bf16[3,1280,512]{2,1,0:T(8,128)(2,1)} copy(bf16[3,1280,512]{1,2,0:T(8,128)(2,1)} %pad_maximum_fusion) | data formatting | bytes 7864320
  264.0 0.9 slice_subtract_fusion
  264.9 0.9 maximum_bitcast_fusion
  (26 shorter events, 1.1 us)
Async XLA Ops:
  13.5 3.5 %collective-permute-start = (bf16[5,256,128]{2,1,0:T(8,128)(2,1)S(1)}, bf16[5,256,128]{2,1,0:T(8,128)(2,1)S(1)}, u32[]{:S(2)}, u32[]{:S(2)}) collective-permute-start(bf16[5,256,128]{2,1,0:T(8,128)(2,1)S(1)} %bitcast.212), channel_id=1, source_target_pairs={{0,1},{1,0},{2,3},{3,2},{4,5},{5,4},{6,7},{7,6},{8,9},{9,8},{10,11... | collective-permute-start | bytes 983048 | tf_op jit(solution)/shard_map/ppermute | solution.py:11
  47.0 21.9 %all-to-all-start.2 = ((bf16[16,32,1280]{2,1,0:T(8,128)(2,1)}), bf16[16,32,1280]{2,1,0:T(8,128)(2,1)S(1)}, u32[]{:S(2)}, u32[]{:S(2)}) async-start(bf16[16,32,1280]{2,1,0:T(8,128)(2,1)} %broadcast_in_dim.66), calls=%async_computation.2 | async-start | bytes 2621440 | tf_op jit(solution)/shard_map/all_to_all | solution.py:65
  69.0 5.9 %copy-start.1 = (f32[64,18,128]{2,0,1:T(8,128)S(1)}, f32[64,18,128]{2,0,1:T(8,128)}, u32[]{:S(2)}) copy-start(f32[64,18,128]{2,0,1:T(8,128)} %param.3) | copy-start | bytes 1769476
  71.2 4.8 %collective-permute-start.1 = (bf16[5,256,128]{2,1,0:T(8,128)(2,1)S(1)}, bf16[5,256,128]{2,1,0:T(8,128)(2,1)S(1)}, u32[]{:S(2)}, u32[]{:S(2)}) collective-permute-start(bf16[5,256,128]{2,1,0:T(8,128)(2,1)S(1)} %fusion.54), channel_id=1, source_target_pairs={{0,1},{1,0},{2,3},{3,2},{4,5},{5,4},{6,7},{7,6},{8,9},{9,8},{10,11... | collective-permute-start | bytes 983048 | tf_op jit(solution)/shard_map/ppermute | solution.py:11
  78.2 9.0 %collective-permute-start.2 = (bf16[5,256,128]{2,1,0:T(8,128)(2,1)S(1)}, bf16[5,256,128]{2,1,0:T(8,128)(2,1)S(1)}, u32[]{:S(2)}, u32[]{:S(2)}) collective-permute-start(bf16[5,256,128]{2,1,0:T(8,128)(2,1)S(1)} %get-tuple-element.31), channel_id=1, source_target_pairs={{0,2},{1,3},{2,0},{3,1},{4,6},{5,7},{6,4},{7,5},{8,10},{9,11},{10,... | collective-permute-start | bytes 983048 | tf_op jit(solution)/shard_map/ppermute | solution.py:11
  87.4 9.3 %collective-permute-start.3 = (bf16[5,256,128]{2,1,0:T(8,128)(2,1)S(1)}, bf16[5,256,128]{2,1,0:T(8,128)(2,1)S(1)}, u32[]{:S(2)}, u32[]{:S(2)}) collective-permute-start(bf16[5,256,128]{2,1,0:T(8,128)(2,1)S(1)} %fusion.79), channel_id=1, source_target_pairs={{0,6},{1,7},{2,4},{3,5},{4,2},{5,3},{6,0},{7,1},{8,14},{9,15},{10,... | collective-permute-start | bytes 983048 | tf_op jit(solution)/shard_map/ppermute | solution.py:11
  97.0 3.5 %collective-permute-start.4 = (bf16[5,256,128]{2,1,0:T(8,128)(2,1)S(1)}, bf16[5,256,128]{2,1,0:T(8,128)(2,1)S(1)}, u32[]{:S(2)}, u32[]{:S(2)}) collective-permute-start(bf16[5,256,128]{2,1,0:T(8,128)(2,1)S(1)} %get-tuple-element.20), channel_id=1, source_target_pairs={{0,1},{1,0},{2,3},{3,2},{4,5},{5,4},{6,7},{7,6},{8,9},{9,8},{10,11... | collective-permute-start | bytes 983048 | tf_op jit(solution)/shard_map/ppermute | solution.py:11
  104.2 25.1 %all-to-all-start.3 = ((bf16[16,32,1280]{2,1,0:T(8,128)(2,1)}), bf16[16,32,1280]{2,1,0:T(8,128)(2,1)S(1)}, u32[]{:S(2)}, u32[]{:S(2)}) async-start(bf16[16,32,1280]{2,1,0:T(8,128)(2,1)} %bitcast.201), calls=%async_computation.3 | async-start | bytes 2621440 | tf_op jit(solution)/shard_map/all_to_all | solution.py:54
  152.2 1.3 copy-start.3
  155.6 2.9 %collective-permute-start.5 = (bf16[5,256,128]{2,1,0:T(8,128)(2,1)S(1)}, bf16[5,256,128]{2,1,0:T(8,128)(2,1)S(1)}, u32[]{:S(2)}, u32[]{:S(2)}) collective-permute-start(bf16[5,256,128]{2,1,0:T(8,128)(2,1)S(1)} %fusion.46), channel_id=1, source_target_pairs={{0,1},{1,0},{2,3},{3,2},{4,5},{5,4},{6,7},{7,6},{8,9},{9,8},{10,11... | collective-permute-start | bytes 983048 | tf_op jit(solution)/shard_map/ppermute | solution.py:11
  160.8 9.0 %collective-permute-start.6 = (bf16[5,256,128]{2,1,0:T(8,128)(2,1)S(1)}, bf16[5,256,128]{2,1,0:T(8,128)(2,1)S(1)}, u32[]{:S(2)}, u32[]{:S(2)}) collective-permute-start(bf16[5,256,128]{2,1,0:T(8,128)(2,1)S(1)} %get-tuple-element.33), channel_id=1, source_target_pairs={{0,2},{1,3},{2,0},{3,1},{4,6},{5,7},{6,4},{7,5},{8,10},{9,11},{10,... | collective-permute-start | bytes 983048 | tf_op jit(solution)/shard_map/ppermute | solution.py:11
  169.9 9.3 %collective-permute-start.7 = (bf16[5,256,128]{2,1,0:T(8,128)(2,1)S(1)}, bf16[5,256,128]{2,1,0:T(8,128)(2,1)S(1)}, u32[]{:S(2)}, u32[]{:S(2)}) collective-permute-start(bf16[5,256,128]{2,1,0:T(8,128)(2,1)S(1)} %fusion.80), channel_id=1, source_target_pairs={{0,6},{1,7},{2,4},{3,5},{4,2},{5,3},{6,0},{7,1},{8,14},{9,15},{10,... | collective-permute-start | bytes 983048 | tf_op jit(solution)/shard_map/ppermute | solution.py:11
  180.1 3.4 %collective-permute-start.8 = (bf16[5,256,128]{2,1,0:T(8,128)(2,1)S(1)}, bf16[5,256,128]{2,1,0:T(8,128)(2,1)S(1)}, u32[]{:S(2)}, u32[]{:S(2)}) collective-permute-start(bf16[5,256,128]{2,1,0:T(8,128)(2,1)S(1)} %get-tuple-element.18), channel_id=1, source_target_pairs={{0,1},{1,0},{2,3},{3,2},{4,5},{5,4},{6,7},{7,6},{8,9},{9,8},{10,11... | collective-permute-start | bytes 983048 | tf_op jit(solution)/shard_map/ppermute | solution.py:11
  187.2 25.8 %all-to-all-start.5 = ((bf16[16,32,1280]{2,1,0:T(8,128)(2,1)}), bf16[16,32,1280]{2,1,0:T(8,128)(2,1)}, u32[]{:S(2)}, u32[]{:S(2)}) async-start(bf16[16,32,1280]{2,1,0:T(8,128)(2,1)} %bitcast.202), calls=%async_computation.5 | async-start | bytes 2621440 | tf_op jit(solution)/shard_map/all_to_all | solution.py:54
  215.7 23.0 %all-to-all-start.6 = ((bf16[16,32,1280]{2,1,0:T(8,128)(2,1)}), bf16[16,32,1280]{2,1,0:T(8,128)(2,1)}, u32[]{:S(2)}, u32[]{:S(2)}) async-start(bf16[16,32,1280]{2,1,0:T(8,128)(2,1)} %broadcast_in_dim.76), calls=%async_computation.6 | async-start | bytes 2621440 | tf_op jit(solution)/shard_map/all_to_all | solution.py:65
  222.9 17.2 %copy-start.4 = (f32[3,512,128]{2,1,0:T(8,128)S(1)}, f32[3,512,128]{2,1,0:T(8,128)}, u32[]{:S(2)}) copy-start(f32[3,512,128]{2,1,0:T(8,128)} %fusion.30) | copy-start | bytes 2359300
  241.8 6.4 %collective-permute-start.9 = (bf16[3,256,128]{2,1,0:T(8,128)(2,1)S(1)}, bf16[3,256,128]{2,1,0:T(8,128)(2,1)S(1)}, u32[]{:S(2)}, u32[]{:S(2)}) collective-permute-start(bf16[3,256,128]{2,1,0:T(8,128)(2,1)S(1)} %fusion.57), channel_id=1, source_target_pairs={{0,1},{1,0},{2,3},{3,2},{4,5},{5,4},{6,7},{7,6},{8,9},{9,8},{10,11... | collective-permute-start | bytes 589832 | tf_op jit(solution)/shard_map/ppermute | solution.py:11
  247.1 1.4 copy-start.5
  248.5 5.9 %copy-start = (bf16[1280,4,2,64]{0,3,2,1:T(8,128)(2,1)S(1)}, bf16[1280,4,2,64]{0,3,2,1:T(8,128)(2,1)}, u32[]{:S(2)}) copy-start(bf16[1280,4,2,64]{0,3,2,1:T(8,128)(2,1)} %copy.35) | copy-start | bytes 3932164
  251.1 12.9 %all-to-all-start.7 = ((bf16[4,3,64,128]{3,2,1,0:T(8,128)(2,1)}), bf16[4,3,64,128]{3,2,1,0:T(8,128)(2,1)S(1)}, u32[]{:S(2)}, u32[]{:S(2)}) async-start(bf16[4,3,64,128]{3,2,1,0:T(8,128)(2,1)} %bitcast.190), calls=%async_computation.7 | async-start | bytes 393216 | tf_op jit(solution)/shard_map/all_to_all | solution.py:88
  257.6 7.3 %copy-start.2 = (f32[5,64,128]{2,1,0:T(8,128)S(1)}, f32[5,64,128]{2,1,0:T(8,128)}, u32[]{:S(2)}) copy-start(f32[5,64,128]{2,1,0:T(8,128)} %get-tuple-element.28) | copy-start | bytes 491524

commit v3 on v2

--- a/solution.py
+++ b/solution.py
@@ -1,14 +1,45 @@
 import jax
 import jax.numpy as jnp
 from jax import lax
+from jax.experimental import pallas as pl
+from jax.experimental.pallas import tpu as pltpu
 from jax.sharding import PartitionSpec as P
 
 BF16 = jnp.bfloat16
 F32 = jnp.float32
 
 
-def swap(block, n_col, mask):
-    return lax.ppermute(block, "col", [(c, c ^ mask) for c in range(n_col)])
+def swap(block, n_col, masks):
+    return lax.ppermute(block, "col", [(c, c ^ masks[c % 2]) for c in range(n_col)])
+
+
+def place_kernel(core_ref, solved_ref, outs_ref, placed_ref):
+    n_z, chunk = solved_ref.shape[1:3]
+    own_first = core_ref[0] == 0
+    for z in range(n_z):
+        own = solved_ref[0, z]
+        other = solved_ref[1, z]
+        pair = jnp.concatenate([jnp.where(own_first, own, other), jnp.where(own_first, other, own)], axis=0)
+        placed_ref[0, :, z * 2 * chunk : (z + 1) * 2 * chunk] = pair.T
+
+
+def place(core, solved, outs, step, n_z):
+    vecs, width = solved.shape
+    tile = width // 5
+    halves = solved.reshape(2, n_z, vecs // (2 * n_z), width)
+    return pl.pallas_call(
+        place_kernel,
+        grid=(width // tile,),
+        in_specs=[
+            pl.BlockSpec(memory_space=pltpu.SMEM),
+            pl.BlockSpec(halves.shape[:3] + (tile,), lambda i: (0, 0, 0, i)),
+            pl.BlockSpec(memory_space=pl.ANY),
+        ],
+        out_specs=pl.BlockSpec((1, tile, vecs), lambda i: (step, i, 0)),
+        out_shape=jax.ShapeDtypeStruct(outs.shape, outs.dtype),
+        input_output_aliases={2: 0},
+        cost_estimate=pl.CostEstimate(flops=0, bytes_accessed=4 * vecs * width, transcendentals=0),
+    )(core, halves, outs)
 
 
 def same_core(n_col):
@@ -33,7 +64,8 @@
     vecs = chunk * n_col
     half = vecs // 2
     my_z = lax.axis_index("col") // 2
-    my_core = lax.axis_index("col") % 2
+    core = (lax.axis_index("col") % 2).astype(jnp.int32).reshape(1)
+    outs = jnp.zeros((steps, width, vecs), BF16)
     noise = noise.transpose(1, 0, 2)
     bounds = [(s * rounds, min((s + 1) * rounds, total)) for s in range(steps + 1)]
 
@@ -45,7 +77,7 @@
     solved_list = []
     later = {}
     for s in range(steps):
-        other = swap(own, n_col, 1)
+        other = swap(own, n_col, (1, 1))
         everyone = jnp.concatenate([own, other], axis=1)
         partial = lax.dot_general(
             everyone, dinv[s], (((0, 2), (1, 2)), ((), ())), preferred_element_type=F32
@@ -58,7 +90,8 @@
                 block = factor[lo - rounds : hi - rounds, :, s - 1, :]
                 more = product(solved_list[s - 1], block)
                 later[n] = more if n not in later else later[n] + more
-            received, *held = tied(received, *[later[n] for n in range(s + 1, steps + 1)])
+            outs = place(core, solved_list[s - 1], outs, s - 1, n_z)
+            received, outs, *held = tied(received, outs, *[later[n] for n in range(s + 1, steps + 1)])
             later.update(zip(range(s + 1, steps + 1), held))
         mine = jnp.sum(received.astype(F32), axis=0).astype(BF16)
         copies = jnp.broadcast_to(mine[None], (n_row,) + mine.shape)
@@ -70,7 +103,7 @@
         update_other = product(solved[half:], block)
         if s > 0:
             update_other = update_other + later[s + 1][:, half:]
-        arrived = swap(update_other.astype(BF16), n_col, 1)
+        arrived = swap(update_other.astype(BF16), n_col, (1, 1))
         update = product(solved[:half], block)
         if s > 0:
             update = update + later[s + 1][:, :half]
@@ -79,8 +112,8 @@
             spread = update.reshape(hi - lo, n_z, chunk, lanes)
             here = (lax.iota(jnp.int32, n_z) == my_z)[None, :, None, None]
             work = (jnp.where(here, noise[lo:hi][:, None], 0.0) - spread).reshape(hi - lo, half, lanes)
-            work = work + swap(work.astype(BF16), n_col, 2).astype(F32)
-            work = work + swap(work.astype(BF16), n_col, n_col - 2).astype(F32)
+            work = work + swap(work.astype(BF16), n_col, (2, n_col - 2)).astype(F32)
+            work = work + swap(work.astype(BF16), n_col, (n_col - 2, 2)).astype(F32)
             done.append(lax.dynamic_slice_in_dim(work, my_z * chunk, chunk, axis=1))
             own = work.astype(BF16)
         else:
@@ -88,12 +121,8 @@
             got = lax.all_to_all(parts, "col", 0, 0, tiled=True, axis_index_groups=same_core(n_col))
             done.append(noise[lo:hi] - jnp.sum(got.astype(F32), axis=0))
 
-    outs = []
-    for solved in solved_list:
-        halves = solved.reshape(2, n_z, chunk, width)
-        ordered = jnp.where(my_core == 0, halves, halves[::-1])
-        outs.append(ordered.transpose(3, 1, 0, 2).reshape(width, vecs))
-    return jnp.stack(outs), jnp.concatenate(done, axis=0).transpose(1, 0, 2)
+    outs = place(core, solved_list[-1], outs, steps - 1, n_z)
+    return outs, jnp.concatenate(done, axis=0).transpose(1, 0, 2)
 
 
 def solution(mesh):

time: 267 us -> 248 us (0.929)
  waiting for transfers between devices: 106 us -> 71.4 us
  blocking collectives: 60.4 us -> 83.1 us
  Pallas kernels: 0 us -> 13 us
  local copies, waits for them, and re-layouts: 17.8 us -> 10.7 us
  other arithmetic: 11 us -> 4 us
  starting transfers between devices: 37 us -> 30.7 us
    all_to_all x1 -> x2, blocking collectives: 22.6 us -> 45.3 us  [local(): lax.all_to_all(copies, 'row', 0, 0, tiled=True).reshape(vecs, width)]
    all_to_all x2 -> x1, waiting for transfers between devices: 34 us -> 18.2 us  [local(): lax.all_to_all(copies, 'row', 0, 0, tiled=True).reshape(vecs, width)]
    pallas_call x0 -> x3, Pallas kernels: none -> 13 us  [place(): pl.pallas_call(place_kernel, grid=(width // tile,), in_specs=[pl.BlockSpe...]
    all_to_all x2, waiting for transfers between devices: 32.7 us -> 21.7 us  [local(): received = lax.all_to_all(parts, 'row', 0, 0, tiled=True)]
    ppermute x10, waiting for transfers between devices: 39.7 us -> 31.4 us  [swap(): lax.ppermute(block, 'col', [(c, c ^ masks[c % 2]) for c in range(n_col)])]
    unnamed x13 -> x18, local copies, waits for them, and re-layouts: 7.84 us -> 3.24 us
    all_to_all x2 -> x1, starting transfers between devices: 8.1 us -> 3.7 us  [local(): lax.all_to_all(copies, 'row', 0, 0, tiled=True).reshape(vecs, width)]
    another operation x1 -> x0, other arithmetic: 3.19 us -> none  [local(): return (jnp.stack(outs), jnp.concatenate(done, axis=0).transpose(1, 0, 2))]
  transfers between devices with their start and end apart: 15 -> 14, of which waited for: 13 -> 14; matrix products, arithmetic and copies ran while one was open for 10% -> 6% of each run, Pallas kernels for 0% -> 5%
where the time goes in v3:
time: 248 us; the launch traced here: 246 us
  blocking collectives  83.1 us (34%)
  waiting for transfers between devices  71.4 us (29%)
  matrix products  32.4 us (13%)
  starting transfers between devices  30.7 us (12%)
  Pallas kernels  13 us (5%)
  local copies, waits for them, and re-layouts  10.7 us (4%)
  other arithmetic  4 us (2%)
    all_to_all x2, blocking collectives, local(): lax.all_to_all(copies, 'row', 0, 0, tiled=True).reshape(vecs, width)  45.3 us
    ppermute x10, waiting for transfers between devices, swap(): lax.ppermute(block, 'col', [(c, c ^ masks[c % 2]) for c in range(n_col)])  31.4 us
    all_to_all x1, blocking collectives, local(): received = lax.all_to_all(parts, 'row', 0, 0, tiled=True)  26 us
    dot_general x9, matrix products, product(): lax.dot_general(solved, block, (((1,), (2,)), ((), ())), preferred_elemen...  22.4 us
    all_to_all x2, waiting for transfers between devices, local(): received = lax.all_to_all(parts, 'row', 0, 0, tiled=True)  21.7 us
    all_to_all x1, waiting for transfers between devices, local(): lax.all_to_all(copies, 'row', 0, 0, tiled=True).reshape(vecs, width)  18.2 us
    ppermute x10, starting transfers between devices, swap(): lax.ppermute(block, 'col', [(c, c ^ masks[c % 2]) for c in range(n_col)])  16.1 us
    pallas_call x3, Pallas kernels, place(): pl.pallas_call(place_kernel, grid=(width // tile,), in_specs=[pl.BlockSpe...  13 us
  transfers between devices with their start and end apart: 14, of which 14 were waited for; matrix products, arithmetic and copies ran while one was open for 6% of the time, Pallas kernels for 5%

profile of v3, /device:TPU:1, one launch (start us, length us, event | category | flops | bytes accessed | tf_op | source)
XLA Modules:
  0.0 246.2 jit_solution(14434310665941084330)
XLA Ops:
  0.6 0.9 slice.207
  1.6 11.8 %all_to_all.40 = bf16[4,5,64,128]{3,2,1,0:T(8,128)(2,1)S(1)} all-to-all(bf16[4,5,64,128]{3,2,1,0:T(8,128)(2,1)S(1)} %broadcast_in_dim.76), channel_id=1, replica_groups={{0,2,4,6},{1,3,5,7},{8,10,12,14},{9,11,13,15},{16,18,20,22},{17,19,21,2..., dimensions={0} | all-to-all | bytes 655360 | tf_op jit(solution)/shard_map/all_to_all | solution.py:74
  13.5 2.2 collective-permute-start
  15.7 1.3 collective-permute-done
  17.0 2.6 %fusion = bf16[512,1280]{1,0:T(8,128)(2,1)S(1)} fusion(bf16[3,1280,5,128]{3,1,2,0:T(8,128)(2,1)} %param.5, bf16[5,256,128]{2,1,0:T(8,128)(2,1)S(1)} %collective-permute-done, bf16[5,256,128]{2,1,0:T(8,128)(2,1)S(1)} %bitcast.201), kind=kOutput, calls=%fused_computation.3 | convolution fusion | flops 840826880 | bytes 3604480 | tf_op jit(solution)/shard_map/dot_general | solution.py:82
  19.6 26.0 %all_to_all.41 = bf16[16,32,1280]{2,1,0:T(8,128)(2,1)S(1)} all-to-all(bf16[16,32,1280]{2,1,0:T(8,128)(2,1)S(1)} %bitcast.191), channel_id=1, replica_groups=mesh['row'=16,'col'=8] {'row'}, dimensions={0} | all-to-all | bytes 2621440 | tf_op jit(solution)/shard_map/all_to_all | solution.py:86
  45.6 0.2 reduce_sum.45
  45.8 1.2 broadcast_in_dim.77
  47.0 3.7 %all-to-all-start.2 = ((bf16[16,32,1280]{2,1,0:T(8,128)(2,1)}), bf16[16,32,1280]{2,1,0:T(8,128)(2,1)S(1)}, u32[]{:S(2)}, u32[]{:S(2)}) async-start(bf16[16,32,1280]{2,1,0:T(8,128)(2,1)} %broadcast_in_dim.77), calls=%async_computation.2 | async-start | bytes 2621440 | tf_op jit(solution)/shard_map/all_to_all | solution.py:98
  50.7 18.2 %all-to-all-done.2 = bf16[16,32,1280]{2,1,0:T(8,128)(2,1)S(1)} async-done(((bf16[16,32,1280]{2,1,0:T(8,128)(2,1)}), bf16[16,32,1280]{2,1,0:T(8,128)(2,1)S(1)}, u32[]{:S(2)}, u32[]{:S(2)}) %all-to-all-start.2) | async-done | bytes 1310752 | tf_op jit(solution)/shard_map/all_to_all | solution.py:98
  69.0 2.5 %fusion.51 = bf16[5,256,128]{2,1,0:T(8,128)(2,1)S(1)} fusion(bf16[256,1280,1]{1,0,2:T(8,128)(2,1)S(1)} %bitcast.197, bf16[13,128,3,1280]{3,1,2,0:T(8,128)(2,1)} %param.4), kind=kOutput, calls=%fused_computation.42 | convolution fusion | flops 419594240 | bytes 2621440 | tf_op jit(solution)/shard_map/dot_general | solution.py:54
  71.6 3.5 %collective-permute-start.1 = (bf16[5,256,128]{2,1,0:T(8,128)(2,1)S(1)}, bf16[5,256,128]{2,1,0:T(8,128)(2,1)S(1)}, u32[]{:S(2)}, u32[]{:S(2)}) collective-permute-start(bf16[5,256,128]{2,1,0:T(8,128)(2,1)S(1)} %fusion.51), channel_id=1, source_target_pairs={{0,1},{1,0},{2,3},{3,2},{4,5},{5,4},{6,7},{7,6},{8,9},{9,8},{10,11... | collective-permute-start | bytes 983048 | tf_op jit(solution)/shard_map/ppermute | solution.py:13
  75.2 0.7 fusion.89
  75.9 0.4 collective-permute-done.1
  76.3 2.1 fusion.83
  78.5 1.0 collective-permute-start.2
  79.5 6.2 %collective-permute-done.2 = bf16[5,256,128]{2,1,0:T(8,128)(2,1)S(1)} collective-permute-done((bf16[5,256,128]{2,1,0:T(8,128)(2,1)S(1)}, bf16[5,256,128]{2,1,0:T(8,128)(2,1)S(1)}, u32[]{:S(2)}, u32[]{:S(2)}) %collective-permute-start.2) | collective-permute-done | bytes 327712 | tf_op jit(solution)/shard_map/ppermute | solution.py:13
  85.7 0.3 fusion.76
  86.1 6.2 %collective-permute-done.3 = bf16[5,256,128]{2,1,0:T(8,128)(2,1)S(1)} collective-permute-done((bf16[5,256,128]{2,1,0:T(8,128)(2,1)S(1)}, bf16[5,256,128]{2,1,0:T(8,128)(2,1)S(1)}, u32[]{:S(2)}, u32[]{:S(2)}) %collective-permute-start.3) | collective-permute-done | bytes 327712 | tf_op jit(solution)/shard_map/ppermute | solution.py:13
  92.3 0.3 fusion.85
  92.6 2.5 collective-permute-start.4
  95.0 1.3 collective-permute-done.4
  96.3 3.7 %fusion.1 = bf16[512,1280]{1,0:T(8,128)(2,1)} fusion(bf16[3,1280,5,128]{3,1,2,0:T(8,128)(2,1)} %param.5, bf16[5,256,128]{2,1,0:T(8,128)(2,1)S(1)} %collective-permute-done.4, bf16[5,256,128]{2,1,0:T(8,128)(2,1)S(1)} %get-tuple-element.18), kind=kOutput, calls=%fused_computation.4 | convolution fusion | flops 840826880 | bytes 3604480 | tf_op jit(solution)/shard_map/dot_general | solution.py:82
  100.0 3.7 %all-to-all-start.3 = ((bf16[16,32,1280]{2,1,0:T(8,128)(2,1)}), bf16[16,32,1280]{2,1,0:T(8,128)(2,1)S(1)}, u32[]{:S(2)}, u32[]{:S(2)}) async-start(bf16[16,32,1280]{2,1,0:T(8,128)(2,1)} %bitcast.18), calls=%async_computation.3 | async-start | bytes 2621440 | tf_op jit(solution)/shard_map/all_to_all | solution.py:86
  103.7 2.2 broadcast_in_dim.78.outs_ref
  106.0 4.3 %shard_map.50.outs_ref = bf16[3,1280,512]{2,1,0:T(8,128)(2,1)} custom-call(s32[1]{0:T(128)} %bitcast.core_ref, bf16[2,4,64,1280]{3,2,1,0:T(8,128)(2,1)} %bitcast.183, bf16[3,1280,512]{2,1,0:T(8,128)(2,1)} %broadcast_in_dim.78.outs_ref), custom_call_target="tpu_custom_call", output_to_operand_aliasing={{}: (2, {})} | custom-call | bytes 2621440 | tf_op jit(solution)/shard_map/pallas_call | solution.py:30
  110.3 3.0 %convolution_bitcast_fusion.4 = f32[3,512,128]{2,1,0:T(8,128)} fusion(bf16[512,1280,1]{1,0,2:T(8,128)(2,1)S(1)} %bitcast.184, bf16[13,128,3,1280]{3,1,2,0:T(8,128)(2,1)} %param.4), kind=kOutput, calls=%fused_computation.30 | convolution fusion | flops 503316480 | bytes 3080192 | tf_op jit(solution)/shard_map/dot_general | solution.py:54
  113.3 3.7 %fusion.24 = f32[5,512,128]{2,1,0:T(8,128)} fusion(bf16[512,1280,1]{1,0,2:T(8,128)(2,1)S(1)} %bitcast.185, bf16[13,128,3,1280]{3,1,2,0:T(8,128)(2,1)} %param.4), kind=kOutput, calls=%fused_computation.27 | convolution fusion | flops 838860800 | bytes 4259840 | tf_op jit(solution)/shard_map/dot_general | solution.py:54
  117.0 8.1 %all-to-all-done.3 = bf16[16,32,1280]{2,1,0:T(8,128)(2,1)S(1)} async-done(((bf16[16,32,1280]{2,1,0:T(8,128)(2,1)}), bf16[16,32,1280]{2,1,0:T(8,128)(2,1)S(1)}, u32[]{:S(2)}, u32[]{:S(2)}) %all-to-all-start.3) | async-done | bytes 1310752 | tf_op jit(solution)/shard_map/all_to_all | solution.py:86
  125.1 0.2 reduce_sum.46
  125.3 0.1 broadcast_in_dim.79
  125.4 22.6 %all_to_all.42 = bf16[16,32,1280]{2,1,0:T(8,128)(2,1)S(1)} all-to-all(bf16[16,32,1280]{2,1,0:T(8,128)(2,1)S(1)} %broadcast_in_dim.79), channel_id=1, replica_groups=mesh['row'=16,'col'=8] {'row'}, dimensions={0} | all-to-all | bytes 2621440 | tf_op jit(solution)/shard_map/all_to_all | solution.py:98
  148.1 1.7 copy-done.7
  149.8 2.1 fusion.43
  151.9 1.7 collective-permute-start.5
  153.6 1.3 collective-permute-done.5
  154.9 2.2 fusion.90
  157.1 1.0 collective-permute-start.6
  158.1 6.2 %collective-permute-done.6 = bf16[5,256,128]{2,1,0:T(8,128)(2,1)S(1)} collective-permute-done((bf16[5,256,128]{2,1,0:T(8,128)(2,1)S(1)}, bf16[5,256,128]{2,1,0:T(8,128)(2,1)S(1)}, u32[]{:S(2)}, u32[]{:S(2)}) %collective-permute-start.6) | collective-permute-done | bytes 327712 | tf_op jit(solution)/shard_map/ppermute | solution.py:13
  164.3 0.1 fusion.77
  164.5 6.2 %collective-permute-done.7 = bf16[5,256,128]{2,1,0:T(8,128)(2,1)S(1)} collective-permute-done((bf16[5,256,128]{2,1,0:T(8,128)(2,1)S(1)}, bf16[5,256,128]{2,1,0:T(8,128)(2,1)S(1)}, u32[]{:S(2)}, u32[]{:S(2)}) %collective-permute-start.7) | collective-permute-done | bytes 327712 | tf_op jit(solution)/shard_map/ppermute | solution.py:13
  170.7 1.0 fusion.84
  171.7 2.4 collective-permute-start.8
  174.0 1.3 collective-permute-done.8
  175.3 3.7 %fusion.2 = bf16[512,1280]{1,0:T(8,128)(2,1)} fusion(bf16[3,1280,5,128]{3,1,2,0:T(8,128)(2,1)} %param.5, bf16[5,256,128]{2,1,0:T(8,128)(2,1)S(1)} %collective-permute-done.8, bf16[5,256,128]{2,1,0:T(8,128)(2,1)S(1)} %get-tuple-element.16), kind=kOutput, calls=%fused_computation.5 | convolution fusion | flops 840826880 | bytes 3604480 | tf_op jit(solution)/shard_map/dot_general | solution.py:82
  179.0 3.9 %all-to-all-start.5 = ((bf16[16,32,1280]{2,1,0:T(8,128)(2,1)}), bf16[16,32,1280]{2,1,0:T(8,128)(2,1)S(1)}, u32[]{:S(2)}, u32[]{:S(2)}) async-start(bf16[16,32,1280]{2,1,0:T(8,128)(2,1)} %bitcast.36), calls=%async_computation.5 | async-start | bytes 2621440 | tf_op jit(solution)/shard_map/all_to_all | solution.py:86
  182.9 4.3 %shard_map.51.outs_ref = bf16[3,1280,512]{2,1,0:T(8,128)(2,1)} custom-call(s32[1]{0:T(128)} %bitcast.core_ref, bf16[2,4,64,1280]{3,2,1,0:T(8,128)(2,1)} %bitcast.186, bf16[3,1280,512]{2,1,0:T(8,128)(2,1)} %shard_map.50.outs_ref), custom_call_target="tpu_custom_call", output_to_operand_aliasing={{}: (2, {})} | custom-call | bytes 2621440 | tf_op jit(solution)/shard_map/pallas_call | solution.py:30
  187.3 3.2 %fusion.27 = f32[3,512,128]{2,1,0:T(8,128)} fusion(f32[3,512,128]{2,1,0:T(8,128)} %convolution_bitcast_fusion.4, bf16[512,1280,1]{1,0,2:T(8,128)(2,1)S(1)} %bitcast.187, bf16[13,128,3,1280]{3,1,2,0:T(8,128)(2,1)} %param.4), kind=kOutput, calls=%fused_computation.29 | convolution fusion | flops 503513088 | bytes 3866624 | tf_op jit(solution)/shard_map/dot_general | solution.py:54
  190.5 13.6 %all-to-all-done.5 = bf16[16,32,1280]{2,1,0:T(8,128)(2,1)S(1)} async-done(((bf16[16,32,1280]{2,1,0:T(8,128)(2,1)}), bf16[16,32,1280]{2,1,0:T(8,128)(2,1)S(1)}, u32[]{:S(2)}, u32[]{:S(2)}) %all-to-all-start.5) | async-done | bytes 1310752 | tf_op jit(solution)/shard_map/all_to_all | solution.py:86
  204.1 0.2 reduce_sum.47
  204.3 0.1 broadcast_in_dim.80
  204.4 22.7 %all_to_all.43 = bf16[16,32,1280]{2,1,0:T(8,128)(2,1)S(1)} all-to-all(bf16[16,32,1280]{2,1,0:T(8,128)(2,1)S(1)} %broadcast_in_dim.80), channel_id=1, replica_groups=mesh['row'=16,'col'=8] {'row'}, dimensions={0} | all-to-all | bytes 2621440 | tf_op jit(solution)/shard_map/all_to_all | solution.py:98
  227.2 1.5 copy-done.8
  228.7 1.7 fusion.54
  230.4 1.7 collective-permute-start.9
  232.1 1.1 collective-permute-done.9
  233.2 1.7 add_convert_fusion
  234.9 0.7 copy.29
  235.6 3.4 %all-to-all-start.7 = ((bf16[4,3,64,128]{3,2,1,0:T(8,128)(2,1)}), bf16[4,3,64,128]{3,2,1,0:T(8,128)(2,1)S(1)}, u32[]{:S(2)}, u32[]{:S(2)}) async-start(bf16[4,3,64,128]{3,2,1,0:T(8,128)(2,1)} %bitcast.182), calls=%async_computation.7 | async-start | bytes 393216 | tf_op jit(solution)/shard_map/all_to_all | solution.py:121
  239.0 0.9 constant_dynamic-slice_fusion
  240.0 4.3 %shard_map.52 = bf16[3,1280,512]{2,1,0:T(8,128)(2,1)} custom-call(s32[1]{0:T(128)} %bitcast.core_ref, bf16[2,4,64,1280]{3,2,1,0:T(8,128)(2,1)} %bitcast.188, bf16[3,1280,512]{2,1,0:T(8,128)(2,1)} %shard_map.51.outs_ref), custom_call_target="tpu_custom_call", output_to_operand_aliasing={{}: (2, {})} | custom-call | bytes 2621440 | tf_op jit(solution)/shard_map/pallas_call | solution.py:30
  244.3 0.1 all-to-all-done.7
  244.4 0.9 slice_subtract_fusion
  245.3 0.9 maximum_bitcast_fusion
  (28 shorter events, 0.8 us)
Async XLA Ops:
  13.5 3.5 %collective-permute-start = (bf16[5,256,128]{2,1,0:T(8,128)(2,1)S(1)}, bf16[5,256,128]{2,1,0:T(8,128)(2,1)S(1)}, u32[]{:S(2)}, u32[]{:S(2)}) collective-permute-start(bf16[5,256,128]{2,1,0:T(8,128)(2,1)S(1)} %bitcast.200), channel_id=1, source_target_pairs={{0,1},{1,0},{2,3},{3,2},{4,5},{5,4},{6,7},{7,6},{8,9},{9,8},{10,11... | collective-permute-start | bytes 983048 | tf_op jit(solution)/shard_map/ppermute | solution.py:13
  47.0 21.9 %all-to-all-start.2 = ((bf16[16,32,1280]{2,1,0:T(8,128)(2,1)}), bf16[16,32,1280]{2,1,0:T(8,128)(2,1)S(1)}, u32[]{:S(2)}, u32[]{:S(2)}) async-start(bf16[16,32,1280]{2,1,0:T(8,128)(2,1)} %broadcast_in_dim.77), calls=%async_computation.2 | async-start | bytes 2621440 | tf_op jit(solution)/shard_map/all_to_all | solution.py:98
  68.9 2.7 %copy-start = (bf16[16,32,1280]{2,1,0:T(8,128)(2,1)}, bf16[16,32,1280]{2,1,0:T(8,128)(2,1)S(1)}, u32[]{:S(2)}) copy-start(bf16[16,32,1280]{2,1,0:T(8,128)(2,1)S(1)} %all-to-all-done.2) | copy-start | bytes 3932164
  69.0 6.2 %copy-start.5 = (f32[64,18,128]{2,0,1:T(8,128)S(1)}, f32[64,18,128]{2,0,1:T(8,128)}, u32[]{:S(2)}) copy-start(f32[64,18,128]{2,0,1:T(8,128)} %param.3) | copy-start | bytes 1769476
  71.6 4.7 %collective-permute-start.1 = (bf16[5,256,128]{2,1,0:T(8,128)(2,1)S(1)}, bf16[5,256,128]{2,1,0:T(8,128)(2,1)S(1)}, u32[]{:S(2)}, u32[]{:S(2)}) collective-permute-start(bf16[5,256,128]{2,1,0:T(8,128)(2,1)S(1)} %fusion.51), channel_id=1, source_target_pairs={{0,1},{1,0},{2,3},{3,2},{4,5},{5,4},{6,7},{7,6},{8,9},{9,8},{10,11... | collective-permute-start | bytes 983048 | tf_op jit(solution)/shard_map/ppermute | solution.py:13
  78.5 7.2 %collective-permute-start.2 = (bf16[5,256,128]{2,1,0:T(8,128)(2,1)S(1)}, bf16[5,256,128]{2,1,0:T(8,128)(2,1)S(1)}, u32[]{:S(2)}, u32[]{:S(2)}) collective-permute-start(bf16[5,256,128]{2,1,0:T(8,128)(2,1)S(1)} %get-tuple-element.29), channel_id=1, source_target_pairs={{0,2},{1,7},{2,0},{3,5},{4,6},{5,3},{6,4},{7,1},{8,10},{9,15},{10,... | collective-permute-start | bytes 983048 | tf_op jit(solution)/shard_map/ppermute | solution.py:13
  86.0 6.3 %collective-permute-start.3 = (bf16[5,256,128]{2,1,0:T(8,128)(2,1)S(1)}, bf16[5,256,128]{2,1,0:T(8,128)(2,1)S(1)}, u32[]{:S(2)}, u32[]{:S(2)}) collective-permute-start(bf16[5,256,128]{2,1,0:T(8,128)(2,1)S(1)} %fusion.76), channel_id=1, source_target_pairs={{0,6},{1,3},{2,4},{3,1},{4,2},{5,7},{6,0},{7,5},{8,14},{9,11},{10,... | collective-permute-start | bytes 983048 | tf_op jit(solution)/shard_map/ppermute | solution.py:13
  92.6 3.7 %collective-permute-start.4 = (bf16[5,256,128]{2,1,0:T(8,128)(2,1)S(1)}, bf16[5,256,128]{2,1,0:T(8,128)(2,1)S(1)}, u32[]{:S(2)}, u32[]{:S(2)}) collective-permute-start(bf16[5,256,128]{2,1,0:T(8,128)(2,1)S(1)} %get-tuple-element.18), channel_id=1, source_target_pairs={{0,1},{1,0},{2,3},{3,2},{4,5},{5,4},{6,7},{7,6},{8,9},{9,8},{10,11... | collective-permute-start | bytes 983048 | tf_op jit(solution)/shard_map/ppermute | solution.py:13
  100.0 25.1 %all-to-all-start.3 = ((bf16[16,32,1280]{2,1,0:T(8,128)(2,1)}), bf16[16,32,1280]{2,1,0:T(8,128)(2,1)S(1)}, u32[]{:S(2)}, u32[]{:S(2)}) async-start(bf16[16,32,1280]{2,1,0:T(8,128)(2,1)} %bitcast.18), calls=%async_computation.3 | async-start | bytes 2621440 | tf_op jit(solution)/shard_map/all_to_all | solution.py:86
  106.0 4.3 %copy-start.1 = (bf16[16,32,1280]{2,1,0:T(8,128)(2,1)S(1)}, bf16[16,32,1280]{2,1,0:T(8,128)(2,1)}, u32[]{:S(2)}) copy-start(bf16[16,32,1280]{2,1,0:T(8,128)(2,1)} %copy-done) | copy-start | bytes 3932164
  148.0 3.9 %copy-start.2 = (bf16[16,32,1280]{2,1,0:T(8,128)(2,1)}, bf16[16,32,1280]{2,1,0:T(8,128)(2,1)S(1)}, u32[]{:S(2)}) copy-start(bf16[16,32,1280]{2,1,0:T(8,128)(2,1)S(1)} %all_to_all.42) | copy-start | bytes 3932164
  148.0 1.8 copy-start.7
  151.9 2.9 %collective-permute-start.5 = (bf16[5,256,128]{2,1,0:T(8,128)(2,1)S(1)}, bf16[5,256,128]{2,1,0:T(8,128)(2,1)S(1)}, u32[]{:S(2)}, u32[]{:S(2)}) collective-permute-start(bf16[5,256,128]{2,1,0:T(8,128)(2,1)S(1)} %fusion.43), channel_id=1, source_target_pairs={{0,1},{1,0},{2,3},{3,2},{4,5},{5,4},{6,7},{7,6},{8,9},{9,8},{10,11... | collective-permute-start | bytes 983048 | tf_op jit(solution)/shard_map/ppermute | solution.py:13
  157.1 7.2 %collective-permute-start.6 = (bf16[5,256,128]{2,1,0:T(8,128)(2,1)S(1)}, bf16[5,256,128]{2,1,0:T(8,128)(2,1)S(1)}, u32[]{:S(2)}, u32[]{:S(2)}) collective-permute-start(bf16[5,256,128]{2,1,0:T(8,128)(2,1)S(1)} %get-tuple-element.31), channel_id=1, source_target_pairs={{0,2},{1,7},{2,0},{3,5},{4,6},{5,3},{6,4},{7,1},{8,10},{9,15},{10,... | collective-permute-start | bytes 983048 | tf_op jit(solution)/shard_map/ppermute | solution.py:13
  164.4 6.3 %collective-permute-start.7 = (bf16[5,256,128]{2,1,0:T(8,128)(2,1)S(1)}, bf16[5,256,128]{2,1,0:T(8,128)(2,1)S(1)}, u32[]{:S(2)}, u32[]{:S(2)}) collective-permute-start(bf16[5,256,128]{2,1,0:T(8,128)(2,1)S(1)} %fusion.77), channel_id=1, source_target_pairs={{0,6},{1,3},{2,4},{3,1},{4,2},{5,7},{6,0},{7,5},{8,14},{9,11},{10,... | collective-permute-start | bytes 983048 | tf_op jit(solution)/shard_map/ppermute | solution.py:13
  171.7 3.6 %collective-permute-start.8 = (bf16[5,256,128]{2,1,0:T(8,128)(2,1)S(1)}, bf16[5,256,128]{2,1,0:T(8,128)(2,1)S(1)}, u32[]{:S(2)}, u32[]{:S(2)}) collective-permute-start(bf16[5,256,128]{2,1,0:T(8,128)(2,1)S(1)} %get-tuple-element.16), channel_id=1, source_target_pairs={{0,1},{1,0},{2,3},{3,2},{4,5},{5,4},{6,7},{7,6},{8,9},{9,8},{10,11... | collective-permute-start | bytes 983048 | tf_op jit(solution)/shard_map/ppermute | solution.py:13
  179.0 25.1 %all-to-all-start.5 = ((bf16[16,32,1280]{2,1,0:T(8,128)(2,1)}), bf16[16,32,1280]{2,1,0:T(8,128)(2,1)S(1)}, u32[]{:S(2)}, u32[]{:S(2)}) async-start(bf16[16,32,1280]{2,1,0:T(8,128)(2,1)} %bitcast.36), calls=%async_computation.5 | async-start | bytes 2621440 | tf_op jit(solution)/shard_map/all_to_all | solution.py:86
  182.9 4.4 %copy-start.3 = (bf16[16,32,1280]{2,1,0:T(8,128)(2,1)S(1)}, bf16[16,32,1280]{2,1,0:T(8,128)(2,1)}, u32[]{:S(2)}) copy-start(bf16[16,32,1280]{2,1,0:T(8,128)(2,1)} %copy-done.2) | copy-start | bytes 3932164
  227.1 3.4 %copy-start.4 = (bf16[16,32,1280]{2,1,0:T(8,128)(2,1)}, bf16[16,32,1280]{2,1,0:T(8,128)(2,1)S(1)}, u32[]{:S(2)}) copy-start(bf16[16,32,1280]{2,1,0:T(8,128)(2,1)S(1)} %all_to_all.43) | copy-start | bytes 3932164
  227.1 1.6 copy-start.8
  230.4 2.8 %collective-permute-start.9 = (bf16[3,256,128]{2,1,0:T(8,128)(2,1)S(1)}, bf16[3,256,128]{2,1,0:T(8,128)(2,1)S(1)}, u32[]{:S(2)}, u32[]{:S(2)}) collective-permute-start(bf16[3,256,128]{2,1,0:T(8,128)(2,1)S(1)} %fusion.54), channel_id=1, source_target_pairs={{0,1},{1,0},{2,3},{3,2},{4,5},{5,4},{6,7},{7,6},{8,9},{9,8},{10,11... | collective-permute-start | bytes 589832 | tf_op jit(solution)/shard_map/ppermute | solution.py:13
  235.6 8.8 %all-to-all-start.7 = ((bf16[4,3,64,128]{3,2,1,0:T(8,128)(2,1)}), bf16[4,3,64,128]{3,2,1,0:T(8,128)(2,1)S(1)}, u32[]{:S(2)}, u32[]{:S(2)}) async-start(bf16[4,3,64,128]{3,2,1,0:T(8,128)(2,1)} %bitcast.182), calls=%async_computation.7 | async-start | bytes 393216 | tf_op jit(solution)/shard_map/all_to_all | solution.py:121
  240.0 5.4 %copy-start.6 = (f32[5,64,128]{2,1,0:T(8,128)S(1)}, f32[5,64,128]{2,1,0:T(8,128)}, u32[]{:S(2)}) copy-start(f32[5,64,128]{2,1,0:T(8,128)} %get-tuple-element.26) | copy-start | bytes 491524

commit v4 on v0

v4 whole, which is shorter than its diff:
```python
import jax
import jax.numpy as jnp
from jax import lax
from jax.experimental import pallas as pl
from jax.experimental.pallas import tpu as pltpu
from jax.sharding import PartitionSpec as P

BF16 = jnp.bfloat16
F32 = jnp.float32


class Places:
    def __init__(self):
        self.n_row = lax.axis_size("row")
        self.n_col = lax.axis_size("col")
        self.n_z = self.n_col // 2

    def column_groups(self):
        return [[2 * z + k for z in range(self.n_z)] for k in range(2)]

    def swap(self, block, masks):
        return lax.ppermute(block, "col", [(c, c ^ masks[c % 2]) for c in range(self.n_col)])


def tied(first, *others):
    return lax.optimization_barrier((first,) + others)


def add_up(parts):
    return jnp.sum(parts.astype(F32), axis=0)


def copies_of(block, count):
    return jnp.broadcast_to(block[None], (count,) + block.shape)


def place_kernel(core_ref, own_ref, other_ref, *refs):
    placed_ref = refs[-1]
    chunk = placed_ref.shape[2] // 8
    own_first = core_ref[0] == 0
    for z in range(own_ref.shape[0] // chunk):
        own = own_ref[z * chunk : (z + 1) * chunk]
        other = other_ref[z * chunk : (z + 1) * chunk]
        pair = jnp.concatenate([jnp.where(own_first, own, other), jnp.where(own_first, other, own)], axis=0)
        placed_ref[0, :, z * 2 * chunk : (z + 1) * 2 * chunk] = pair.T


def place(core, both, crossed, outs, step, steps):
    half, width = crossed.shape
    tile = width // 5
    block = pl.BlockSpec((half, tile), lambda i: (0, i))
    given = [core, both, crossed] + ([] if outs is None else [outs])
    return pl.pallas_call(
        place_kernel,
        grid=(width // tile,),
        in_specs=[pl.BlockSpec(memory_space=pltpu.SMEM), block, block] + [pl.BlockSpec(memory_space=pl.ANY)] * (len(given) - 3),
        out_specs=pl.BlockSpec((1, tile, 2 * half), lambda i: (step, i, 0)),
        out_shape=jax.ShapeDtypeStruct((steps, width, 2 * half), BF16),
        input_output_aliases={} if outs is None else {3: 0},
        cost_estimate=pl.CostEstimate(flops=0, bytes_accessed=8 * half * width, transcendentals=0),
    )(*given)


def inverse_times(current, inverse):
    return lax.dot_general(current, inverse, (((0, 2), (0, 2)), ((), ())), preferred_element_type=F32).astype(BF16)


def factor_times(solved, block):
    out = lax.dot_general(solved, block, (((1,), (2,)), ((), ())), preferred_element_type=F32)
    return out.transpose(1, 0, 2)


def local(noise, factor, dinv):
    steps, width, rounds, lanes = dinv.shape
    at = Places()
    n_z, n_col, n_row = at.n_z, at.n_col, at.n_row
    chunk, total, _ = noise.shape
    half = chunk * n_z
    my_z = lax.axis_index("col") // 2
    core = (lax.axis_index("col") % 2).astype(jnp.int32).reshape(1)
    noise = noise.transpose(1, 0, 2)
    dinv = dinv.transpose(0, 2, 1, 3).reshape(steps * rounds, width, lanes)
    factor = factor.transpose(0, 2, 1, 3).reshape(total - rounds, steps * lanes, width)
    bounds = [(s * rounds, min((s + 1) * rounds, total)) for s in range(steps + 1)]
    partner = (1, 1)

    dinv_theirs = at.swap(dinv, partner)
    first = noise[:rounds].astype(BF16)
    current = lax.all_to_all(copies_of(first, n_z), "col", 0, 0, tiled=True, axis_index_groups=at.column_groups())
    current = current.transpose(1, 0, 2, 3).reshape(rounds, half, lanes)
    done = [noise[:rounds]]
    later = {}
    outs = None
    solved = None
    for s in range(steps):
        lo, hi = bounds[s + 1]
        if s == 0:
            products = jnp.concatenate([inverse_times(current, dinv[:rounds]), inverse_times(current, dinv_theirs[:rounds])], axis=1)
            products, factor, noise = tied(products, factor, noise)
            factor_theirs = at.swap(factor, partner)
        else:
            products = inverse_times(current, inverse)
        products, before = tied(products, solved) if s > 0 else (products, None)
        received = lax.all_to_all(products.reshape(n_row, half // n_row, 2 * width), "row", 0, 0, tiled=True)
        if s > 0:
            for n in range(s + 1, steps + 1):
                start, end = bounds[n]
                for mine, source in enumerate((factor_theirs, factor)):
                    columns = before[:, :width] if mine else before[:, width:]
                    more = factor_times(columns, source[start - rounds : end - rounds, (s - 1) * lanes : s * lanes])
                    later[n] = more if n not in later else later[n] + more
            outs = place(core, before, at.swap(before[:, width:], partner), outs, s - 1, steps)
            received, outs, *held = tied(received, outs, *[later[n] for n in range(s + 1, steps + 1)])
            later.update(zip(range(s + 1, steps + 1), held))
        solved = jnp.sum(received.astype(F32), axis=0).astype(BF16)
        copies, factor, factor_theirs, dinv, dinv_theirs = tied(copies_of(solved, n_row), factor, factor_theirs, dinv, dinv_theirs)
        solved = lax.all_to_all(copies, "row", 0, 0, tiled=True)
        block = jnp.concatenate([f[lo - rounds : hi - rounds, s * lanes : (s + 1) * lanes] for f in (factor, factor_theirs)], axis=2)
        if s + 1 < steps:
            inverse = jnp.concatenate([d[(s + 1) * rounds : (s + 2) * rounds] for d in (dinv, dinv_theirs)], axis=1)
            solved, block, inverse = tied(solved, block, inverse)
        else:
            solved, block = tied(solved, block)
        solved = solved.reshape(half, 2 * width)

        update = factor_times(solved, block)
        if s > 0:
            update = update + later[s + 1]
        if s + 1 < steps:
            spread = update.reshape(hi - lo, n_z, chunk, lanes)
            here = (lax.iota(jnp.int32, n_z) == my_z)[None, :, None, None]
            work = (jnp.where(here, noise[lo:hi][:, None], 0.0) - spread).reshape(hi - lo, half, lanes)
            work = work + at.swap(work.astype(BF16), (2, n_col - 2)).astype(F32)
            work = work + at.swap(work.astype(BF16), (n_col - 2, 2)).astype(F32)
            done.append(lax.dynamic_slice_in_dim(work, my_z * chunk, chunk, axis=1))
            current = work.astype(BF16)
        else:
            parts = update.astype(BF16).reshape(hi - lo, n_z, chunk, lanes).transpose(1, 0, 2, 3)
            parts, last = tied(parts, solved)
            got = lax.all_to_all(parts, "col", 0, 0, tiled=True, axis_index_groups=at.column_groups())
            outs = place(core, last, at.swap(last[:, width:], partner), outs, s, steps)
            got, outs = tied(got, outs)
            done.append(noise[lo:hi] - add_up(got))
    return outs, jnp.concatenate(done, axis=0).transpose(1, 0, 2)


def solution(mesh):
    placed = (P("col", None, "row"), P(None, "row", None, "col"), P(None, "col", None, "row"))
    return jax.shard_map(
        local,
        mesh=mesh,
        in_specs=placed,
        out_specs=(P(None, "col", None), P("col", None, "row")),
        check_vma=False,
    )
```

time: 463 us -> 233 us (0.50)
  blocking collectives: 302 us -> 38.1 us
  starting transfers between devices: 0.12 us -> 45.8 us
  waiting for transfers between devices: 109 us -> 66.7 us
  local copies, waits for them, and re-layouts: 1.92 us -> 27.8 us
  Pallas kernels: 0 us -> 13 us
  between operations: 13.8 us -> 1.07 us
    psum x3 -> x0, blocking collectives: 253 us -> none  [local(): solution = lax.psum(partial_sum, 'row').astype(jnp.bfloat16)]
    reduce_scatter x3 -> x0, waiting for transfers between devices: 109 us -> none  [local(): lax.psum_scatter(lax.dot_general(solution_wide, panel_rows, (((0,), (2,))...]
    all_gather x3 -> x0, blocking collectives: 49.5 us -> none  [local(): lax.all_gather(current, 'col', axis=0, tiled=True).astype(jnp.float32)]
    all_to_all x0 -> x6, waiting for transfers between devices: none -> 42.1 us  [the longest x3 39.1 us: local(): solved = lax.all_to_all(copies, 'row', 0, 0, tiled=True)]
    all_to_all x0 -> x2, blocking collectives: none -> 38.1 us  [the longest x1 26.2 us: local(): lax.all_to_all(products.reshape(n_row, half // n_row, 2 * width), 'row',...]
    all_to_all x0 -> x6, starting transfers between devices: none -> 28.6 us  [the longest x3 15.8 us: local(): solved = lax.all_to_all(copies, 'row', 0, 0, tiled=True)]
    ppermute x0 -> x9, waiting for transfers between devices: none -> 24.6 us  [swap(): lax.ppermute(block, 'col', [(c, c ^ masks[c % 2]) for c in range(self.n_c...]
    ppermute x0 -> x9, starting transfers between devices: none -> 17.2 us  [swap(): lax.ppermute(block, 'col', [(c, c ^ masks[c % 2]) for c in range(self.n_c...]
  transfers between devices with their start and end apart: 3 -> 15, of which waited for: 3 -> 8; matrix products, arithmetic and copies ran while one was open for 1% -> 18% of each run, Pallas kernels for 0% -> 6%
where the time goes in v4:
time: 233 us; the launch traced here: 231 us
  waiting for transfers between devices  66.7 us (29%)
  starting transfers between devices  45.8 us (20%)
  blocking collectives  38.1 us (16%)
  matrix products  29.5 us (13%)
  local copies, waits for them, and re-layouts  27.8 us (12%)
  Pallas kernels  13 us (6%)
  other arithmetic  9.24 us (4%)
    all_to_all x3, waiting for transfers between devices, local(): solved = lax.all_to_all(copies, 'row', 0, 0, tiled=True)  39.1 us
    all_to_all x1, blocking collectives, local(): lax.all_to_all(products.reshape(n_row, half // n_row, 2 * width), 'row',...  26.2 us
    ppermute x9, waiting for transfers between devices, swap(): lax.ppermute(block, 'col', [(c, c ^ masks[c % 2]) for c in range(self.n_c...  24.6 us
    dot_general x9, matrix products, factor_times(): lax.dot_general(solved, block, (((1,), (2,)), ((), ())), preferred_elemen...  22.1 us
    ppermute x9, starting transfers between devices, swap(): lax.ppermute(block, 'col', [(c, c ^ masks[c % 2]) for c in range(self.n_c...  17.2 us
    all_to_all x3, starting transfers between devices, local(): solved = lax.all_to_all(copies, 'row', 0, 0, tiled=True)  15.8 us
    pallas_call x3, Pallas kernels, place(): pl.pallas_call(place_kernel, grid=(width // tile,), in_specs=[pl.BlockSpe...  13 us
    all_to_all x1, blocking collectives, local(): lax.all_to_all(copies_of(first, n_z), 'col', 0, 0, tiled=True, axis_index...  11.8 us
  transfers between devices with their start and end apart: 15, of which 8 were waited for; matrix products, arithmetic and copies ran while one was open for 18% of the time, Pallas kernels for 6%

profile of v4, /device:TPU:1, one launch (start us, length us, event | category | flops | bytes accessed | tf_op | source)
XLA Modules:
  0.0 231.2 jit_solution(10153300851447154594)
XLA Ops:
  0.6 1.5 collective-permute-start
  2.1 0.9 slice.166
  3.1 11.8 %all_to_all.40 = bf16[4,5,64,128]{3,2,1,0:T(8,128)(2,1)S(1)} all-to-all(bf16[4,5,64,128]{3,2,1,0:T(8,128)(2,1)S(1)} %broadcast_in_dim.68), channel_id=1, replica_groups={{0,2,4,6},{1,3,5,7},{8,10,12,14},{9,11,13,15},{16,18,20,22},{17,19,21,2..., dimensions={0} | all-to-all | bytes 655360 | tf_op jit(solution)/shard_map/all_to_all | solution.py:89
  15.0 2.1 fusion.2
  17.2 2.2 copy-done.1
  20.1 1.5 collective-permute-start.1
  21.6 26.2 %all_to_all.41 = bf16[16,16,2560]{2,1,0:T(8,128)(2,1)S(1)} all-to-all(bf16[16,16,2560]{2,1,0:T(8,128)(2,1)S(1)} %bitcast.101), channel_id=1, replica_groups=mesh['row'=16,'col'=8] {'row'}, dimensions={0} | all-to-all | bytes 2621440 | tf_op jit(solution)/shard_map/all_to_all | solution.py:104
  48.1 1.2 broadcast_in_dim.74
  49.3 4.4 %all-to-all-start.2 = ((bf16[16,16,2560]{2,1,0:T(8,128)(2,1)}), bf16[16,16,2560]{2,1,0:T(8,128)(2,1)}, u32[]{:S(2)}, u32[]{:S(2)}) async-start(bf16[16,16,2560]{2,1,0:T(8,128)(2,1)} %broadcast_in_dim.74), calls=%async_computation.2 | async-start | bytes 2621440 | tf_op jit(solution)/shard_map/all_to_all | solution.py:117
  53.9 0.9 bitcast_select_fusion
  54.8 1.5 slice.97
  56.4 1.7 slice.95
  58.0 1.5 slice.96
  59.8 2.0 pad_maximum_fusion
  61.8 10.4 %all-to-all-done.2 = bf16[16,16,2560]{2,1,0:T(8,128)(2,1)} async-done(((bf16[16,16,2560]{2,1,0:T(8,128)(2,1)}), bf16[16,16,2560]{2,1,0:T(8,128)(2,1)}, u32[]{:S(2)}, u32[]{:S(2)}) %all-to-all-start.2) | async-done | bytes 1310752 | tf_op jit(solution)/shard_map/all_to_all | solution.py:117
  72.2 3.7 %fusion.42 = (bf16[5,256,128]{2,1,0:T(8,128)(2,1)S(1)}, f32[5,256,128]{2,1,0:T(8,128)S(1)}) fusion(f32[5,256,128]{2,1,0:T(8,128)} %bitcast_select_fusion, bf16[256,2560,1]{1,0,2:T(8,128)(2,1)} %bitcast.15, bf16[5,128,2560]{2,1,0:T(8,128)(2,1)} %pad_maximum_fusion), kind=kOutput, calls=%fused_computation.70 | convolution fusion | flops 839188480 | bytes 6225920 | tf_op jit(solution)/shard_map/dot_general | solution.py:69
  75.9 1.0 collective-permute-start.2
  76.8 6.2 %collective-permute-done.2 = bf16[5,256,128]{2,1,0:T(8,128)(2,1)S(1)} collective-permute-done((bf16[5,256,128]{2,1,0:T(8,128)(2,1)S(1)}, bf16[5,256,128]{2,1,0:T(8,128)(2,1)S(1)}, u32[]{:S(2)}, u32[]{:S(2)}) %collective-permute-start.2) | collective-permute-done | bytes 327712 | tf_op jit(solution)/shard_map/ppermute | solution.py:22
  83.2 5.9 %collective-permute-done.3 = bf16[5,256,128]{2,1,0:T(8,128)(2,1)S(1)} collective-permute-done((bf16[5,256,128]{2,1,0:T(8,128)(2,1)S(1)}, bf16[5,256,128]{2,1,0:T(8,128)(2,1)S(1)}, u32[]{:S(2)}, u32[]{:S(2)}) %collective-permute-start.3) | collective-permute-done | bytes 327712 | tf_op jit(solution)/shard_map/ppermute | solution.py:22
  89.3 2.3 fusion
  91.6 5.7 %all-to-all-start.3 = ((bf16[16,16,2560]{2,1,0:T(8,128)(2,1)}), bf16[16,16,2560]{2,1,0:T(8,128)(2,1)S(1)}, u32[]{:S(2)}, u32[]{:S(2)}) async-start(bf16[16,16,2560]{2,1,0:T(8,128)(2,1)} %bitcast.99), calls=%async_computation.3 | async-start | bytes 2621440 | tf_op jit(solution)/shard_map/all_to_all | solution.py:104
  97.3 1.1 slice.99
  98.4 3.6 %collective-permute-start.4 = (bf16[256,1280]{1,0:T(8,128)(2,1)S(1)}, bf16[256,1280]{1,0:T(8,128)(2,1)S(1)}, u32[]{:S(2)}, u32[]{:S(2)}) collective-permute-start(bf16[256,1280]{1,0:T(8,128)(2,1)S(1)} %slice.99), channel_id=1, source_target_pairs={{0,1},{1,0},{2,3},{3,2},{4,5},{5,4},{6,7},{7,6},{8,9},{9,8},{10,11... | collective-permute-start | bytes 1966088 | tf_op jit(solution)/shard_map/ppermute | solution.py:22
  102.0 1.9 fusion.19
  104.0 2.7 %fusion.16 = f32[3,256,128]{2,1,0:T(8,128)} fusion(f32[256,3,128]{2,0,1:T(8,128)S(1)} %fusion.19, bf16[13,384,1280]{2,1,0:T(8,128)(2,1)} %collective-permute-done.1, bf16[256,2560]{1,0:T(8,128)(2,1)} %bitcast.14.own_ref), kind=kOutput, calls=%fused_computation.29 | convolution fusion | flops 251756544 | bytes 2424832 | tf_op jit(solution)/shard_map/dot_general | solution.py:69
  106.6 2.3 %fusion.5 = f32[256,5,128]{2,0,1:T(8,128)S(1)} fusion(bf16[13,384,1280]{2,1,0:T(8,128)(2,1)} %bitcast.109, bf16[256,2560]{1,0:T(8,128)(2,1)} %bitcast.14.own_ref), kind=kOutput, calls=%fused_computation.15 | convolution fusion | flops 419430400 | bytes 2949120 | tf_op jit(solution)/shard_map/dot_general | solution.py:69
  109.0 3.2 %fusion.12 = f32[5,256,128]{2,1,0:T(8,128)} fusion(f32[256,5,128]{2,0,1:T(8,128)S(1)} %fusion.5, bf16[13,384,1280]{2,1,0:T(8,128)(2,1)} %collective-permute-done.1, bf16[256,2560]{1,0:T(8,128)(2,1)} %bitcast.14.own_ref), kind=kOutput, calls=%fused_computation.23 | convolution fusion | flops 419594240 | bytes 3604480 | tf_op jit(solution)/shard_map/dot_general | solution.py:69
  112.2 0.9 copy-done.8
  113.1 4.3 %shard_map.50.refs_0_ = bf16[3,1280,512]{2,1,0:T(8,128)(2,1)} custom-call(s32[1]{0:T(128)} %bitcast.19.core_ref, bf16[256,2560]{1,0:T(8,128)(2,1)} %bitcast.14.own_ref, bf16[256,1280]{1,0:T(8,128)(2,1)} %copy-done.8), custom_call_target="tpu_custom_call" | custom-call | bytes 2621440 | tf_op jit(solution)/shard_map/pallas_call | solution.py:53
  117.6 1.2 broadcast_in_dim.75
  118.8 6.9 %all-to-all-start.4 = ((bf16[16,16,2560]{2,1,0:T(8,128)(2,1)}), bf16[16,16,2560]{2,1,0:T(8,128)(2,1)}, u32[]{:S(2)}, u32[]{:S(2)}) async-start(bf16[16,16,2560]{2,1,0:T(8,128)(2,1)} %broadcast_in_dim.75), calls=%async_computation.4 | async-start | bytes 2621440 | tf_op jit(solution)/shard_map/all_to_all | solution.py:117
  125.7 1.5 slice.107
  127.2 1.7 slice.105
  128.9 1.5 slice.106
  130.7 1.9 pad_maximum_fusion.2
  132.6 14.7 %all-to-all-done.4 = bf16[16,16,2560]{2,1,0:T(8,128)(2,1)} async-done(((bf16[16,16,2560]{2,1,0:T(8,128)(2,1)}), bf16[16,16,2560]{2,1,0:T(8,128)(2,1)}, u32[]{:S(2)}, u32[]{:S(2)}) %all-to-all-start.4) | async-done | bytes 1310752 | tf_op jit(solution)/shard_map/all_to_all | solution.py:117
  147.3 3.6 %convolution_bitcast_fusion.4 = f32[5,256,128]{2,1,0:T(8,128)S(1)} fusion(bf16[256,2560,1]{1,0,2:T(8,128)(2,1)} %bitcast.25, bf16[5,128,2560]{2,1,0:T(8,128)(2,1)} %pad_maximum_fusion.2), kind=kOutput, calls=%fused_computation.20 | convolution fusion | flops 838860800 | bytes 5242880 | tf_op jit(solution)/shard_map/dot_general | solution.py:69
  151.2 1.0 collective-permute-start.5
  152.2 6.2 %collective-permute-done.5 = bf16[5,256,128]{2,1,0:T(8,128)(2,1)S(1)} collective-permute-done((bf16[5,256,128]{2,1,0:T(8,128)(2,1)S(1)}, bf16[5,256,128]{2,1,0:T(8,128)(2,1)S(1)}, u32[]{:S(2)}, u32[]{:S(2)}) %collective-permute-start.5) | collective-permute-done | bytes 327712 | tf_op jit(solution)/shard_map/ppermute | solution.py:22
  158.7 6.2 %collective-permute-done.6 = bf16[5,256,128]{2,1,0:T(8,128)(2,1)S(1)} collective-permute-done((bf16[5,256,128]{2,1,0:T(8,128)(2,1)S(1)}, bf16[5,256,128]{2,1,0:T(8,128)(2,1)S(1)}, u32[]{:S(2)}, u32[]{:S(2)}) %collective-permute-start.6) | collective-permute-done | bytes 327712 | tf_op jit(solution)/shard_map/ppermute | solution.py:22
  165.0 2.3 fusion.1
  167.3 3.7 %all-to-all-start.5 = ((bf16[16,16,2560]{2,1,0:T(8,128)(2,1)}), bf16[16,16,2560]{2,1,0:T(8,128)(2,1)S(1)}, u32[]{:S(2)}, u32[]{:S(2)}) async-start(bf16[16,16,2560]{2,1,0:T(8,128)(2,1)} %bitcast.100), calls=%async_computation.5 | async-start | bytes 2621440 | tf_op jit(solution)/shard_map/all_to_all | solution.py:104
  171.0 1.1 slice.109
  172.2 3.2 %collective-permute-start.7 = (bf16[256,1280]{1,0:T(8,128)(2,1)S(1)}, bf16[256,1280]{1,0:T(8,128)(2,1)S(1)}, u32[]{:S(2)}, u32[]{:S(2)}) collective-permute-start(bf16[256,1280]{1,0:T(8,128)(2,1)S(1)} %slice.109), channel_id=1, source_target_pairs={{0,1},{1,0},{2,3},{3,2},{4,5},{5,4},{6,7},{7,6},{8,9},{9,8},{10,11... | collective-permute-start | bytes 1966088 | tf_op jit(solution)/shard_map/ppermute | solution.py:22
  175.4 1.9 convolution_bitcast_fusion.8
  177.3 1.9 convolution_bitcast_fusion.7
  180.1 0.8 copy-done.7
  180.9 4.3 %shard_map.51.refs_0_ = bf16[3,1280,512]{2,1,0:T(8,128)(2,1)} custom-call(s32[1]{0:T(128)} %bitcast.19.core_ref, bf16[256,2560]{1,0:T(8,128)(2,1)} %bitcast.24.own_ref, bf16[256,1280]{1,0:T(8,128)(2,1)} %copy-done.7, bf16[3,1280,512]{2,1,0:T(8,128)(2,1)} %shard_map.50.refs_0_), custom_call_target="tpu_custom_call", output_to_operand_aliasing={{}: (3, {})} | custom-call | bytes 2621440 | tf_op jit(solution)/shard_map/pallas_call | solution.py:53
  185.2 3.0 %all-to-all-done.5 = bf16[16,16,2560]{2,1,0:T(8,128)(2,1)S(1)} async-done(((bf16[16,16,2560]{2,1,0:T(8,128)(2,1)}), bf16[16,16,2560]{2,1,0:T(8,128)(2,1)S(1)}, u32[]{:S(2)}, u32[]{:S(2)}) %all-to-all-start.5) | async-done | bytes 1310752 | tf_op jit(solution)/shard_map/all_to_all | solution.py:104
  188.4 1.2 broadcast_in_dim.76
  189.6 4.5 %all-to-all-start.6 = ((bf16[16,16,2560]{2,1,0:T(8,128)(2,1)}), bf16[16,16,2560]{2,1,0:T(8,128)(2,1)S(1)}, u32[]{:S(2)}, u32[]{:S(2)}) async-start(bf16[16,16,2560]{2,1,0:T(8,128)(2,1)} %broadcast_in_dim.76), calls=%async_computation.6 | async-start | bytes 2621440 | tf_op jit(solution)/shard_map/all_to_all | solution.py:117
  194.1 1.3 slice.113
  195.4 1.3 slice.114
  196.8 14.0 %all-to-all-done.6 = bf16[16,16,2560]{2,1,0:T(8,128)(2,1)S(1)} async-done(((bf16[16,16,2560]{2,1,0:T(8,128)(2,1)}), bf16[16,16,2560]{2,1,0:T(8,128)(2,1)S(1)}, u32[]{:S(2)}, u32[]{:S(2)}) %all-to-all-start.6) | async-done | bytes 1310752 | tf_op jit(solution)/shard_map/all_to_all | solution.py:117
  210.9 0.9 convolution_bitcast_fusion.6
  212.9 5.0 %collective-permute-start.8 = (bf16[256,1280]{1,0:T(8,128)(2,1)S(1)}, bf16[256,1280]{1,0:T(8,128)(2,1)S(1)}, u32[]{:S(2)}, u32[]{:S(2)}) collective-permute-start(bf16[256,1280]{1,0:T(8,128)(2,1)S(1)} %slice.115), channel_id=1, source_target_pairs={{0,1},{1,0},{2,3},{3,2},{4,5},{5,4},{6,7},{7,6},{8,9},{9,8},{10,11... | collective-permute-start | bytes 1966088 | tf_op jit(solution)/shard_map/ppermute | solution.py:22
  217.9 0.9 slice.117
  218.9 3.4 %all-to-all-start.7 = ((bf16[4,3,64,128]{3,2,1,0:T(8,128)(2,1)}), bf16[4,3,64,128]{3,2,1,0:T(8,128)(2,1)S(1)}, u32[]{:S(2)}, u32[]{:S(2)}) async-start(bf16[4,3,64,128]{3,2,1,0:T(8,128)(2,1)} %bitcast.95), calls=%async_computation.7 | async-start | bytes 393216 | tf_op jit(solution)/shard_map/all_to_all | solution.py:140
  222.3 0.9 constant_dynamic-slice_fusion.1
  223.2 0.9 constant_dynamic-slice_fusion
  224.2 0.9 copy-done.6
  225.0 4.3 %shard_map.52 = bf16[3,1280,512]{2,1,0:T(8,128)(2,1)} custom-call(s32[1]{0:T(128)} %bitcast.19.core_ref, bf16[256,2560]{1,0:T(8,128)(2,1)} %bitcast.98, bf16[256,1280]{1,0:T(8,128)(2,1)} %copy-done.6, bf16[3,1280,512]{2,1,0:T(8,128)(2,1)} %shard_map.51.refs_0_), custom_call_target="tpu_custom_call", output_to_operand_aliasing={{}: (3, {})} | custom-call | bytes 2621440 | tf_op jit(solution)/shard_map/pallas_call | solution.py:53
  229.4 0.9 slice_subtract_fusion
  230.3 0.9 maximum_bitcast_fusion
  (55 shorter events, 5.1 us)
Async XLA Ops:
  0.6 16.5 %collective-permute-start = (bf16[15,1280,128]{2,1,0:T(8,128)(2,1)}, bf16[15,1280,128]{2,1,0:T(8,128)(2,1)S(1)}, u32[]{:S(2)}, u32[]{:S(2)}) collective-permute-start(bf16[15,1280,128]{2,1,0:T(8,128)(2,1)} %bitcast.102), channel_id=1, source_target_pairs={{0,1},{1,0},{2,3},{3,2},{4,5},{5,4},{6,7},{7,6},{8,9},{9,8},{10,11... | collective-permute-start | bytes 14745608 | tf_op jit(solution)/shard_map/ppermute | solution.py:22
  17.1 2.2 copy-start.1
  20.1 27.9 %collective-permute-start.1 = (bf16[13,384,1280]{2,1,0:T(8,128)(2,1)}, bf16[13,384,1280]{2,1,0:T(8,128)(2,1)}, u32[]{:S(2)}, u32[]{:S(2)}) collective-permute-start(bf16[13,384,1280]{2,1,0:T(8,128)(2,1)} %bitcast.106), channel_id=1, source_target_pairs={{0,1},{1,0},{2,3},{3,2},{4,5},{5,4},{6,7},{7,6},{8,9},{9,8},{10,11... | collective-permute-start | bytes 38338568 | tf_op jit(solution)/shard_map/ppermute | solution.py:22
  47.9 6.0 %copy-start.5 = (f32[64,18,128]{2,0,1:T(8,128)S(1)}, f32[64,18,128]{2,0,1:T(8,128)}, u32[]{:S(2)}) copy-start(f32[64,18,128]{2,0,1:T(8,128)} %param.3) | copy-start | bytes 1769476
  49.3 22.9 %all-to-all-start.2 = ((bf16[16,16,2560]{2,1,0:T(8,128)(2,1)}), bf16[16,16,2560]{2,1,0:T(8,128)(2,1)}, u32[]{:S(2)}, u32[]{:S(2)}) async-start(bf16[16,16,2560]{2,1,0:T(8,128)(2,1)} %broadcast_in_dim.74), calls=%async_computation.2 | async-start | bytes 2621440 | tf_op jit(solution)/shard_map/all_to_all | solution.py:117
  56.4 3.2 %slice-start = ((bf16[15,1280,128]{2,1,0:T(8,128)(2,1)}), bf16[5,1280,128]{2,1,0:T(8,128)(2,1)S(1)}, s32[]{:S(2)}) async-start(bf16[15,1280,128]{2,1,0:T(8,128)(2,1)} %copy-done.1), calls=%async_computation.8 | async-start | bytes 3276800 | tf_op jit(solution)/shard_map/slice | solution.py:120
  75.9 7.2 %collective-permute-start.2 = (bf16[5,256,128]{2,1,0:T(8,128)(2,1)S(1)}, bf16[5,256,128]{2,1,0:T(8,128)(2,1)S(1)}, u32[]{:S(2)}, u32[]{:S(2)}) collective-permute-start(bf16[5,256,128]{2,1,0:T(8,128)(2,1)S(1)} %get-tuple-element.84), channel_id=1, source_target_pairs={{0,2},{1,7},{2,0},{3,5},{4,6},{5,3},{6,4},{7,1},{8,10},{9,15},{10,... | collective-permute-start | bytes 983048 | tf_op jit(solution)/shard_map/ppermute | solution.py:22
  83.2 6.0 %collective-permute-start.3 = (bf16[5,256,128]{2,1,0:T(8,128)(2,1)S(1)}, bf16[5,256,128]{2,1,0:T(8,128)(2,1)S(1)}, u32[]{:S(2)}, u32[]{:S(2)}) collective-permute-start(bf16[5,256,128]{2,1,0:T(8,128)(2,1)S(1)} %fusion.32), channel_id=1, source_target_pairs={{0,6},{1,3},{2,4},{3,1},{4,2},{5,7},{6,0},{7,5},{8,14},{9,11},{10,... | collective-permute-start | bytes 983048 | tf_op jit(solution)/shard_map/ppermute | solution.py:22
  89.3 2.3 copy-start.2
  91.6 25.8 %all-to-all-start.3 = ((bf16[16,16,2560]{2,1,0:T(8,128)(2,1)}), bf16[16,16,2560]{2,1,0:T(8,128)(2,1)S(1)}, u32[]{:S(2)}, u32[]{:S(2)}) async-start(bf16[16,16,2560]{2,1,0:T(8,128)(2,1)} %bitcast.99), calls=%async_computation.3 | async-start | bytes 2621440 | tf_op jit(solution)/shard_map/all_to_all | solution.py:104
  98.4 13.7 %collective-permute-start.4 = (bf16[256,1280]{1,0:T(8,128)(2,1)S(1)}, bf16[256,1280]{1,0:T(8,128)(2,1)S(1)}, u32[]{:S(2)}, u32[]{:S(2)}) collective-permute-start(bf16[256,1280]{1,0:T(8,128)(2,1)S(1)} %slice.99), channel_id=1, source_target_pairs={{0,1},{1,0},{2,3},{3,2},{4,5},{5,4},{6,7},{7,6},{8,9},{9,8},{10,11... | collective-permute-start | bytes 1966088 | tf_op jit(solution)/shard_map/ppermute | solution.py:22
  112.2 0.9 copy-start.8
  118.8 28.6 %all-to-all-start.4 = ((bf16[16,16,2560]{2,1,0:T(8,128)(2,1)}), bf16[16,16,2560]{2,1,0:T(8,128)(2,1)}, u32[]{:S(2)}, u32[]{:S(2)}) async-start(bf16[16,16,2560]{2,1,0:T(8,128)(2,1)} %broadcast_in_dim.75), calls=%async_computation.4 | async-start | bytes 2621440 | tf_op jit(solution)/shard_map/all_to_all | solution.py:117
  127.2 3.2 %slice-start.1 = ((bf16[15,1280,128]{2,1,0:T(8,128)(2,1)}), bf16[5,1280,128]{2,1,0:T(8,128)(2,1)S(1)}, s32[]{:S(2)}) async-start(bf16[15,1280,128]{2,1,0:T(8,128)(2,1)} %copy-done.1), calls=%async_computation.9 | async-start | bytes 3276800 | tf_op jit(solution)/shard_map/slice | solution.py:120
  147.3 3.6 %copy-start.9 = (f32[5,256,128]{2,1,0:T(8,128)S(1)}, f32[5,256,128]{2,1,0:T(8,128)}, u32[]{:S(2)}) copy-start(f32[5,256,128]{2,1,0:T(8,128)} %fusion.12) | copy-start | bytes 1966084
  151.2 7.2 %collective-permute-start.5 = (bf16[5,256,128]{2,1,0:T(8,128)(2,1)S(1)}, bf16[5,256,128]{2,1,0:T(8,128)(2,1)S(1)}, u32[]{:S(2)}, u32[]{:S(2)}) collective-permute-start(bf16[5,256,128]{2,1,0:T(8,128)(2,1)S(1)} %get-tuple-element.80), channel_id=1, source_target_pairs={{0,2},{1,7},{2,0},{3,5},{4,6},{5,3},{6,4},{7,1},{8,10},{9,15},{10,... | collective-permute-start | bytes 983048 | tf_op jit(solution)/shard_map/ppermute | solution.py:22
  158.5 6.5 %collective-permute-start.6 = (bf16[5,256,128]{2,1,0:T(8,128)(2,1)S(1)}, bf16[5,256,128]{2,1,0:T(8,128)(2,1)S(1)}, u32[]{:S(2)}, u32[]{:S(2)}) collective-permute-start(bf16[5,256,128]{2,1,0:T(8,128)(2,1)S(1)} %fusion.33), channel_id=1, source_target_pairs={{0,6},{1,3},{2,4},{3,1},{4,2},{5,7},{6,0},{7,5},{8,14},{9,11},{10,... | collective-permute-start | bytes 983048 | tf_op jit(solution)/shard_map/ppermute | solution.py:22
  165.0 2.3 copy-start.3
  167.3 20.9 %all-to-all-start.5 = ((bf16[16,16,2560]{2,1,0:T(8,128)(2,1)}), bf16[16,16,2560]{2,1,0:T(8,128)(2,1)S(1)}, u32[]{:S(2)}, u32[]{:S(2)}) async-start(bf16[16,16,2560]{2,1,0:T(8,128)(2,1)} %bitcast.100), calls=%async_computation.5 | async-start | bytes 2621440 | tf_op jit(solution)/shard_map/all_to_all | solution.py:104
  172.2 7.1 %copy-start.10 = (f32[3,256,128]{2,1,0:T(8,128)S(1)}, f32[3,256,128]{2,1,0:T(8,128)}, u32[]{:S(2)}) copy-start(f32[3,256,128]{2,1,0:T(8,128)} %fusion.16) | copy-start | bytes 1179652
  172.2 7.9 %collective-permute-start.7 = (bf16[256,1280]{1,0:T(8,128)(2,1)S(1)}, bf16[256,1280]{1,0:T(8,128)(2,1)S(1)}, u32[]{:S(2)}, u32[]{:S(2)}) collective-permute-start(bf16[256,1280]{1,0:T(8,128)(2,1)S(1)} %slice.109), channel_id=1, source_target_pairs={{0,1},{1,0},{2,3},{3,2},{4,5},{5,4},{6,7},{7,6},{8,9},{9,8},{10,11... | collective-permute-start | bytes 1966088 | tf_op jit(solution)/shard_map/ppermute | solution.py:22
  180.1 0.8 copy-start.7
  189.6 21.2 %all-to-all-start.6 = ((bf16[16,16,2560]{2,1,0:T(8,128)(2,1)}), bf16[16,16,2560]{2,1,0:T(8,128)(2,1)S(1)}, u32[]{:S(2)}, u32[]{:S(2)}) async-start(bf16[16,16,2560]{2,1,0:T(8,128)(2,1)} %broadcast_in_dim.76), calls=%async_computation.6 | async-start | bytes 2621440 | tf_op jit(solution)/shard_map/all_to_all | solution.py:117
  210.9 2.0 copy-start
  210.9 1.3 copy-start.4
  212.9 11.3 %collective-permute-start.8 = (bf16[256,1280]{1,0:T(8,128)(2,1)S(1)}, bf16[256,1280]{1,0:T(8,128)(2,1)S(1)}, u32[]{:S(2)}, u32[]{:S(2)}) collective-permute-start(bf16[256,1280]{1,0:T(8,128)(2,1)S(1)} %slice.115), channel_id=1, source_target_pairs={{0,1},{1,0},{2,3},{3,2},{4,5},{5,4},{6,7},{7,6},{8,9},{9,8},{10,11... | collective-permute-start | bytes 1966088 | tf_op jit(solution)/shard_map/ppermute | solution.py:22
  218.9 10.5 %all-to-all-start.7 = ((bf16[4,3,64,128]{3,2,1,0:T(8,128)(2,1)}), bf16[4,3,64,128]{3,2,1,0:T(8,128)(2,1)S(1)}, u32[]{:S(2)}, u32[]{:S(2)}) async-start(bf16[4,3,64,128]{3,2,1,0:T(8,128)(2,1)} %bitcast.95), calls=%async_computation.7 | async-start | bytes 393216 | tf_op jit(solution)/shard_map/all_to_all | solution.py:140
  224.2 0.9 copy-start.6

commit v5 on v4

--- a/solution.py
+++ b/solution.py
@@ -61,6 +61,45 @@
     )(*given)
 
 
+def join_kernel(*refs):
+    count = len(refs) // 3
+    for n in range(count):
+        mine_ref, theirs_ref, out_ref = refs[2 * n], refs[2 * n + 1], refs[2 * count + n]
+        rows, lanes = mine_ref.shape[1:]
+        out_ref[0, :rows, :lanes] = mine_ref[0]
+        out_ref[0, -rows:, -lanes:] = theirs_ref[0]
+
+
+def joined(sources, pieces):
+    given, in_specs, out_specs, shapes = [], [], [], []
+    moved = 0
+    for which, first, rounds, row, rows, axis in pieces:
+        lanes = sources[which].shape[2]
+
+        def block(i, first=first, rounds=rounds, row=row):
+            return (first + jnp.minimum(i, rounds - 1), row, 0)
+
+        def out_block(i, rounds=rounds):
+            return (jnp.minimum(i, rounds - 1), 0, 0)
+
+        shape = [rounds, rows, lanes]
+        shape[axis] *= 2
+        moved += 4 * shape[0] * shape[1] * shape[2]
+        given += sources[which : which + 2]
+        in_specs += [pl.BlockSpec((1, rows, lanes), block)] * 2
+        out_specs.append(pl.BlockSpec((1, shape[1], shape[2]), out_block))
+        shapes.append(jax.ShapeDtypeStruct(tuple(shape), BF16))
+    return pl.pallas_call(
+        join_kernel,
+        grid=(max(piece[2] for piece in pieces),),
+        in_specs=in_specs,
+        out_specs=out_specs,
+        out_shape=shapes,
+        compiler_params=pltpu.CompilerParams(vmem_limit_bytes=32 * 2**20),
+        cost_estimate=pl.CostEstimate(flops=0, bytes_accessed=moved, transcendentals=0),
+    )(*given)
+
+
 def inverse_times(current, inverse):
     return lax.dot_general(current, inverse, (((0, 2), (0, 2)), ((), ())), preferred_element_type=F32).astype(BF16)
 
@@ -88,7 +127,7 @@
     first = noise[:rounds].astype(BF16)
     current = lax.all_to_all(copies_of(first, n_z), "col", 0, 0, tiled=True, axis_index_groups=at.column_groups())
     current = current.transpose(1, 0, 2, 3).reshape(rounds, half, lanes)
-    done = [noise[:rounds]]
+    done = []
     later = {}
     outs = None
     solved = None
@@ -99,7 +138,7 @@
             products, factor, noise = tied(products, factor, noise)
             factor_theirs = at.swap(factor, partner)
         else:
-            products = inverse_times(current, inverse)
+            products = inverse_times(current, inverses[s])
         products, before = tied(products, solved) if s > 0 else (products, None)
         received = lax.all_to_all(products.reshape(n_row, half // n_row, 2 * width), "row", 0, 0, tiled=True)
         if s > 0:
@@ -113,17 +152,19 @@
             received, outs, *held = tied(received, outs, *[later[n] for n in range(s + 1, steps + 1)])
             later.update(zip(range(s + 1, steps + 1), held))
         solved = jnp.sum(received.astype(F32), axis=0).astype(BF16)
-        copies, factor, factor_theirs, dinv, dinv_theirs = tied(copies_of(solved, n_row), factor, factor_theirs, dinv, dinv_theirs)
+        copies = copies_of(solved, n_row)
+        if s == 0:
+            copies, factor, factor_theirs, dinv, dinv_theirs = tied(copies, factor, factor_theirs, dinv, dinv_theirs)
         solved = lax.all_to_all(copies, "row", 0, 0, tiled=True)
-        block = jnp.concatenate([f[lo - rounds : hi - rounds, s * lanes : (s + 1) * lanes] for f in (factor, factor_theirs)], axis=2)
-        if s + 1 < steps:
-            inverse = jnp.concatenate([d[(s + 1) * rounds : (s + 2) * rounds] for d in (dinv, dinv_theirs)], axis=1)
-            solved, block, inverse = tied(solved, block, inverse)
-        else:
-            solved, block = tied(solved, block)
+        if s == 0:
+            pieces = [(0, t * rounds, hi - lo, t, lanes, 2) for t, (lo, hi) in enumerate(bounds[1:])]
+            pieces += [(2, t * rounds, rounds, 0, width, 1) for t in range(1, steps)]
+            held = joined((factor, factor_theirs, dinv, dinv_theirs), pieces)
+            solved, *held = tied(solved, *held)
+            blocks, inverses = held[:steps], [None] + held[steps:]
         solved = solved.reshape(half, 2 * width)
 
-        update = factor_times(solved, block)
+        update = factor_times(solved, blocks[s])
         if s > 0:
             update = update + later[s + 1]
         if s + 1 < steps:
@@ -136,12 +177,12 @@
             current = work.astype(BF16)
         else:
             parts = update.astype(BF16).reshape(hi - lo, n_z, chunk, lanes).transpose(1, 0, 2, 3)
-            parts, last = tied(parts, solved)
+            parts, last, noise = tied(parts, solved, noise)
             got = lax.all_to_all(parts, "col", 0, 0, tiled=True, axis_index_groups=at.column_groups())
             outs = place(core, last, at.swap(last[:, width:], partner), outs, s, steps)
             got, outs = tied(got, outs)
             done.append(noise[lo:hi] - add_up(got))
-    return outs, jnp.concatenate(done, axis=0).transpose(1, 0, 2)
+    return outs, jnp.concatenate([noise[:rounds]] + done, axis=0).transpose(1, 0, 2)
 
 
 def solution(mesh):

time: 233 us -> 226 us (0.970)
  blocking collectives: 38.1 us -> 86.1 us
  waiting for transfers between devices: 66.7 us -> 33.1 us
  starting transfers between devices: 45.8 us -> 34.2 us
  local copies, waits for them, and re-layouts: 27.8 us -> 19.5 us
  Pallas kernels: 13 us -> 18.7 us
  other arithmetic: 9.24 us -> 5.3 us
  matrix products: 29.5 us -> 26.8 us
    all_to_all x0 -> x2, blocking collectives: none -> 48 us  [local(): solved = lax.all_to_all(copies, 'row', 0, 0, tiled=True)]
    all_to_all x3 -> x1, waiting for transfers between devices: 39.1 us -> 2.8 us  [local(): solved = lax.all_to_all(copies, 'row', 0, 0, tiled=True)]
    all_to_all x3 -> x1, starting transfers between devices: 15.8 us -> 4.4 us  [local(): solved = lax.all_to_all(copies, 'row', 0, 0, tiled=True)]
    slice x12 -> x1, local copies, waits for them, and re-layouts: 12 us -> 0.93 us  [local(): noise[:rounds]]
    unnamed x22 -> x36, local copies, waits for them, and re-layouts: 5.16 us -> 12.2 us
    pallas_call x0 -> x1, Pallas kernels: none -> 5.75 us  [joined(): pl.pallas_call(join_kernel, grid=(max((piece[2] for piece in pieces)),),...]
    concatenate x5 -> x0, other arithmetic: 4.5 us -> none  [the longest x3 4.08 us: local(): jnp.concatenate([f[lo - rounds:hi - rounds, s * lanes:(s + 1) * lanes] fo...]
    dot_general x9, matrix products: 22.1 us -> 19.3 us  [factor_times(): lax.dot_general(solved, block, (((1,), (2,)), ((), ())), preferred_elemen...]
  transfers between devices with their start and end apart: 15 -> 13, of which waited for: 8 -> 6; matrix products, arithmetic and copies ran while one was open for 18% -> 10% of each run, Pallas kernels for 6% -> 8%
where the time goes in v5:
time: 226 us; the launch traced here: 225 us
  blocking collectives  86.1 us (38%)
  starting transfers between devices  34.2 us (15%)
  waiting for transfers between devices  33.1 us (15%)
  matrix products  26.8 us (12%)
  local copies, waits for them, and re-layouts  19.5 us (9%)
  Pallas kernels  18.7 us (8%)
  other arithmetic  5.3 us (2%)
    all_to_all x2, blocking collectives, local(): solved = lax.all_to_all(copies, 'row', 0, 0, tiled=True)  48 us
    all_to_all x1, blocking collectives, local(): lax.all_to_all(products.reshape(n_row, half // n_row, 2 * width), 'row',...  26.2 us
    ppermute x9, waiting for transfers between devices, swap(): lax.ppermute(block, 'col', [(c, c ^ masks[c % 2]) for c in range(self.n_c...  24.6 us
    dot_general x9, matrix products, factor_times(): lax.dot_general(solved, block, (((1,), (2,)), ((), ())), preferred_elemen...  19.3 us
    ppermute x9, starting transfers between devices, swap(): lax.ppermute(block, 'col', [(c, c ^ masks[c % 2]) for c in range(self.n_c...  16.8 us
    pallas_call x3, Pallas kernels, place(): pl.pallas_call(place_kernel, grid=(width // tile,), in_specs=[pl.BlockSpe...  13 us
    unnamed x36, local copies, waits for them, and re-layouts  12.2 us
    all_to_all x1, blocking collectives, local(): lax.all_to_all(copies_of(first, n_z), 'col', 0, 0, tiled=True, axis_index...  11.8 us
  transfers between devices with their start and end apart: 13, of which 6 were waited for; matrix products, arithmetic and copies ran while one was open for 10% of the time, Pallas kernels for 8%

profile of v5, /device:TPU:1, one launch (start us, length us, event | category | flops | bytes accessed | tf_op | source)
XLA Modules:
  0.0 224.8 jit_solution(11752195853034681527)
XLA Ops:
  0.6 1.5 collective-permute-start
  2.1 0.9 slice.130
  3.1 11.8 %all_to_all.40 = bf16[4,5,64,128]{3,2,1,0:T(8,128)(2,1)S(1)} all-to-all(bf16[4,5,64,128]{3,2,1,0:T(8,128)(2,1)S(1)} %broadcast_in_dim.68), channel_id=1, replica_groups={{0,2,4,6},{1,3,5,7},{8,10,12,14},{9,11,13,15},{16,18,20,22},{17,19,21,2..., dimensions={0} | all-to-all | bytes 655360 | tf_op jit(solution)/shard_map/all_to_all | solution.py:128
  15.0 2.1 fusion.2
  17.2 2.2 copy-done.8
  19.3 0.7 fusion.3
  20.1 1.5 collective-permute-start.1
  21.6 26.2 %all_to_all.41 = bf16[16,16,2560]{2,1,0:T(8,128)(2,1)S(1)} all-to-all(bf16[16,16,2560]{2,1,0:T(8,128)(2,1)S(1)} %bitcast.119), channel_id=1, replica_groups=mesh['row'=16,'col'=8] {'row'}, dimensions={0} | all-to-all | bytes 2621440 | tf_op jit(solution)/shard_map/all_to_all | solution.py:143
  47.9 0.2 reduce_sum.45
  48.1 1.2 broadcast_in_dim.74
  49.3 4.4 %all-to-all-start.2 = ((bf16[16,16,2560]{2,1,0:T(8,128)(2,1)}), bf16[16,16,2560]{2,1,0:T(8,128)(2,1)}, u32[]{:S(2)}, u32[]{:S(2)}) async-start(bf16[16,16,2560]{2,1,0:T(8,128)(2,1)} %broadcast_in_dim.74), calls=%async_computation.2 | async-start | bytes 2621440 | tf_op jit(solution)/shard_map/all_to_all | solution.py:158
  53.9 1.0 bitcast_select_fusion
  54.9 2.4 %copy-done = bf16[3,1280,5,128]{3,1,2,0:T(8,128)(2,1)S(1)} copy-done((bf16[3,1280,5,128]{3,1,2,0:T(8,128)(2,1)S(1)}, bf16[3,1280,5,128]{3,1,2,0:T(8,128)(2,1)}, u32[]{:S(2)}) %copy-start) | copy-done | bytes 4915224
  57.3 5.8 %shard_map.50 = (bf16[5,128,2560]{2,1,0:T(8,128)(2,1)S(1)}, bf16[5,128,2560]{2,1,0:T(8,128)(2,1)S(1)}, bf16[3,128,2560]{2,1,0:T(8,128)(2,1)S(1)}, bf16[5,2560,12...) custom-call(bf16[13,384,1280]{2,1,0:T(8,128)(2,1)} %bitcast.103, ...), custom_call_target="tpu_custom_call" | custom-call | bytes 30146560 | tf_op jit(solution)/shard_map/pallas_call | solution.py:92
  63.0 1.7 copy-done.1
  64.7 1.7 copy-done.3
  66.4 1.7 copy-done.5
  68.1 1.3 copy-done.6
  69.4 2.8 %all-to-all-done.2 = bf16[16,16,2560]{2,1,0:T(8,128)(2,1)} async-done(((bf16[16,16,2560]{2,1,0:T(8,128)(2,1)}), bf16[16,16,2560]{2,1,0:T(8,128)(2,1)}, u32[]{:S(2)}, u32[]{:S(2)}) %all-to-all-start.2) | async-done | bytes 1310752 | tf_op jit(solution)/shard_map/all_to_all | solution.py:158
  72.2 3.7 %fusion.42 = (bf16[5,256,128]{2,1,0:T(8,128)(2,1)S(1)}, f32[5,256,128]{2,1,0:T(8,128)S(1)}) fusion(f32[5,256,128]{2,1,0:T(8,128)} %bitcast_select_fusion, bf16[256,2560,1]{1,0,2:T(8,128)(2,1)} %bitcast.15, bf16[5,128,2560]{2,1,0:T(8,128)(2,1)} %copy-done.5), kind=kOutput, calls=%fused_computation.65 | convolution fusion | flops 839188480 | bytes 6225920 | tf_op jit(solution)/shard_map/dot_general | solution.py:108
  75.9 1.0 collective-permute-start.2
  76.9 6.2 %collective-permute-done.2 = bf16[5,256,128]{2,1,0:T(8,128)(2,1)S(1)} collective-permute-done((bf16[5,256,128]{2,1,0:T(8,128)(2,1)S(1)}, bf16[5,256,128]{2,1,0:T(8,128)(2,1)S(1)}, u32[]{:S(2)}, u32[]{:S(2)}) %collective-permute-start.2) | collective-permute-done | bytes 327712 | tf_op jit(solution)/shard_map/ppermute | solution.py:22
  83.3 5.9 %collective-permute-done.3 = bf16[5,256,128]{2,1,0:T(8,128)(2,1)S(1)} collective-permute-done((bf16[5,256,128]{2,1,0:T(8,128)(2,1)S(1)}, bf16[5,256,128]{2,1,0:T(8,128)(2,1)S(1)}, u32[]{:S(2)}, u32[]{:S(2)}) %collective-permute-start.3) | collective-permute-done | bytes 327712 | tf_op jit(solution)/shard_map/ppermute | solution.py:22
  89.2 0.1 convert_add_fusion.2
  89.3 2.3 %fusion = bf16[256,2560]{1,0:T(8,128)(2,1)} fusion(bf16[5,2560,128]{2,1,0:T(8,128)(2,1)S(1)} %copy-done.2, f32[5,256,128]{2,1,0:T(8,128)S(1)} %convert_add_fusion.2), kind=kOutput, calls=%fused_computation.2 | convolution fusion | flops 839680000 | bytes 5242880 | tf_op jit(solution)/shard_map/dot_general | solution.py:104
  91.6 5.8 %all-to-all-start.3 = ((bf16[16,16,2560]{2,1,0:T(8,128)(2,1)}), bf16[16,16,2560]{2,1,0:T(8,128)(2,1)}, u32[]{:S(2)}, u32[]{:S(2)}) async-start(bf16[16,16,2560]{2,1,0:T(8,128)(2,1)} %bitcast.117), calls=%async_computation.3 | async-start | bytes 2621440 | tf_op jit(solution)/shard_map/all_to_all | solution.py:143
  97.4 1.1 slice.68
  98.6 4.2 %collective-permute-start.4 = (bf16[256,1280]{1,0:T(8,128)(2,1)S(1)}, bf16[256,1280]{1,0:T(8,128)(2,1)}, u32[]{:S(2)}, u32[]{:S(2)}) collective-permute-start(bf16[256,1280]{1,0:T(8,128)(2,1)S(1)} %slice.68), channel_id=1, source_target_pairs={{0,1},{1,0},{2,3},{3,2},{4,5},{5,4},{6,7},{7,6},{8,9},{9,8},{10,11... | collective-permute-start | bytes 1966088 | tf_op jit(solution)/shard_map/ppermute | solution.py:22
  102.8 1.9 fusion.19
  104.7 2.7 %fusion.16 = f32[3,256,128]{2,1,0:T(8,128)} fusion(f32[256,3,128]{2,0,1:T(8,128)S(1)} %fusion.19, bf16[13,384,1280]{2,1,0:T(8,128)(2,1)} %collective-permute-done.1.refs_1_.refs_3_.refs_5_, bf16[256,2560]{1,0:T(8,128)(2,1)} %bitcast.14.own_ref), kind=kOutput, calls=%fused_computation.24 | convolution fusion | flops 251756544 | bytes 2424832 | tf_op jit(solution)/shard_map/dot_general | solution.py:108
  107.4 2.3 %fusion.5 = f32[256,5,128]{2,0,1:T(8,128)S(1)} fusion(bf16[13,384,1280]{2,1,0:T(8,128)(2,1)} %bitcast.107, bf16[256,2560]{1,0:T(8,128)(2,1)} %bitcast.14.own_ref), kind=kOutput, calls=%fused_computation.10 | convolution fusion | flops 419430400 | bytes 2949120 | tf_op jit(solution)/shard_map/dot_general | solution.py:108
  109.7 3.2 %fusion.12 = f32[5,256,128]{2,1,0:T(8,128)} fusion(f32[256,5,128]{2,0,1:T(8,128)S(1)} %fusion.5, bf16[13,384,1280]{2,1,0:T(8,128)(2,1)} %collective-permute-done.1.refs_1_.refs_3_.refs_5_, bf16[256,2560]{1,0:T(8,128)(2,1)} %bitcast.14.own_ref), kind=kOutput, calls=%fused_computation.18 | convolution fusion | flops 419594240 | bytes 3604480 | tf_op jit(solution)/shard_map/dot_general | solution.py:108
  113.0 4.3 %shard_map.51.refs_0_ = bf16[3,1280,512]{2,1,0:T(8,128)(2,1)} custom-call(s32[1]{0:T(128)} %bitcast.19.core_ref, bf16[256,2560]{1,0:T(8,128)(2,1)} %bitcast.14.own_ref, bf16[256,1280]{1,0:T(8,128)(2,1)} %collective-permute-done.4.other_ref), custom_call_target="tpu_custom_call" | custom-call | bytes 2621440 | tf_op jit(solution)/shard_map/pallas_call | solution.py:53
  117.3 1.5 reduce_sum.46
  118.8 0.1 broadcast_in_dim.75
  118.9 26.6 %all_to_all.42 = bf16[16,16,2560]{2,1,0:T(8,128)(2,1)S(1)} all-to-all(bf16[16,16,2560]{2,1,0:T(8,128)(2,1)S(1)} %broadcast_in_dim.75), channel_id=1, replica_groups=mesh['row'=16,'col'=8] {'row'}, dimensions={0} | all-to-all | bytes 2621440 | tf_op jit(solution)/shard_map/all_to_all | solution.py:158
  145.5 1.2 convolution_bitcast_fusion.4
  146.7 0.3 copy-done.16
  147.1 0.2 fusion.39
  147.3 1.0 collective-permute-start.5
  148.3 6.2 %collective-permute-done.5 = bf16[5,256,128]{2,1,0:T(8,128)(2,1)S(1)} collective-permute-done((bf16[5,256,128]{2,1,0:T(8,128)(2,1)S(1)}, bf16[5,256,128]{2,1,0:T(8,128)(2,1)S(1)}, u32[]{:S(2)}, u32[]{:S(2)}) %collective-permute-start.5) | collective-permute-done | bytes 327712 | tf_op jit(solution)/shard_map/ppermute | solution.py:22
  154.7 6.2 %collective-permute-done.6 = bf16[5,256,128]{2,1,0:T(8,128)(2,1)S(1)} collective-permute-done((bf16[5,256,128]{2,1,0:T(8,128)(2,1)S(1)}, bf16[5,256,128]{2,1,0:T(8,128)(2,1)S(1)}, u32[]{:S(2)}, u32[]{:S(2)}) %collective-permute-start.6) | collective-permute-done | bytes 327712 | tf_op jit(solution)/shard_map/ppermute | solution.py:22
  160.9 0.1 convert_add_fusion
  161.0 2.3 %fusion.1 = bf16[256,2560]{1,0:T(8,128)(2,1)} fusion(bf16[5,2560,128]{2,1,0:T(8,128)(2,1)S(1)} %get-tuple-element.58, f32[5,256,128]{2,1,0:T(8,128)S(1)} %convert_add_fusion), kind=kOutput, calls=%fused_computation.3 | convolution fusion | flops 839680000 | bytes 5242880 | tf_op jit(solution)/shard_map/dot_general | solution.py:104
  163.3 3.8 %all-to-all-start.5 = ((bf16[16,16,2560]{2,1,0:T(8,128)(2,1)}), bf16[16,16,2560]{2,1,0:T(8,128)(2,1)S(1)}, u32[]{:S(2)}, u32[]{:S(2)}) async-start(bf16[16,16,2560]{2,1,0:T(8,128)(2,1)} %bitcast.118), calls=%async_computation.5 | async-start | bytes 2621440 | tf_op jit(solution)/shard_map/all_to_all | solution.py:143
  167.2 3.5 %collective-permute-start.7 = (bf16[256,1280]{1,0:T(8,128)(2,1)S(1)}, bf16[256,1280]{1,0:T(8,128)(2,1)}, u32[]{:S(2)}, u32[]{:S(2)}) collective-permute-start(bf16[256,1280]{1,0:T(8,128)(2,1)S(1)} %slice.74), channel_id=1, source_target_pairs={{0,1},{1,0},{2,3},{3,2},{4,5},{5,4},{6,7},{7,6},{8,9},{9,8},{10,11... | collective-permute-start | bytes 1966088 | tf_op jit(solution)/shard_map/ppermute | solution.py:22
  170.7 1.7 convolution_bitcast_fusion.8
  172.5 1.7 add_add_fusion
  174.2 4.3 %shard_map.52.refs_0_ = bf16[3,1280,512]{2,1,0:T(8,128)(2,1)} custom-call(s32[1]{0:T(128)} %bitcast.19.core_ref, bf16[256,2560]{1,0:T(8,128)(2,1)} %bitcast.110, bf16[256,1280]{1,0:T(8,128)(2,1)} %collective-permute-done.7.other_ref, bf16[3,1280,512]{2,1,0:T(8,128)(2,1)} %shard_map.51.refs_0_), custom_call_target="tpu_custom_call", output_to_operand_aliasing={{}: (3, {})} | custom-call | bytes 2621440 | tf_op jit(solution)/shard_map/pallas_call | solution.py:53
  178.6 5.7 %all-to-all-done.5 = bf16[16,16,2560]{2,1,0:T(8,128)(2,1)S(1)} async-done(((bf16[16,16,2560]{2,1,0:T(8,128)(2,1)}), bf16[16,16,2560]{2,1,0:T(8,128)(2,1)S(1)}, u32[]{:S(2)}, u32[]{:S(2)}) %all-to-all-start.5) | async-done | bytes 1310752 | tf_op jit(solution)/shard_map/all_to_all | solution.py:143
  184.2 0.2 reduce_sum.47
  184.4 0.1 broadcast_in_dim.76
  184.5 21.4 %all_to_all.43 = bf16[16,16,2560]{2,1,0:T(8,128)(2,1)S(1)} all-to-all(bf16[16,16,2560]{2,1,0:T(8,128)(2,1)S(1)} %broadcast_in_dim.76), channel_id=1, replica_groups=mesh['row'=16,'col'=8] {'row'}, dimensions={0} | all-to-all | bytes 2621440 | tf_op jit(solution)/shard_map/all_to_all | solution.py:158
  205.9 0.9 convolution_bitcast_fusion.6
  206.9 0.7 copy.10
  207.6 4.0 %collective-permute-start.8 = (bf16[256,1280]{1,0:T(8,128)(2,1)S(1)}, bf16[256,1280]{1,0:T(8,128)(2,1)S(1)}, u32[]{:S(2)}, u32[]{:S(2)}) collective-permute-start(bf16[256,1280]{1,0:T(8,128)(2,1)S(1)} %slice.78), channel_id=1, source_target_pairs={{0,1},{1,0},{2,3},{3,2},{4,5},{5,4},{6,7},{7,6},{8,9},{9,8},{10,11... | collective-permute-start | bytes 1966088 | tf_op jit(solution)/shard_map/ppermute | solution.py:22
  211.6 3.4 %all-to-all-start.7 = ((bf16[4,3,64,128]{3,2,1,0:T(8,128)(2,1)}), bf16[4,3,64,128]{3,2,1,0:T(8,128)(2,1)S(1)}, u32[]{:S(2)}, u32[]{:S(2)}) async-start(bf16[4,3,64,128]{3,2,1,0:T(8,128)(2,1)} %bitcast.97), calls=%async_computation.7 | async-start | bytes 393216 | tf_op jit(solution)/shard_map/all_to_all | solution.py:181
  215.0 0.9 constant_dynamic-slice_fusion.1
  215.9 0.9 constant_dynamic-slice_fusion
  216.8 0.9 slice.79
  217.8 0.9 copy-done.15
  218.7 4.3 %shard_map.53 = bf16[3,1280,512]{2,1,0:T(8,128)(2,1)} custom-call(s32[1]{0:T(128)} %bitcast.19.core_ref, bf16[256,2560]{1,0:T(8,128)(2,1)} %bitcast.116, bf16[256,1280]{1,0:T(8,128)(2,1)} %copy-done.15, bf16[3,1280,512]{2,1,0:T(8,128)(2,1)} %shard_map.52.refs_0_), custom_call_target="tpu_custom_call", output_to_operand_aliasing={{}: (3, {})} | custom-call | bytes 2621440 | tf_op jit(solution)/shard_map/pallas_call | solution.py:53
  223.0 0.9 slice_subtract_fusion
  223.9 0.9 maximum_bitcast_fusion
  (50 shorter events, 0.9 us)
Async XLA Ops:
  0.6 16.5 %collective-permute-start = (bf16[15,1280,128]{2,1,0:T(8,128)(2,1)}, bf16[15,1280,128]{2,1,0:T(8,128)(2,1)S(1)}, u32[]{:S(2)}, u32[]{:S(2)}) collective-permute-start(bf16[15,1280,128]{2,1,0:T(8,128)(2,1)} %bitcast.98), channel_id=1, source_target_pairs={{0,1},{1,0},{2,3},{3,2},{4,5},{5,4},{6,7},{7,6},{8,9},{9,8},{10,11... | collective-permute-start | bytes 14745608 | tf_op jit(solution)/shard_map/ppermute | solution.py:22
  17.1 2.2 copy-start.8
  20.1 27.9 %collective-permute-start.1 = (bf16[13,384,1280]{2,1,0:T(8,128)(2,1)}, bf16[13,384,1280]{2,1,0:T(8,128)(2,1)}, u32[]{:S(2)}, u32[]{:S(2)}) collective-permute-start(bf16[13,384,1280]{2,1,0:T(8,128)(2,1)} %bitcast.102), channel_id=1, source_target_pairs={{0,1},{1,0},{2,3},{3,2},{4,5},{5,4},{6,7},{7,6},{8,9},{9,8},{10,11... | collective-permute-start | bytes 38338568 | tf_op jit(solution)/shard_map/ppermute | solution.py:22
  48.1 5.8 %copy-start.14 = (f32[64,18,128]{2,0,1:T(8,128)S(1)}, f32[64,18,128]{2,0,1:T(8,128)}, u32[]{:S(2)}) copy-start(f32[64,18,128]{2,0,1:T(8,128)} %param.3) | copy-start | bytes 1769476
  49.3 22.9 %all-to-all-start.2 = ((bf16[16,16,2560]{2,1,0:T(8,128)(2,1)}), bf16[16,16,2560]{2,1,0:T(8,128)(2,1)}, u32[]{:S(2)}, u32[]{:S(2)}) async-start(bf16[16,16,2560]{2,1,0:T(8,128)(2,1)} %broadcast_in_dim.74), calls=%async_computation.2 | async-start | bytes 2621440 | tf_op jit(solution)/shard_map/all_to_all | solution.py:158
  54.9 2.4 %copy-start = (bf16[3,1280,5,128]{3,1,2,0:T(8,128)(2,1)S(1)}, bf16[3,1280,5,128]{3,1,2,0:T(8,128)(2,1)}, u32[]{:S(2)}) copy-start(bf16[3,1280,5,128]{3,1,2,0:T(8,128)(2,1)} %param.5) | copy-start | bytes 14745604
  63.0 1.7 copy-start.1
  64.7 1.7 copy-start.3
  66.4 1.7 copy-start.5
  68.1 1.3 copy-start.6
  75.9 13.4 %copy-start.2 = (bf16[5,2560,128]{2,1,0:T(8,128)(2,1)S(1)}, bf16[5,2560,128]{2,1,0:T(8,128)(2,1)}, u32[]{:S(2)}) copy-start(bf16[5,2560,128]{2,1,0:T(8,128)(2,1)} %copy-done.1) | copy-start | bytes 9830404
  75.9 7.2 %collective-permute-start.2 = (bf16[5,256,128]{2,1,0:T(8,128)(2,1)S(1)}, bf16[5,256,128]{2,1,0:T(8,128)(2,1)S(1)}, u32[]{:S(2)}, u32[]{:S(2)}) collective-permute-start(bf16[5,256,128]{2,1,0:T(8,128)(2,1)S(1)} %get-tuple-element.76), channel_id=1, source_target_pairs={{0,2},{1,7},{2,0},{3,5},{4,6},{5,3},{6,4},{7,1},{8,10},{9,15},{10,... | collective-permute-start | bytes 983048 | tf_op jit(solution)/shard_map/ppermute | solution.py:22
  83.2 6.0 %collective-permute-start.3 = (bf16[5,256,128]{2,1,0:T(8,128)(2,1)S(1)}, bf16[5,256,128]{2,1,0:T(8,128)(2,1)S(1)}, u32[]{:S(2)}, u32[]{:S(2)}) collective-permute-start(bf16[5,256,128]{2,1,0:T(8,128)(2,1)S(1)} %fusion.32), channel_id=1, source_target_pairs={{0,6},{1,3},{2,4},{3,1},{4,2},{5,7},{6,0},{7,5},{8,14},{9,11},{10,... | collective-permute-start | bytes 983048 | tf_op jit(solution)/shard_map/ppermute | solution.py:22
  89.3 2.3 %copy-start.12 = (f32[5,256,128]{2,1,0:T(8,128)}, f32[5,256,128]{2,1,0:T(8,128)S(1)}, u32[]{:S(2)}) copy-start(f32[5,256,128]{2,1,0:T(8,128)S(1)} %convert_add_fusion.2) | copy-start | bytes 1966084
  91.6 25.6 %all-to-all-start.3 = ((bf16[16,16,2560]{2,1,0:T(8,128)(2,1)}), bf16[16,16,2560]{2,1,0:T(8,128)(2,1)}, u32[]{:S(2)}, u32[]{:S(2)}) async-start(bf16[16,16,2560]{2,1,0:T(8,128)(2,1)} %bitcast.117), calls=%async_computation.3 | async-start | bytes 2621440 | tf_op jit(solution)/shard_map/all_to_all | solution.py:143
  98.6 14.4 %collective-permute-start.4 = (bf16[256,1280]{1,0:T(8,128)(2,1)S(1)}, bf16[256,1280]{1,0:T(8,128)(2,1)}, u32[]{:S(2)}, u32[]{:S(2)}) collective-permute-start(bf16[256,1280]{1,0:T(8,128)(2,1)S(1)} %slice.68), channel_id=1, source_target_pairs={{0,1},{1,0},{2,3},{3,2},{4,5},{5,4},{6,7},{7,6},{8,9},{9,8},{10,11... | collective-permute-start | bytes 1966088 | tf_op jit(solution)/shard_map/ppermute | solution.py:22
  118.8 26.7 %copy-start.4 = (bf16[5,128,2560]{2,1,0:T(8,128)(2,1)S(1)}, bf16[5,128,2560]{2,1,0:T(8,128)(2,1)}, u32[]{:S(2)}) copy-start(bf16[5,128,2560]{2,1,0:T(8,128)(2,1)} %copy-done.3) | copy-start | bytes 9830404
  145.5 1.2 copy-start.9
  145.5 1.6 copy-start.16
  147.3 7.2 %collective-permute-start.5 = (bf16[5,256,128]{2,1,0:T(8,128)(2,1)S(1)}, bf16[5,256,128]{2,1,0:T(8,128)(2,1)S(1)}, u32[]{:S(2)}, u32[]{:S(2)}) collective-permute-start(bf16[5,256,128]{2,1,0:T(8,128)(2,1)S(1)} %get-tuple-element.72), channel_id=1, source_target_pairs={{0,2},{1,7},{2,0},{3,5},{4,6},{5,3},{6,4},{7,1},{8,10},{9,15},{10,... | collective-permute-start | bytes 983048 | tf_op jit(solution)/shard_map/ppermute | solution.py:22
  154.6 6.3 %collective-permute-start.6 = (bf16[5,256,128]{2,1,0:T(8,128)(2,1)S(1)}, bf16[5,256,128]{2,1,0:T(8,128)(2,1)S(1)}, u32[]{:S(2)}, u32[]{:S(2)}) collective-permute-start(bf16[5,256,128]{2,1,0:T(8,128)(2,1)S(1)} %fusion.33), channel_id=1, source_target_pairs={{0,6},{1,3},{2,4},{3,1},{4,2},{5,7},{6,0},{7,5},{8,14},{9,11},{10,... | collective-permute-start | bytes 983048 | tf_op jit(solution)/shard_map/ppermute | solution.py:22
  161.0 2.3 %copy-start.13 = (f32[5,256,128]{2,1,0:T(8,128)}, f32[5,256,128]{2,1,0:T(8,128)S(1)}, u32[]{:S(2)}) copy-start(f32[5,256,128]{2,1,0:T(8,128)S(1)} %convert_add_fusion) | copy-start | bytes 1966084
  163.3 3.8 %copy-start.10 = (bf16[16,16,2560]{2,1,0:T(8,128)(2,1)S(1)}, bf16[16,16,2560]{2,1,0:T(8,128)(2,1)}, u32[]{:S(2)}) copy-start(bf16[16,16,2560]{2,1,0:T(8,128)(2,1)} %copy-done.9) | copy-start | bytes 3932164
  163.3 20.9 %all-to-all-start.5 = ((bf16[16,16,2560]{2,1,0:T(8,128)(2,1)}), bf16[16,16,2560]{2,1,0:T(8,128)(2,1)S(1)}, u32[]{:S(2)}, u32[]{:S(2)}) async-start(bf16[16,16,2560]{2,1,0:T(8,128)(2,1)} %bitcast.118), calls=%async_computation.5 | async-start | bytes 2621440 | tf_op jit(solution)/shard_map/all_to_all | solution.py:143
  167.2 5.3 %copy-start.17 = (f32[3,256,128]{2,1,0:T(8,128)S(1)}, f32[3,256,128]{2,1,0:T(8,128)}, u32[]{:S(2)}) copy-start(f32[3,256,128]{2,1,0:T(8,128)} %fusion.16) | copy-start | bytes 1179652
  167.2 7.0 %collective-permute-start.7 = (bf16[256,1280]{1,0:T(8,128)(2,1)S(1)}, bf16[256,1280]{1,0:T(8,128)(2,1)}, u32[]{:S(2)}, u32[]{:S(2)}) collective-permute-start(bf16[256,1280]{1,0:T(8,128)(2,1)S(1)} %slice.74), channel_id=1, source_target_pairs={{0,1},{1,0},{2,3},{3,2},{4,5},{5,4},{6,7},{7,6},{8,9},{9,8},{10,11... | collective-permute-start | bytes 1966088 | tf_op jit(solution)/shard_map/ppermute | solution.py:22
  184.4 21.5 %copy-start.7 = (bf16[3,128,2560]{2,1,0:T(8,128)(2,1)S(1)}, bf16[3,128,2560]{2,1,0:T(8,128)(2,1)}, u32[]{:S(2)}) copy-start(bf16[3,128,2560]{2,1,0:T(8,128)(2,1)} %copy-done.6) | copy-start | bytes 5898244
  205.9 1.6 copy-start.11
  207.6 10.2 %collective-permute-start.8 = (bf16[256,1280]{1,0:T(8,128)(2,1)S(1)}, bf16[256,1280]{1,0:T(8,128)(2,1)S(1)}, u32[]{:S(2)}, u32[]{:S(2)}) collective-permute-start(bf16[256,1280]{1,0:T(8,128)(2,1)S(1)} %slice.78), channel_id=1, source_target_pairs={{0,1},{1,0},{2,3},{3,2},{4,5},{5,4},{6,7},{7,6},{8,9},{9,8},{10,11... | collective-permute-start | bytes 1966088 | tf_op jit(solution)/shard_map/ppermute | solution.py:22
  211.6 11.4 %all-to-all-start.7 = ((bf16[4,3,64,128]{3,2,1,0:T(8,128)(2,1)}), bf16[4,3,64,128]{3,2,1,0:T(8,128)(2,1)S(1)}, u32[]{:S(2)}, u32[]{:S(2)}) async-start(bf16[4,3,64,128]{3,2,1,0:T(8,128)(2,1)} %bitcast.97), calls=%async_computation.7 | async-start | bytes 393216 | tf_op jit(solution)/shard_map/all_to_all | solution.py:181
  217.8 0.9 copy-start.15

commit v6 on v5

--- a/solution.py
+++ b/solution.py
@@ -18,16 +18,15 @@
     def column_groups(self):
         return [[2 * z + k for z in range(self.n_z)] for k in range(2)]
 
+    def shift(self, block, hops):
+        return lax.ppermute(block, "col", [(c, (c + 2 * hops) % self.n_col) for c in range(self.n_col)])
+
     def swap(self, block, masks):
         return lax.ppermute(block, "col", [(c, c ^ masks[c % 2]) for c in range(self.n_col)])
 
 
 def tied(first, *others):
     return lax.optimization_barrier((first,) + others)
-
-
-def add_up(parts):
-    return jnp.sum(parts.astype(F32), axis=0)
 
 
 def copies_of(block, count):
@@ -46,14 +45,16 @@
 
 
 def place(core, both, crossed, outs, step, steps):
-    half, width = crossed.shape
+    half, width = both.shape[0], both.shape[1] // 2
+    ahead = 5 * (crossed.shape[1] // width - 1)
     tile = width // 5
     block = pl.BlockSpec((half, tile), lambda i: (0, i))
+    crossing = pl.BlockSpec((half, tile), lambda i: (0, ahead + i))
     given = [core, both, crossed] + ([] if outs is None else [outs])
     return pl.pallas_call(
         place_kernel,
         grid=(width // tile,),
-        in_specs=[pl.BlockSpec(memory_space=pltpu.SMEM), block, block] + [pl.BlockSpec(memory_space=pl.ANY)] * (len(given) - 3),
+        in_specs=[pl.BlockSpec(memory_space=pltpu.SMEM), block, crossing] + [pl.BlockSpec(memory_space=pl.ANY)] * (len(given) - 3),
         out_specs=pl.BlockSpec((1, tile, 2 * half), lambda i: (step, i, 0)),
         out_shape=jax.ShapeDtypeStruct((steps, width, 2 * half), BF16),
         input_output_aliases={} if outs is None else {3: 0},
@@ -151,6 +152,10 @@
             outs = place(core, before, at.swap(before[:, width:], partner), outs, s - 1, steps)
             received, outs, *held = tied(received, outs, *[later[n] for n in range(s + 1, steps + 1)])
             later.update(zip(range(s + 1, steps + 1), held))
+            if s + 1 == steps:
+                starts = [((my_z + hops) % n_z * chunk).astype(jnp.uint32) for hops in range(n_z)]
+                received, *held = tied(received, noise[:rounds], *done, *starts)
+                done, starts = held[:steps], held[steps:]
         solved = jnp.sum(received.astype(F32), axis=0).astype(BF16)
         copies = copies_of(solved, n_row)
         if s == 0:
@@ -176,13 +181,17 @@
             done.append(lax.dynamic_slice_in_dim(work, my_z * chunk, chunk, axis=1))
             current = work.astype(BF16)
         else:
-            parts = update.astype(BF16).reshape(hi - lo, n_z, chunk, lanes).transpose(1, 0, 2, 3)
-            parts, last, noise = tied(parts, solved, noise)
-            got = lax.all_to_all(parts, "col", 0, 0, tiled=True, axis_index_groups=at.column_groups())
-            outs = place(core, last, at.swap(last[:, width:], partner), outs, s, steps)
-            got, outs = tied(got, outs)
-            done.append(noise[lo:hi] - add_up(got))
-    return outs, jnp.concatenate([noise[:rounds]] + done, axis=0).transpose(1, 0, 2)
+            pieces = [lax.dynamic_slice_in_dim(update, start, chunk, axis=1) for start in starts]
+            sent = [piece.astype(BF16) for piece in pieces[1:]]
+            last, noise, *sent = tied(solved, noise, *sent)
+            got = [at.shift(piece, hops + 1) for hops, piece in enumerate(sent)]
+            outs = place(core, last, at.swap(last, partner), outs, s, steps)
+            outs, *got = tied(outs, *got)
+            reduced = pieces[0]
+            for part in got:
+                reduced = reduced + part.astype(F32)
+            done.append(noise[lo:hi] - reduced)
+    return outs, jnp.concatenate(done, axis=0).transpose(1, 0, 2)
 
 
 def solution(mesh):

time: 226 us -> 224 us (level)
  waiting for transfers between devices: 33.1 us -> 29.1 us
    ppermute x0 -> x3, starting transfers between devices: none -> 3.58 us  [shift(): lax.ppermute(block, 'col', [(c, (c + 2 * hops) % self.n_col) for c in ran...]
    all_to_all x1 -> x0, starting transfers between devices: 3.37 us -> none  [local(): lax.all_to_all(parts, 'col', 0, 0, tiled=True, axis_index_groups=at.colum...]
    all_to_all x2, waiting for transfers between devices: 5.65 us -> 2.41 us  [local(): lax.all_to_all(products.reshape(n_row, half // n_row, 2 * width), 'row',...]
    unnamed x36 -> x40, local copies, waits for them, and re-layouts: 12.2 us -> 12.5 us
  transfers between devices with their start and end apart: 13 -> 15, of which waited for: 6 -> 6; matrix products, arithmetic and copies ran while one was open for 10% -> 10% of each run, Pallas kernels for 8% -> 8%
where the time goes in v6:
time: 224 us; the launch traced here: 223 us
  blocking collectives  86 us (38%)
  starting transfers between devices  34.5 us (15%)
  waiting for transfers between devices  29.1 us (13%)
  matrix products  26.8 us (12%)
  local copies, waits for them, and re-layouts  20.3 us (9%)
  Pallas kernels  18.8 us (8%)
  other arithmetic  6.26 us (3%)
    all_to_all x2, blocking collectives, local(): solved = lax.all_to_all(copies, 'row', 0, 0, tiled=True)  48 us
    all_to_all x1, blocking collectives, local(): lax.all_to_all(products.reshape(n_row, half // n_row, 2 * width), 'row',...  26.3 us
    ppermute x9, waiting for transfers between devices, swap(): lax.ppermute(block, 'col', [(c, c ^ masks[c % 2]) for c in range(self.n_c...  24.6 us
    dot_general x9, matrix products, factor_times(): lax.dot_general(solved, block, (((1,), (2,)), ((), ())), preferred_elemen...  19.3 us
    ppermute x9, starting transfers between devices, swap(): lax.ppermute(block, 'col', [(c, c ^ masks[c % 2]) for c in range(self.n_c...  16.8 us
    pallas_call x3, Pallas kernels, place(): pl.pallas_call(place_kernel, grid=(width // tile,), in_specs=[pl.BlockSpe...  13 us
    unnamed x40, local copies, waits for them, and re-layouts  12.5 us
    all_to_all x1, blocking collectives, local(): lax.all_to_all(copies_of(first, n_z), 'col', 0, 0, tiled=True, axis_index...  11.8 us
  transfers between devices with their start and end apart: 15, of which 6 were waited for; matrix products, arithmetic and copies ran while one was open for 10% of the time, Pallas kernels for 8%

profile of v6, /device:TPU:1, one launch (start us, length us, event | category | flops | bytes accessed | tf_op | source)
XLA Modules:
  0.0 222.8 jit_solution(3959624468156369636)
XLA Ops:
  0.6 1.5 collective-permute-start
  2.1 0.9 slice.126
  3.1 11.8 %all_to_all.35 = bf16[4,5,64,128]{3,2,1,0:T(8,128)(2,1)S(1)} all-to-all(bf16[4,5,64,128]{3,2,1,0:T(8,128)(2,1)S(1)} %broadcast_in_dim.68), channel_id=1, replica_groups={{0,2,4,6},{1,3,5,7},{8,10,12,14},{9,11,13,15},{16,18,20,22},{17,19,21,2..., dimensions={0} | all-to-all | bytes 655360 | tf_op jit(solution)/shard_map/all_to_all | solution.py:129
  15.0 2.1 fusion.2
  17.2 2.2 copy-done.8
  19.3 0.7 fusion.3
  20.1 1.5 collective-permute-start.1
  21.6 26.3 %all_to_all.36 = bf16[16,16,2560]{2,1,0:T(8,128)(2,1)S(1)} all-to-all(bf16[16,16,2560]{2,1,0:T(8,128)(2,1)S(1)} %bitcast.112), channel_id=1, replica_groups=mesh['row'=16,'col'=8] {'row'}, dimensions={0} | all-to-all | bytes 2621440 | tf_op jit(solution)/shard_map/all_to_all | solution.py:144
  47.9 0.2 reduce_sum.36
  48.1 1.2 broadcast_in_dim.74
  49.3 4.5 %all-to-all-start.2 = ((bf16[16,16,2560]{2,1,0:T(8,128)(2,1)}), bf16[16,16,2560]{2,1,0:T(8,128)(2,1)}, u32[]{:S(2)}, u32[]{:S(2)}) async-start(bf16[16,16,2560]{2,1,0:T(8,128)(2,1)} %broadcast_in_dim.74), calls=%async_computation.2 | async-start | bytes 2621440 | tf_op jit(solution)/shard_map/all_to_all | solution.py:163
  54.0 0.7 fusion.41
  54.7 1.0 bitcast_select_fusion
  55.7 2.4 %copy-done = bf16[3,1280,5,128]{3,1,2,0:T(8,128)(2,1)S(1)} copy-done((bf16[3,1280,5,128]{3,1,2,0:T(8,128)(2,1)S(1)}, bf16[3,1280,5,128]{3,1,2,0:T(8,128)(2,1)}, u32[]{:S(2)}) %copy-start) | copy-done | bytes 4915224
  58.1 5.8 %shard_map.50 = (bf16[5,128,2560]{2,1,0:T(8,128)(2,1)S(1)}, bf16[5,128,2560]{2,1,0:T(8,128)(2,1)S(1)}, bf16[3,128,2560]{2,1,0:T(8,128)(2,1)S(1)}, bf16[5,2560,12...) custom-call(bf16[13,384,1280]{2,1,0:T(8,128)(2,1)} %bitcast.99, ...), custom_call_target="tpu_custom_call" | custom-call | bytes 30146560 | tf_op jit(solution)/shard_map/pallas_call | solution.py:93
  63.9 1.7 copy-done.1
  65.6 1.7 copy-done.3
  67.2 1.7 copy-done.5
  68.9 1.3 copy-done.6
  70.2 2.1 all-to-all-done.2
  72.3 3.7 %fusion.42 = (bf16[5,256,128]{2,1,0:T(8,128)(2,1)S(1)}, f32[5,256,128]{2,1,0:T(8,128)S(1)}) fusion(f32[5,256,128]{2,1,0:T(8,128)} %bitcast_select_fusion, bf16[256,2560,1]{1,0,2:T(8,128)(2,1)} %bitcast.16, bf16[5,128,2560]{2,1,0:T(8,128)(2,1)} %copy-done.5), kind=kOutput, calls=%fused_computation.65 | convolution fusion | flops 839188480 | bytes 6225920 | tf_op jit(solution)/shard_map/dot_general | solution.py:109
  76.0 1.0 collective-permute-start.2
  77.0 6.2 %collective-permute-done.2 = bf16[5,256,128]{2,1,0:T(8,128)(2,1)S(1)} collective-permute-done((bf16[5,256,128]{2,1,0:T(8,128)(2,1)S(1)}, bf16[5,256,128]{2,1,0:T(8,128)(2,1)S(1)}, u32[]{:S(2)}, u32[]{:S(2)}) %collective-permute-start.2) | collective-permute-done | bytes 327712 | tf_op jit(solution)/shard_map/ppermute | solution.py:25
  83.4 5.9 %collective-permute-done.3 = bf16[5,256,128]{2,1,0:T(8,128)(2,1)S(1)} collective-permute-done((bf16[5,256,128]{2,1,0:T(8,128)(2,1)S(1)}, bf16[5,256,128]{2,1,0:T(8,128)(2,1)S(1)}, u32[]{:S(2)}, u32[]{:S(2)}) %collective-permute-start.3) | collective-permute-done | bytes 327712 | tf_op jit(solution)/shard_map/ppermute | solution.py:25
  89.3 0.1 convert_add_fusion.2
  89.4 2.3 %fusion = bf16[256,2560]{1,0:T(8,128)(2,1)} fusion(bf16[5,2560,128]{2,1,0:T(8,128)(2,1)S(1)} %copy-done.2, f32[5,256,128]{2,1,0:T(8,128)S(1)} %convert_add_fusion.2), kind=kOutput, calls=%fused_computation.2 | convolution fusion | flops 839680000 | bytes 5242880 | tf_op jit(solution)/shard_map/dot_general | solution.py:105
  91.7 5.8 %all-to-all-start.3 = ((bf16[16,16,2560]{2,1,0:T(8,128)(2,1)}), bf16[16,16,2560]{2,1,0:T(8,128)(2,1)}, u32[]{:S(2)}, u32[]{:S(2)}) async-start(bf16[16,16,2560]{2,1,0:T(8,128)(2,1)} %bitcast.111), calls=%async_computation.3 | async-start | bytes 2621440 | tf_op jit(solution)/shard_map/all_to_all | solution.py:144
  97.5 1.1 slice.65
  98.7 4.2 %collective-permute-start.4 = (bf16[256,1280]{1,0:T(8,128)(2,1)S(1)}, bf16[256,1280]{1,0:T(8,128)(2,1)}, u32[]{:S(2)}, u32[]{:S(2)}) collective-permute-start(bf16[256,1280]{1,0:T(8,128)(2,1)S(1)} %slice.65), channel_id=1, source_target_pairs={{0,1},{1,0},{2,3},{3,2},{4,5},{5,4},{6,7},{7,6},{8,9},{9,8},{10,11... | collective-permute-start | bytes 1966088 | tf_op jit(solution)/shard_map/ppermute | solution.py:25
  102.9 1.9 fusion.19
  104.8 2.7 %fusion.16 = f32[3,256,128]{2,1,0:T(8,128)} fusion(f32[256,3,128]{2,0,1:T(8,128)S(1)} %fusion.19, bf16[13,384,1280]{2,1,0:T(8,128)(2,1)} %collective-permute-done.1.refs_1_.refs_3_.refs_5_, bf16[256,2560]{1,0:T(8,128)(2,1)} %bitcast.15.own_ref), kind=kOutput, calls=%fused_computation.24 | convolution fusion | flops 251756544 | bytes 2424832 | tf_op jit(solution)/shard_map/dot_general | solution.py:109
  107.5 2.3 %fusion.5 = f32[256,5,128]{2,0,1:T(8,128)S(1)} fusion(bf16[13,384,1280]{2,1,0:T(8,128)(2,1)} %bitcast.103, bf16[256,2560]{1,0:T(8,128)(2,1)} %bitcast.15.own_ref), kind=kOutput, calls=%fused_computation.10 | convolution fusion | flops 419430400 | bytes 2949120 | tf_op jit(solution)/shard_map/dot_general | solution.py:109
  109.8 3.2 %fusion.12 = f32[5,256,128]{2,1,0:T(8,128)} fusion(f32[256,5,128]{2,0,1:T(8,128)S(1)} %fusion.5, bf16[13,384,1280]{2,1,0:T(8,128)(2,1)} %collective-permute-done.1.refs_1_.refs_3_.refs_5_, bf16[256,2560]{1,0:T(8,128)(2,1)} %bitcast.15.own_ref), kind=kOutput, calls=%fused_computation.18 | convolution fusion | flops 419594240 | bytes 3604480 | tf_op jit(solution)/shard_map/dot_general | solution.py:109
  113.0 4.3 %shard_map.51.refs_0_ = bf16[3,1280,512]{2,1,0:T(8,128)(2,1)} custom-call(s32[1]{0:T(128)} %bitcast.core_ref, bf16[256,2560]{1,0:T(8,128)(2,1)} %bitcast.15.own_ref, bf16[256,1280]{1,0:T(8,128)(2,1)} %collective-permute-done.4.other_ref), custom_call_target="tpu_custom_call" | custom-call | bytes 2621440 | tf_op jit(solution)/shard_map/pallas_call | solution.py:54
  117.4 1.5 reduce_sum.37
  118.9 0.1 broadcast_in_dim.75
  119.0 26.6 %all_to_all.37 = bf16[16,16,2560]{2,1,0:T(8,128)(2,1)S(1)} all-to-all(bf16[16,16,2560]{2,1,0:T(8,128)(2,1)S(1)} %broadcast_in_dim.75), channel_id=1, replica_groups=mesh['row'=16,'col'=8] {'row'}, dimensions={0} | all-to-all | bytes 2621440 | tf_op jit(solution)/shard_map/all_to_all | solution.py:163
  145.6 1.2 convolution_bitcast_fusion.4
  146.8 0.3 copy-done.18
  147.2 0.2 fusion.39
  147.4 1.0 collective-permute-start.5
  148.4 6.2 %collective-permute-done.5 = bf16[5,256,128]{2,1,0:T(8,128)(2,1)S(1)} collective-permute-done((bf16[5,256,128]{2,1,0:T(8,128)(2,1)S(1)}, bf16[5,256,128]{2,1,0:T(8,128)(2,1)S(1)}, u32[]{:S(2)}, u32[]{:S(2)}) %collective-permute-start.5) | collective-permute-done | bytes 327712 | tf_op jit(solution)/shard_map/ppermute | solution.py:25
  154.8 6.2 %collective-permute-done.6 = bf16[5,256,128]{2,1,0:T(8,128)(2,1)S(1)} collective-permute-done((bf16[5,256,128]{2,1,0:T(8,128)(2,1)S(1)}, bf16[5,256,128]{2,1,0:T(8,128)(2,1)S(1)}, u32[]{:S(2)}, u32[]{:S(2)}) %collective-permute-start.6) | collective-permute-done | bytes 327712 | tf_op jit(solution)/shard_map/ppermute | solution.py:25
  161.1 2.3 %fusion.1 = bf16[256,2560]{1,0:T(8,128)(2,1)} fusion(bf16[5,2560,128]{2,1,0:T(8,128)(2,1)S(1)} %get-tuple-element.70, f32[5,256,128]{2,1,0:T(8,128)S(1)} %convert_add_fusion), kind=kOutput, calls=%fused_computation.3 | convolution fusion | flops 839680000 | bytes 5242880 | tf_op jit(solution)/shard_map/dot_general | solution.py:105
  163.4 3.8 %all-to-all-start.5 = ((bf16[16,16,2560]{2,1,0:T(8,128)(2,1)}), bf16[16,16,2560]{2,1,0:T(8,128)(2,1)S(1)}, u32[]{:S(2)}, u32[]{:S(2)}) async-start(bf16[16,16,2560]{2,1,0:T(8,128)(2,1)} %bitcast.110), calls=%async_computation.5 | async-start | bytes 2621440 | tf_op jit(solution)/shard_map/all_to_all | solution.py:144
  167.3 1.6 constant_dynamic-slice_fusion.1
  168.9 3.5 %collective-permute-start.7 = (bf16[256,1280]{1,0:T(8,128)(2,1)S(1)}, bf16[256,1280]{1,0:T(8,128)(2,1)}, u32[]{:S(2)}, u32[]{:S(2)}) collective-permute-start(bf16[256,1280]{1,0:T(8,128)(2,1)S(1)} %slice.71), channel_id=1, source_target_pairs={{0,1},{1,0},{2,3},{3,2},{4,5},{5,4},{6,7},{7,6},{8,9},{9,8},{10,11... | collective-permute-start | bytes 1966088 | tf_op jit(solution)/shard_map/ppermute | solution.py:25
  172.4 1.6 constant_dynamic-slice_fusion
  174.1 1.7 convolution_bitcast_fusion.8
  175.8 1.7 add_add_fusion
  177.5 4.3 %shard_map.52.refs_0_ = bf16[3,1280,512]{2,1,0:T(8,128)(2,1)} custom-call(s32[1]{0:T(128)} %bitcast.core_ref, bf16[256,2560]{1,0:T(8,128)(2,1)} %bitcast.106, bf16[256,1280]{1,0:T(8,128)(2,1)} %collective-permute-done.7.other_ref, bf16[3,1280,512]{2,1,0:T(8,128)(2,1)} %shard_map.51.refs_0_), custom_call_target="tpu_custom_call", output_to_operand_aliasing={{}: (3, {})} | custom-call | bytes 2621440 | tf_op jit(solution)/shard_map/pallas_call | solution.py:54
  181.9 2.4 %all-to-all-done.5 = bf16[16,16,2560]{2,1,0:T(8,128)(2,1)S(1)} async-done(((bf16[16,16,2560]{2,1,0:T(8,128)(2,1)}), bf16[16,16,2560]{2,1,0:T(8,128)(2,1)S(1)}, u32[]{:S(2)}, u32[]{:S(2)}) %all-to-all-start.5) | async-done | bytes 1310752 | tf_op jit(solution)/shard_map/all_to_all | solution.py:144
  184.3 0.2 reduce_sum.38
  184.5 0.1 broadcast_in_dim.76
  184.6 21.4 %all_to_all.38 = bf16[16,16,2560]{2,1,0:T(8,128)(2,1)S(1)} all-to-all(bf16[16,16,2560]{2,1,0:T(8,128)(2,1)S(1)} %broadcast_in_dim.76), channel_id=1, replica_groups=mesh['row'=16,'col'=8] {'row'}, dimensions={0} | all-to-all | bytes 2621440 | tf_op jit(solution)/shard_map/all_to_all | solution.py:163
  206.0 0.9 convolution_bitcast_fusion.6
  206.9 0.1 copy-done.11
  207.1 3.9 %collective-permute-start.8 = (bf16[256,2560]{1,0:T(8,128)(2,1)S(1)}, bf16[256,2560]{1,0:T(8,128)(2,1)S(1)}, u32[]{:S(2)}, u32[]{:S(2)}) collective-permute-start(bf16[256,2560]{1,0:T(8,128)(2,1)S(1)} %bitcast.114), channel_id=1, source_target_pairs={{0,1},{1,0},{2,3},{3,2},{4,5},{5,4},{6,7},{7,6},{8,9},{9,8},{10,11... | collective-permute-start | bytes 3932168 | tf_op jit(solution)/shard_map/ppermute | solution.py:25
  211.0 1.8 collective-permute-start.10
  212.8 1.8 collective-permute-start.11
  214.6 1.1 copy-done.14
  215.6 4.3 %shard_map.53 = bf16[3,1280,512]{2,1,0:T(8,128)(2,1)} custom-call(s32[1]{0:T(128)} %bitcast.core_ref, bf16[256,2560]{1,0:T(8,128)(2,1)} %bitcast.115, bf16[256,2560]{1,0:T(8,128)(2,1)} %copy-done.14, bf16[3,1280,512]{2,1,0:T(8,128)(2,1)} %shard_map.52.refs_0_), custom_call_target="tpu_custom_call", output_to_operand_aliasing={{}: (3, {})} | custom-call | bytes 2621440 | tf_op jit(solution)/shard_map/pallas_call | solution.py:54
  220.0 1.0 add_subtract_fusion
  221.0 1.8 maximum_bitcast_fusion
  (55 shorter events, 1.0 us)
Async XLA Ops:
  0.6 16.5 %collective-permute-start = (bf16[15,1280,128]{2,1,0:T(8,128)(2,1)}, bf16[15,1280,128]{2,1,0:T(8,128)(2,1)S(1)}, u32[]{:S(2)}, u32[]{:S(2)}) collective-permute-start(bf16[15,1280,128]{2,1,0:T(8,128)(2,1)} %bitcast.94), channel_id=1, source_target_pairs={{0,1},{1,0},{2,3},{3,2},{4,5},{5,4},{6,7},{7,6},{8,9},{9,8},{10,11... | collective-permute-start | bytes 14745608 | tf_op jit(solution)/shard_map/ppermute | solution.py:25
  17.1 2.2 copy-start.8
  20.1 27.9 %collective-permute-start.1 = (bf16[13,384,1280]{2,1,0:T(8,128)(2,1)}, bf16[13,384,1280]{2,1,0:T(8,128)(2,1)}, u32[]{:S(2)}, u32[]{:S(2)}) collective-permute-start(bf16[13,384,1280]{2,1,0:T(8,128)(2,1)} %bitcast.98), channel_id=1, source_target_pairs={{0,1},{1,0},{2,3},{3,2},{4,5},{5,4},{6,7},{7,6},{8,9},{9,8},{10,11... | collective-permute-start | bytes 38338568 | tf_op jit(solution)/shard_map/ppermute | solution.py:25
  49.3 4.7 %copy-start.15 = (f32[64,18,128]{2,0,1:T(8,128)S(1)}, f32[64,18,128]{2,0,1:T(8,128)}, u32[]{:S(2)}) copy-start(f32[64,18,128]{2,0,1:T(8,128)} %param.3) | copy-start | bytes 1769476
  49.3 23.0 %all-to-all-start.2 = ((bf16[16,16,2560]{2,1,0:T(8,128)(2,1)}), bf16[16,16,2560]{2,1,0:T(8,128)(2,1)}, u32[]{:S(2)}, u32[]{:S(2)}) async-start(bf16[16,16,2560]{2,1,0:T(8,128)(2,1)} %broadcast_in_dim.74), calls=%async_computation.2 | async-start | bytes 2621440 | tf_op jit(solution)/shard_map/all_to_all | solution.py:163
  55.7 2.4 %copy-start = (bf16[3,1280,5,128]{3,1,2,0:T(8,128)(2,1)S(1)}, bf16[3,1280,5,128]{3,1,2,0:T(8,128)(2,1)}, u32[]{:S(2)}) copy-start(bf16[3,1280,5,128]{3,1,2,0:T(8,128)(2,1)} %param.5) | copy-start | bytes 14745604
  63.8 1.7 copy-start.1
  65.6 1.7 copy-start.3
  67.2 1.7 copy-start.5
  68.9 1.3 copy-start.6
  76.0 7.2 %collective-permute-start.2 = (bf16[5,256,128]{2,1,0:T(8,128)(2,1)S(1)}, bf16[5,256,128]{2,1,0:T(8,128)(2,1)S(1)}, u32[]{:S(2)}, u32[]{:S(2)}) collective-permute-start(bf16[5,256,128]{2,1,0:T(8,128)(2,1)S(1)} %get-tuple-element.104), channel_id=1, source_target_pairs={{0,2},{1,7},{2,0},{3,5},{4,6},{5,3},{6,4},{7,1},{8,10},{9,15},{10,... | collective-permute-start | bytes 983048 | tf_op jit(solution)/shard_map/ppermute | solution.py:25
  83.2 6.2 %copy-start.2 = (bf16[5,2560,128]{2,1,0:T(8,128)(2,1)S(1)}, bf16[5,2560,128]{2,1,0:T(8,128)(2,1)}, u32[]{:S(2)}) copy-start(bf16[5,2560,128]{2,1,0:T(8,128)(2,1)} %copy-done.1) | copy-start | bytes 9830404
  83.3 6.0 %collective-permute-start.3 = (bf16[5,256,128]{2,1,0:T(8,128)(2,1)S(1)}, bf16[5,256,128]{2,1,0:T(8,128)(2,1)S(1)}, u32[]{:S(2)}, u32[]{:S(2)}) collective-permute-start(bf16[5,256,128]{2,1,0:T(8,128)(2,1)S(1)} %fusion.32), channel_id=1, source_target_pairs={{0,6},{1,3},{2,4},{3,1},{4,2},{5,7},{6,0},{7,5},{8,14},{9,11},{10,... | collective-permute-start | bytes 983048 | tf_op jit(solution)/shard_map/ppermute | solution.py:25
  89.4 2.3 %copy-start.12 = (f32[5,256,128]{2,1,0:T(8,128)}, f32[5,256,128]{2,1,0:T(8,128)S(1)}, u32[]{:S(2)}) copy-start(f32[5,256,128]{2,1,0:T(8,128)S(1)} %convert_add_fusion.2) | copy-start | bytes 1966084
  91.7 25.6 %all-to-all-start.3 = ((bf16[16,16,2560]{2,1,0:T(8,128)(2,1)}), bf16[16,16,2560]{2,1,0:T(8,128)(2,1)}, u32[]{:S(2)}, u32[]{:S(2)}) async-start(bf16[16,16,2560]{2,1,0:T(8,128)(2,1)} %bitcast.111), calls=%async_computation.3 | async-start | bytes 2621440 | tf_op jit(solution)/shard_map/all_to_all | solution.py:144
  98.7 14.4 %collective-permute-start.4 = (bf16[256,1280]{1,0:T(8,128)(2,1)S(1)}, bf16[256,1280]{1,0:T(8,128)(2,1)}, u32[]{:S(2)}, u32[]{:S(2)}) collective-permute-start(bf16[256,1280]{1,0:T(8,128)(2,1)S(1)} %slice.65), channel_id=1, source_target_pairs={{0,1},{1,0},{2,3},{3,2},{4,5},{5,4},{6,7},{7,6},{8,9},{9,8},{10,11... | collective-permute-start | bytes 1966088 | tf_op jit(solution)/shard_map/ppermute | solution.py:25
  118.9 26.7 %copy-start.4 = (bf16[5,128,2560]{2,1,0:T(8,128)(2,1)S(1)}, bf16[5,128,2560]{2,1,0:T(8,128)(2,1)}, u32[]{:S(2)}) copy-start(bf16[5,128,2560]{2,1,0:T(8,128)(2,1)} %copy-done.3) | copy-start | bytes 9830404
  145.6 1.2 copy-start.9
  145.6 1.6 copy-start.18
  147.4 7.2 %collective-permute-start.5 = (bf16[5,256,128]{2,1,0:T(8,128)(2,1)S(1)}, bf16[5,256,128]{2,1,0:T(8,128)(2,1)S(1)}, u32[]{:S(2)}, u32[]{:S(2)}) collective-permute-start(bf16[5,256,128]{2,1,0:T(8,128)(2,1)S(1)} %get-tuple-element.96), channel_id=1, source_target_pairs={{0,2},{1,7},{2,0},{3,5},{4,6},{5,3},{6,4},{7,1},{8,10},{9,15},{10,... | collective-permute-start | bytes 983048 | tf_op jit(solution)/shard_map/ppermute | solution.py:25
  154.7 6.3 %collective-permute-start.6 = (bf16[5,256,128]{2,1,0:T(8,128)(2,1)S(1)}, bf16[5,256,128]{2,1,0:T(8,128)(2,1)S(1)}, u32[]{:S(2)}, u32[]{:S(2)}) collective-permute-start(bf16[5,256,128]{2,1,0:T(8,128)(2,1)S(1)} %fusion.33), channel_id=1, source_target_pairs={{0,6},{1,3},{2,4},{3,1},{4,2},{5,7},{6,0},{7,5},{8,14},{9,11},{10,... | collective-permute-start | bytes 983048 | tf_op jit(solution)/shard_map/ppermute | solution.py:25
  161.1 2.3 %copy-start.13 = (f32[5,256,128]{2,1,0:T(8,128)}, f32[5,256,128]{2,1,0:T(8,128)S(1)}, u32[]{:S(2)}) copy-start(f32[5,256,128]{2,1,0:T(8,128)S(1)} %convert_add_fusion) | copy-start | bytes 1966084
  163.4 5.5 %copy-start.10 = (bf16[16,16,2560]{2,1,0:T(8,128)(2,1)S(1)}, bf16[16,16,2560]{2,1,0:T(8,128)(2,1)}, u32[]{:S(2)}) copy-start(bf16[16,16,2560]{2,1,0:T(8,128)(2,1)} %copy-done.9) | copy-start | bytes 3932164
  163.4 20.9 %all-to-all-start.5 = ((bf16[16,16,2560]{2,1,0:T(8,128)(2,1)}), bf16[16,16,2560]{2,1,0:T(8,128)(2,1)S(1)}, u32[]{:S(2)}, u32[]{:S(2)}) async-start(bf16[16,16,2560]{2,1,0:T(8,128)(2,1)} %bitcast.110), calls=%async_computation.5 | async-start | bytes 2621440 | tf_op jit(solution)/shard_map/all_to_all | solution.py:144
  168.9 6.8 %copy-start.19 = (f32[3,256,128]{2,1,0:T(8,128)S(1)}, f32[3,256,128]{2,1,0:T(8,128)}, u32[]{:S(2)}) copy-start(f32[3,256,128]{2,1,0:T(8,128)} %fusion.16) | copy-start | bytes 1179652
  168.9 8.6 %collective-permute-start.7 = (bf16[256,1280]{1,0:T(8,128)(2,1)S(1)}, bf16[256,1280]{1,0:T(8,128)(2,1)}, u32[]{:S(2)}, u32[]{:S(2)}) collective-permute-start(bf16[256,1280]{1,0:T(8,128)(2,1)S(1)} %slice.71), channel_id=1, source_target_pairs={{0,1},{1,0},{2,3},{3,2},{4,5},{5,4},{6,7},{7,6},{8,9},{9,8},{10,11... | collective-permute-start | bytes 1966088 | tf_op jit(solution)/shard_map/ppermute | solution.py:25
  184.6 21.4 %copy-start.7 = (bf16[3,128,2560]{2,1,0:T(8,128)(2,1)S(1)}, bf16[3,128,2560]{2,1,0:T(8,128)(2,1)}, u32[]{:S(2)}) copy-start(bf16[3,128,2560]{2,1,0:T(8,128)(2,1)} %copy-done.6) | copy-start | bytes 5898244
  206.0 1.1 copy-start.11
  207.1 13.9 %copy-start.16 = (f32[5,64,128]{2,1,0:T(8,128)S(1)}, f32[5,64,128]{2,1,0:T(8,128)}, u32[]{:S(2)}) copy-start(f32[5,64,128]{2,1,0:T(8,128)} %constant_dynamic-slice_fusion.1) | copy-start | bytes 491524
  207.1 13.9 %copy-start.17 = (f32[5,64,128]{2,1,0:T(8,128)S(1)}, f32[5,64,128]{2,1,0:T(8,128)}, u32[]{:S(2)}) copy-start(f32[5,64,128]{2,1,0:T(8,128)} %constant_dynamic-slice_fusion) | copy-start | bytes 491524
  207.1 7.5 %collective-permute-start.8 = (bf16[256,2560]{1,0:T(8,128)(2,1)S(1)}, bf16[256,2560]{1,0:T(8,128)(2,1)S(1)}, u32[]{:S(2)}, u32[]{:S(2)}) collective-permute-start(bf16[256,2560]{1,0:T(8,128)(2,1)S(1)} %bitcast.114), channel_id=1, source_target_pairs={{0,1},{1,0},{2,3},{3,2},{4,5},{5,4},{6,7},{7,6},{8,9},{9,8},{10,11... | collective-permute-start | bytes 3932168 | tf_op jit(solution)/shard_map/ppermute | solution.py:25
  211.0 9.0 %collective-permute-start.10 = (bf16[3,64,128]{2,1,0:T(8,128)(2,1)S(1)}, bf16[3,64,128]{2,1,0:T(8,128)(2,1)S(1)}, u32[]{:S(2)}, u32[]{:S(2)}) collective-permute-start(bf16[3,64,128]{2,1,0:T(8,128)(2,1)S(1)} %get-tuple-element.85), channel_id=1, source_target_pairs={{0,4},{1,5},{2,6},{3,7},{4,0},{5,1},{6,2},{7,3},{8,12},{9,13},{10,... | collective-permute-start | bytes 147464 | tf_op jit(solution)/shard_map/ppermute | solution.py:22
  212.8 7.2 %collective-permute-start.11 = (bf16[3,64,128]{2,1,0:T(8,128)(2,1)S(1)}, bf16[3,64,128]{2,1,0:T(8,128)(2,1)}, u32[]{:S(2)}, u32[]{:S(2)}) collective-permute-start(bf16[3,64,128]{2,1,0:T(8,128)(2,1)S(1)} %get-tuple-element.86), channel_id=1, source_target_pairs={{0,6},{1,7},{2,0},{3,1},{4,2},{5,3},{6,4},{7,5},{8,14},{9,15},{10,... | collective-permute-start | bytes 147464 | tf_op jit(solution)/shard_map/ppermute | solution.py:22
  214.6 5.4 %collective-permute-start.9 = (bf16[3,64,128]{2,1,0:T(8,128)(2,1)S(1)}, bf16[3,64,128]{2,1,0:T(8,128)(2,1)}, u32[]{:S(2)}, u32[]{:S(2)}) collective-permute-start(bf16[3,64,128]{2,1,0:T(8,128)(2,1)S(1)} %get-tuple-element.84), channel_id=1, source_target_pairs={{0,2},{1,3},{2,4},{3,5},{4,6},{5,7},{6,0},{7,1},{8,10},{9,11},{10,... | collective-permute-start | bytes 147464 | tf_op jit(solution)/shard_map/ppermute | solution.py:22
  214.6 1.1 copy-start.14

commit v7 on v6

--- a/solution.py
+++ b/solution.py
@@ -67,8 +67,9 @@
     for n in range(count):
         mine_ref, theirs_ref, out_ref = refs[2 * n], refs[2 * n + 1], refs[2 * count + n]
         rows, lanes = mine_ref.shape[1:]
-        out_ref[0, :rows, :lanes] = mine_ref[0]
-        out_ref[0, -rows:, -lanes:] = theirs_ref[0]
+        at = pl.program_id(0) if out_ref.shape[0] > 1 else 0
+        out_ref[at, :rows, :lanes] = mine_ref[0]
+        out_ref[at, -rows:, -lanes:] = theirs_ref[0]
 
 
 def joined(sources, pieces):
@@ -88,8 +89,12 @@
         moved += 4 * shape[0] * shape[1] * shape[2]
         given += sources[which : which + 2]
         in_specs += [pl.BlockSpec((1, rows, lanes), block)] * 2
-        out_specs.append(pl.BlockSpec((1, shape[1], shape[2]), out_block))
-        shapes.append(jax.ShapeDtypeStruct(tuple(shape), BF16))
+        if shapes:
+            out_specs.append(pl.BlockSpec((1, shape[1], shape[2]), out_block))
+            shapes.append(pltpu.HBM(tuple(shape), BF16))
+        else:
+            out_specs.append(pl.BlockSpec(memory_space=pltpu.VMEM))
+            shapes.append(pltpu.VMEM(tuple(shape), BF16))
     return pl.pallas_call(
         join_kernel,
         grid=(max(piece[2] for piece in pieces),),

time: 224 us -> 222 us (level)
  local copies, waits for them, and re-layouts: 20.3 us -> 16.2 us
  Pallas kernels: 18.8 us -> 22 us
    pallas_call x1, Pallas kernels: 5.75 us -> 9.02 us  [joined(): pl.pallas_call(join_kernel, grid=(max((piece[2] for piece in pieces)),),...]
    unnamed x40 -> x34, local copies, waits for them, and re-layouts: 12.5 us -> 9.4 us
  transfers between devices with their start and end apart: 15 -> 15, of which waited for: 6 -> 6; matrix products, arithmetic and copies ran while one was open for 10% -> 10% of each run, Pallas kernels for 8% -> 10%
where the time goes in v7:
time: 222 us; the launch traced here: 221 us
  blocking collectives  86.1 us (39%)
  starting transfers between devices  33.6 us (15%)
  waiting for transfers between devices  30.8 us (14%)
  matrix products  25.8 us (12%)
  Pallas kernels  22 us (10%)
  local copies, waits for them, and re-layouts  16.2 us (7%)
  other arithmetic  4.92 us (2%)
    all_to_all x2, blocking collectives, local(): solved = lax.all_to_all(copies, 'row', 0, 0, tiled=True)  48.1 us
    all_to_all x1, blocking collectives, local(): lax.all_to_all(products.reshape(n_row, half // n_row, 2 * width), 'row',...  26.3 us
    ppermute x9, waiting for transfers between devices, swap(): lax.ppermute(block, 'col', [(c, c ^ masks[c % 2]) for c in range(self.n_c...  24.6 us
    dot_general x9, matrix products, factor_times(): lax.dot_general(solved, block, (((1,), (2,)), ((), ())), preferred_elemen...  18.3 us
    ppermute x9, starting transfers between devices, swap(): lax.ppermute(block, 'col', [(c, c ^ masks[c % 2]) for c in range(self.n_c...  16.1 us
    pallas_call x3, Pallas kernels, place(): pl.pallas_call(place_kernel, grid=(width // tile,), in_specs=[pl.BlockSpe...  13 us
    all_to_all x1, blocking collectives, local(): lax.all_to_all(copies_of(first, n_z), 'col', 0, 0, tiled=True, axis_index...  11.8 us
    all_to_all x2, starting transfers between devices, local(): lax.all_to_all(products.reshape(n_row, half // n_row, 2 * width), 'row',...  9.42 us
  transfers between devices with their start and end apart: 15, of which 6 were waited for; matrix products, arithmetic and copies ran while one was open for 10% of the time, Pallas kernels for 10%

profile of v7, /device:TPU:1, one launch (start us, length us, event | category | flops | bytes accessed | tf_op | source)
XLA Modules:
  0.0 220.5 jit_solution(8975440725131390859)
XLA Ops:
  0.6 1.5 collective-permute-start
  2.1 0.9 slice.126
  3.1 11.8 %all_to_all.35 = bf16[4,5,64,128]{3,2,1,0:T(8,128)(2,1)S(1)} all-to-all(bf16[4,5,64,128]{3,2,1,0:T(8,128)(2,1)S(1)} %broadcast_in_dim.68), channel_id=1, replica_groups={{0,2,4,6},{1,3,5,7},{8,10,12,14},{9,11,13,15},{16,18,20,22},{17,19,21,2..., dimensions={0} | all-to-all | bytes 655360 | tf_op jit(solution)/shard_map/all_to_all | solution.py:134
  15.0 2.1 fusion.2
  17.1 0.7 fusion.3
  17.9 2.2 copy-done.1
  20.1 1.5 collective-permute-start.1
  21.6 26.3 %all_to_all.36 = bf16[16,16,2560]{2,1,0:T(8,128)(2,1)S(1)} all-to-all(bf16[16,16,2560]{2,1,0:T(8,128)(2,1)S(1)} %bitcast.110), channel_id=1, replica_groups=mesh['row'=16,'col'=8] {'row'}, dimensions={0} | all-to-all | bytes 2621440 | tf_op jit(solution)/shard_map/all_to_all | solution.py:149
  47.9 0.2 reduce_sum.36
  48.0 1.2 broadcast_in_dim.74
  49.3 4.5 %all-to-all-start.2 = ((bf16[16,16,2560]{2,1,0:T(8,128)(2,1)}), bf16[16,16,2560]{2,1,0:T(8,128)(2,1)}, u32[]{:S(2)}, u32[]{:S(2)}) async-start(bf16[16,16,2560]{2,1,0:T(8,128)(2,1)} %broadcast_in_dim.74), calls=%async_computation.2 | async-start | bytes 2621440 | tf_op jit(solution)/shard_map/all_to_all | solution.py:168
  53.9 0.1 broadcast_in_dim.66
  54.0 0.7 fusion.41
  54.7 0.9 bitcast_select_fusion
  55.6 2.4 %copy-done = bf16[3,1280,5,128]{3,1,2,0:T(8,128)(2,1)S(1)} copy-done((bf16[3,1280,5,128]{3,1,2,0:T(8,128)(2,1)S(1)}, bf16[3,1280,5,128]{3,1,2,0:T(8,128)(2,1)}, u32[]{:S(2)}) %copy-start) | copy-done | bytes 4915224
  58.0 2.4 %copy-done.2 = bf16[15,1280,128]{2,1,0:T(8,128)(2,1)S(1)} copy-done((bf16[15,1280,128]{2,1,0:T(8,128)(2,1)S(1)}, bf16[15,1280,128]{2,1,0:T(8,128)(2,1)}, u32[]{:S(2)}) %copy-start.2) | copy-done | bytes 4915224
  60.4 9.0 %shard_map.50 = (bf16[5,128,2560]{2,1,0:T(8,128)(2,1)S(1)}, bf16[5,128,2560]{2,1,0:T(8,128)(2,1)}, bf16[3,128,2560]{2,1,0:T(8,128)(2,1)}, bf16[5,2560,128]{2,1,0:T(8,128)(2,1)}, bf16[5,2560,128]{2,1,0:T(8,128)(2,1)}) custom-call(bf16[13,384,1280]{2,1,0:T(8,128)(2,1)} %bitcast.99, bf16[13,384,1280]{2,1,0:T(8,128)(2,1)} %collective-permute-done.1.refs_1_.refs_3_.refs_5_, ...), custom_call_target="tpu_custom_call" | custom-call | bytes 30146560 | tf_op jit(solution)/shard_map/pallas_call | solution.py:98
  69.4 2.9 %all-to-all-done.2 = bf16[16,16,2560]{2,1,0:T(8,128)(2,1)} async-done(((bf16[16,16,2560]{2,1,0:T(8,128)(2,1)}), bf16[16,16,2560]{2,1,0:T(8,128)(2,1)}, u32[]{:S(2)}, u32[]{:S(2)}) %all-to-all-start.2) | async-done | bytes 1310752 | tf_op jit(solution)/shard_map/all_to_all | solution.py:168
  72.3 2.7 %fusion.42 = (bf16[5,256,128]{2,1,0:T(8,128)(2,1)S(1)}, f32[5,256,128]{2,1,0:T(8,128)S(1)}) fusion(f32[5,256,128]{2,1,0:T(8,128)} %bitcast_select_fusion, bf16[256,2560,1]{1,0,2:T(8,128)(2,1)} %bitcast.16, bf16[5,128,2560]{2,1,0:T(8,128)(2,1)S(1)} %get-tuple-element.63), kind=kOutput, calls=%fused_computation.65 | convolution fusion | flops 839188480 | bytes 6225920 | tf_op jit(solution)/shard_map/dot_general | solution.py:114
  75.0 1.0 collective-permute-start.2
  76.0 6.2 %collective-permute-done.2 = bf16[5,256,128]{2,1,0:T(8,128)(2,1)S(1)} collective-permute-done((bf16[5,256,128]{2,1,0:T(8,128)(2,1)S(1)}, bf16[5,256,128]{2,1,0:T(8,128)(2,1)S(1)}, u32[]{:S(2)}, u32[]{:S(2)}) %collective-permute-start.2) | collective-permute-done | bytes 327712 | tf_op jit(solution)/shard_map/ppermute | solution.py:25
  82.4 5.9 %collective-permute-done.3 = bf16[5,256,128]{2,1,0:T(8,128)(2,1)S(1)} collective-permute-done((bf16[5,256,128]{2,1,0:T(8,128)(2,1)S(1)}, bf16[5,256,128]{2,1,0:T(8,128)(2,1)S(1)}, u32[]{:S(2)}, u32[]{:S(2)}) %collective-permute-start.3) | collective-permute-done | bytes 327712 | tf_op jit(solution)/shard_map/ppermute | solution.py:25
  88.3 0.1 convert_add_fusion.2
  88.4 2.3 %fusion = bf16[256,2560]{1,0:T(8,128)(2,1)} fusion(bf16[5,2560,128]{2,1,0:T(8,128)(2,1)S(1)} %copy-done.7, f32[5,256,128]{2,1,0:T(8,128)S(1)} %convert_add_fusion.2), kind=kOutput, calls=%fused_computation.2 | convolution fusion | flops 839680000 | bytes 5242880 | tf_op jit(solution)/shard_map/dot_general | solution.py:110
  90.7 5.7 %all-to-all-start.3 = ((bf16[16,16,2560]{2,1,0:T(8,128)(2,1)}), bf16[16,16,2560]{2,1,0:T(8,128)(2,1)S(1)}, u32[]{:S(2)}, u32[]{:S(2)}) async-start(bf16[16,16,2560]{2,1,0:T(8,128)(2,1)} %bitcast.19), calls=%async_computation.3 | async-start | bytes 2621440 | tf_op jit(solution)/shard_map/all_to_all | solution.py:149
  96.4 1.1 slice.65
  97.6 3.6 %collective-permute-start.4 = (bf16[256,1280]{1,0:T(8,128)(2,1)S(1)}, bf16[256,1280]{1,0:T(8,128)(2,1)S(1)}, u32[]{:S(2)}, u32[]{:S(2)}) collective-permute-start(bf16[256,1280]{1,0:T(8,128)(2,1)S(1)} %slice.65), channel_id=1, source_target_pairs={{0,1},{1,0},{2,3},{3,2},{4,5},{5,4},{6,7},{7,6},{8,9},{9,8},{10,11... | collective-permute-start | bytes 1966088 | tf_op jit(solution)/shard_map/ppermute | solution.py:25
  101.2 1.9 fusion.19
  103.1 2.7 %fusion.16 = f32[3,256,128]{2,1,0:T(8,128)} fusion(f32[256,3,128]{2,0,1:T(8,128)S(1)} %fusion.19, bf16[13,384,1280]{2,1,0:T(8,128)(2,1)} %collective-permute-done.1.refs_1_.refs_3_.refs_5_, bf16[256,2560]{1,0:T(8,128)(2,1)} %bitcast.15.own_ref), kind=kOutput, calls=%fused_computation.24 | convolution fusion | flops 251756544 | bytes 2424832 | tf_op jit(solution)/shard_map/dot_general | solution.py:114
  105.8 2.3 %fusion.5 = f32[256,5,128]{2,0,1:T(8,128)S(1)} fusion(bf16[13,384,1280]{2,1,0:T(8,128)(2,1)} %bitcast.103, bf16[256,2560]{1,0:T(8,128)(2,1)} %bitcast.15.own_ref), kind=kOutput, calls=%fused_computation.10 | convolution fusion | flops 419430400 | bytes 2949120 | tf_op jit(solution)/shard_map/dot_general | solution.py:114
  108.1 3.2 %fusion.12 = f32[5,256,128]{2,1,0:T(8,128)} fusion(f32[256,5,128]{2,0,1:T(8,128)S(1)} %fusion.5, bf16[13,384,1280]{2,1,0:T(8,128)(2,1)} %collective-permute-done.1.refs_1_.refs_3_.refs_5_, bf16[256,2560]{1,0:T(8,128)(2,1)} %bitcast.15.own_ref), kind=kOutput, calls=%fused_computation.18 | convolution fusion | flops 419594240 | bytes 3604480 | tf_op jit(solution)/shard_map/dot_general | solution.py:114
  111.3 0.9 copy-done.10
  112.2 4.3 %shard_map.51.refs_0_ = bf16[3,1280,512]{2,1,0:T(8,128)(2,1)} custom-call(s32[1]{0:T(128)} %bitcast.core_ref, bf16[256,2560]{1,0:T(8,128)(2,1)} %bitcast.15.own_ref, bf16[256,1280]{1,0:T(8,128)(2,1)} %copy-done.10), custom_call_target="tpu_custom_call" | custom-call | bytes 2621440 | tf_op jit(solution)/shard_map/pallas_call | solution.py:54
  116.5 0.2 reduce_sum.37
  116.7 0.1 broadcast_in_dim.75
  116.9 26.6 %all_to_all.37 = bf16[16,16,2560]{2,1,0:T(8,128)(2,1)S(1)} all-to-all(bf16[16,16,2560]{2,1,0:T(8,128)(2,1)S(1)} %broadcast_in_dim.75), channel_id=1, replica_groups=mesh['row'=16,'col'=8] {'row'}, dimensions={0} | all-to-all | bytes 2621440 | tf_op jit(solution)/shard_map/all_to_all | solution.py:168
  143.5 1.2 convolution_bitcast_fusion.4
  144.7 0.4 copy-done.13
  145.1 0.2 fusion.39
  145.3 1.0 collective-permute-start.5
  146.3 6.2 %collective-permute-done.5 = bf16[5,256,128]{2,1,0:T(8,128)(2,1)S(1)} collective-permute-done((bf16[5,256,128]{2,1,0:T(8,128)(2,1)S(1)}, bf16[5,256,128]{2,1,0:T(8,128)(2,1)S(1)}, u32[]{:S(2)}, u32[]{:S(2)}) %collective-permute-start.5) | collective-permute-done | bytes 327712 | tf_op jit(solution)/shard_map/ppermute | solution.py:25
  152.7 6.2 %collective-permute-done.6 = bf16[5,256,128]{2,1,0:T(8,128)(2,1)S(1)} collective-permute-done((bf16[5,256,128]{2,1,0:T(8,128)(2,1)S(1)}, bf16[5,256,128]{2,1,0:T(8,128)(2,1)S(1)}, u32[]{:S(2)}, u32[]{:S(2)}) %collective-permute-start.6) | collective-permute-done | bytes 327712 | tf_op jit(solution)/shard_map/ppermute | solution.py:25
  158.9 0.1 convert_add_fusion
  159.0 2.3 %fusion.1 = bf16[256,2560]{1,0:T(8,128)(2,1)} fusion(bf16[5,2560,128]{2,1,0:T(8,128)(2,1)S(1)} %copy-done.6, f32[5,256,128]{2,1,0:T(8,128)S(1)} %convert_add_fusion), kind=kOutput, calls=%fused_computation.3 | convolution fusion | flops 839680000 | bytes 5242880 | tf_op jit(solution)/shard_map/dot_general | solution.py:110
  161.3 3.7 %all-to-all-start.5 = ((bf16[16,16,2560]{2,1,0:T(8,128)(2,1)}), bf16[16,16,2560]{2,1,0:T(8,128)(2,1)S(1)}, u32[]{:S(2)}, u32[]{:S(2)}) async-start(bf16[16,16,2560]{2,1,0:T(8,128)(2,1)} %bitcast.28), calls=%async_computation.5 | async-start | bytes 2621440 | tf_op jit(solution)/shard_map/all_to_all | solution.py:149
  165.1 0.7 constant_dynamic-slice_fusion.1
  165.8 3.5 %collective-permute-start.7 = (bf16[256,1280]{1,0:T(8,128)(2,1)S(1)}, bf16[256,1280]{1,0:T(8,128)(2,1)}, u32[]{:S(2)}, u32[]{:S(2)}) collective-permute-start(bf16[256,1280]{1,0:T(8,128)(2,1)S(1)} %slice.71), channel_id=1, source_target_pairs={{0,1},{1,0},{2,3},{3,2},{4,5},{5,4},{6,7},{7,6},{8,9},{9,8},{10,11... | collective-permute-start | bytes 1966088 | tf_op jit(solution)/shard_map/ppermute | solution.py:25
  169.3 1.6 constant_dynamic-slice_fusion
  170.9 1.7 convolution_bitcast_fusion.8
  172.6 1.7 add_add_fusion
  174.4 4.3 %shard_map.52.refs_0_ = bf16[3,1280,512]{2,1,0:T(8,128)(2,1)} custom-call(s32[1]{0:T(128)} %bitcast.core_ref, bf16[256,2560]{1,0:T(8,128)(2,1)} %bitcast.109, bf16[256,1280]{1,0:T(8,128)(2,1)} %collective-permute-done.7.other_ref, bf16[3,1280,512]{2,1,0:T(8,128)(2,1)} %shard_map.51.refs_0_), custom_call_target="tpu_custom_call", output_to_operand_aliasing={{}: (3, {})} | custom-call | bytes 2621440 | tf_op jit(solution)/shard_map/pallas_call | solution.py:54
  178.7 3.3 %all-to-all-done.5 = bf16[16,16,2560]{2,1,0:T(8,128)(2,1)S(1)} async-done(((bf16[16,16,2560]{2,1,0:T(8,128)(2,1)}), bf16[16,16,2560]{2,1,0:T(8,128)(2,1)S(1)}, u32[]{:S(2)}, u32[]{:S(2)}) %all-to-all-start.5) | async-done | bytes 1310752 | tf_op jit(solution)/shard_map/all_to_all | solution.py:149
  182.1 0.2 reduce_sum.38
  182.2 0.1 broadcast_in_dim.76
  182.4 21.4 %all_to_all.38 = bf16[16,16,2560]{2,1,0:T(8,128)(2,1)S(1)} all-to-all(bf16[16,16,2560]{2,1,0:T(8,128)(2,1)S(1)} %broadcast_in_dim.76), channel_id=1, replica_groups=mesh['row'=16,'col'=8] {'row'}, dimensions={0} | all-to-all | bytes 2621440 | tf_op jit(solution)/shard_map/all_to_all | solution.py:168
  203.8 0.9 convolution_bitcast_fusion.6
  204.8 0.1 copy-done.4
  204.9 3.9 %collective-permute-start.8 = (bf16[256,2560]{1,0:T(8,128)(2,1)S(1)}, bf16[256,2560]{1,0:T(8,128)(2,1)S(1)}, u32[]{:S(2)}, u32[]{:S(2)}) collective-permute-start(bf16[256,2560]{1,0:T(8,128)(2,1)S(1)} %bitcast.112), channel_id=1, source_target_pairs={{0,1},{1,0},{2,3},{3,2},{4,5},{5,4},{6,7},{7,6},{8,9},{9,8},{10,11... | collective-permute-start | bytes 3932168 | tf_op jit(solution)/shard_map/ppermute | solution.py:25
  208.8 1.8 collective-permute-start.10
  210.5 1.8 collective-permute-start.11
  212.3 1.1 copy-done.8
  213.4 4.3 %shard_map.53 = bf16[3,1280,512]{2,1,0:T(8,128)(2,1)} custom-call(s32[1]{0:T(128)} %bitcast.core_ref, bf16[256,2560]{1,0:T(8,128)(2,1)} %bitcast.113, bf16[256,2560]{1,0:T(8,128)(2,1)} %copy-done.8, bf16[3,1280,512]{2,1,0:T(8,128)(2,1)} %shard_map.52.refs_0_), custom_call_target="tpu_custom_call", output_to_operand_aliasing={{}: (3, {})} | custom-call | bytes 2621440 | tf_op jit(solution)/shard_map/pallas_call | solution.py:54
  217.8 1.0 add_subtract_fusion
  218.8 1.8 maximum_bitcast_fusion
  (49 shorter events, 0.8 us)
Async XLA Ops:
  0.6 16.5 %collective-permute-start = (bf16[15,1280,128]{2,1,0:T(8,128)(2,1)}, bf16[15,1280,128]{2,1,0:T(8,128)(2,1)S(1)}, u32[]{:S(2)}, u32[]{:S(2)}) collective-permute-start(bf16[15,1280,128]{2,1,0:T(8,128)(2,1)} %bitcast.94), channel_id=1, source_target_pairs={{0,1},{1,0},{2,3},{3,2},{4,5},{5,4},{6,7},{7,6},{8,9},{9,8},{10,11... | collective-permute-start | bytes 14745608 | tf_op jit(solution)/shard_map/ppermute | solution.py:25
  17.9 2.2 copy-start.1
  20.1 27.9 %collective-permute-start.1 = (bf16[13,384,1280]{2,1,0:T(8,128)(2,1)}, bf16[13,384,1280]{2,1,0:T(8,128)(2,1)}, u32[]{:S(2)}, u32[]{:S(2)}) collective-permute-start(bf16[13,384,1280]{2,1,0:T(8,128)(2,1)} %bitcast.98), channel_id=1, source_target_pairs={{0,1},{1,0},{2,3},{3,2},{4,5},{5,4},{6,7},{7,6},{8,9},{9,8},{10,11... | collective-permute-start | bytes 38338568 | tf_op jit(solution)/shard_map/ppermute | solution.py:25
  49.3 4.7 %copy-start.9 = (f32[64,18,128]{2,0,1:T(8,128)S(1)}, f32[64,18,128]{2,0,1:T(8,128)}, u32[]{:S(2)}) copy-start(f32[64,18,128]{2,0,1:T(8,128)} %param.3) | copy-start | bytes 1769476
  49.3 23.0 %all-to-all-start.2 = ((bf16[16,16,2560]{2,1,0:T(8,128)(2,1)}), bf16[16,16,2560]{2,1,0:T(8,128)(2,1)}, u32[]{:S(2)}, u32[]{:S(2)}) async-start(bf16[16,16,2560]{2,1,0:T(8,128)(2,1)} %broadcast_in_dim.74), calls=%async_computation.2 | async-start | bytes 2621440 | tf_op jit(solution)/shard_map/all_to_all | solution.py:168
  55.6 2.4 %copy-start = (bf16[3,1280,5,128]{3,1,2,0:T(8,128)(2,1)S(1)}, bf16[3,1280,5,128]{3,1,2,0:T(8,128)(2,1)}, u32[]{:S(2)}) copy-start(bf16[3,1280,5,128]{3,1,2,0:T(8,128)(2,1)} %param.5) | copy-start | bytes 14745604
  58.0 2.4 %copy-start.2 = (bf16[15,1280,128]{2,1,0:T(8,128)(2,1)S(1)}, bf16[15,1280,128]{2,1,0:T(8,128)(2,1)}, u32[]{:S(2)}) copy-start(bf16[15,1280,128]{2,1,0:T(8,128)(2,1)} %copy-done.1) | copy-start | bytes 14745604
  75.0 7.2 %collective-permute-start.2 = (bf16[5,256,128]{2,1,0:T(8,128)(2,1)S(1)}, bf16[5,256,128]{2,1,0:T(8,128)(2,1)S(1)}, u32[]{:S(2)}, u32[]{:S(2)}) collective-permute-start(bf16[5,256,128]{2,1,0:T(8,128)(2,1)S(1)} %get-tuple-element.104), channel_id=1, source_target_pairs={{0,2},{1,7},{2,0},{3,5},{4,6},{5,3},{6,4},{7,1},{8,10},{9,15},{10,... | collective-permute-start | bytes 983048 | tf_op jit(solution)/shard_map/ppermute | solution.py:25
  82.2 6.2 %copy-start.7 = (bf16[5,2560,128]{2,1,0:T(8,128)(2,1)S(1)}, bf16[5,2560,128]{2,1,0:T(8,128)(2,1)}, u32[]{:S(2)}) copy-start(bf16[5,2560,128]{2,1,0:T(8,128)(2,1)} %get-tuple-element.64) | copy-start | bytes 9830404
  82.3 6.0 %collective-permute-start.3 = (bf16[5,256,128]{2,1,0:T(8,128)(2,1)S(1)}, bf16[5,256,128]{2,1,0:T(8,128)(2,1)S(1)}, u32[]{:S(2)}, u32[]{:S(2)}) collective-permute-start(bf16[5,256,128]{2,1,0:T(8,128)(2,1)S(1)} %fusion.32), channel_id=1, source_target_pairs={{0,6},{1,3},{2,4},{3,1},{4,2},{5,7},{6,0},{7,5},{8,14},{9,11},{10,... | collective-permute-start | bytes 983048 | tf_op jit(solution)/shard_map/ppermute | solution.py:25
  90.7 25.8 %all-to-all-start.3 = ((bf16[16,16,2560]{2,1,0:T(8,128)(2,1)}), bf16[16,16,2560]{2,1,0:T(8,128)(2,1)S(1)}, u32[]{:S(2)}, u32[]{:S(2)}) async-start(bf16[16,16,2560]{2,1,0:T(8,128)(2,1)} %bitcast.19), calls=%async_computation.3 | async-start | bytes 2621440 | tf_op jit(solution)/shard_map/all_to_all | solution.py:149
  97.6 13.7 %collective-permute-start.4 = (bf16[256,1280]{1,0:T(8,128)(2,1)S(1)}, bf16[256,1280]{1,0:T(8,128)(2,1)S(1)}, u32[]{:S(2)}, u32[]{:S(2)}) collective-permute-start(bf16[256,1280]{1,0:T(8,128)(2,1)S(1)} %slice.65), channel_id=1, source_target_pairs={{0,1},{1,0},{2,3},{3,2},{4,5},{5,4},{6,7},{7,6},{8,9},{9,8},{10,11... | collective-permute-start | bytes 1966088 | tf_op jit(solution)/shard_map/ppermute | solution.py:25
  111.3 0.9 copy-start.10
  116.7 26.8 %copy-start.15 = (bf16[5,128,2560]{2,1,0:T(8,128)(2,1)S(1)}, bf16[5,128,2560]{2,1,0:T(8,128)(2,1)}, u32[]{:S(2)}) copy-start(bf16[5,128,2560]{2,1,0:T(8,128)(2,1)} %get-tuple-element.68) | copy-start | bytes 9830404
  143.5 29.1 %copy-start.3 = (bf16[16,16,2560]{2,1,0:T(8,128)(2,1)}, bf16[16,16,2560]{2,1,0:T(8,128)(2,1)S(1)}, u32[]{:S(2)}) copy-start(bf16[16,16,2560]{2,1,0:T(8,128)(2,1)S(1)} %all_to_all.37) | copy-start | bytes 3932164
  143.5 1.6 copy-start.13
  145.3 7.2 %collective-permute-start.5 = (bf16[5,256,128]{2,1,0:T(8,128)(2,1)S(1)}, bf16[5,256,128]{2,1,0:T(8,128)(2,1)S(1)}, u32[]{:S(2)}, u32[]{:S(2)}) collective-permute-start(bf16[5,256,128]{2,1,0:T(8,128)(2,1)S(1)} %get-tuple-element.96), channel_id=1, source_target_pairs={{0,2},{1,7},{2,0},{3,5},{4,6},{5,3},{6,4},{7,1},{8,10},{9,15},{10,... | collective-permute-start | bytes 983048 | tf_op jit(solution)/shard_map/ppermute | solution.py:25
  152.5 6.5 %copy-start.6 = (bf16[5,2560,128]{2,1,0:T(8,128)(2,1)S(1)}, bf16[5,2560,128]{2,1,0:T(8,128)(2,1)}, u32[]{:S(2)}) copy-start(bf16[5,2560,128]{2,1,0:T(8,128)(2,1)} %get-tuple-element.70) | copy-start | bytes 9830404
  152.6 6.3 %collective-permute-start.6 = (bf16[5,256,128]{2,1,0:T(8,128)(2,1)S(1)}, bf16[5,256,128]{2,1,0:T(8,128)(2,1)S(1)}, u32[]{:S(2)}, u32[]{:S(2)}) collective-permute-start(bf16[5,256,128]{2,1,0:T(8,128)(2,1)S(1)} %fusion.33), channel_id=1, source_target_pairs={{0,6},{1,3},{2,4},{3,1},{4,2},{5,7},{6,0},{7,5},{8,14},{9,11},{10,... | collective-permute-start | bytes 983048 | tf_op jit(solution)/shard_map/ppermute | solution.py:25
  159.0 2.3 %copy-start.5 = (f32[5,256,128]{2,1,0:T(8,128)}, f32[5,256,128]{2,1,0:T(8,128)S(1)}, u32[]{:S(2)}) copy-start(f32[5,256,128]{2,1,0:T(8,128)S(1)} %convert_add_fusion) | copy-start | bytes 1966084
  161.3 20.8 %all-to-all-start.5 = ((bf16[16,16,2560]{2,1,0:T(8,128)(2,1)}), bf16[16,16,2560]{2,1,0:T(8,128)(2,1)S(1)}, u32[]{:S(2)}, u32[]{:S(2)}) async-start(bf16[16,16,2560]{2,1,0:T(8,128)(2,1)} %bitcast.28), calls=%async_computation.5 | async-start | bytes 2621440 | tf_op jit(solution)/shard_map/all_to_all | solution.py:149
  165.8 6.8 %copy-start.14 = (f32[3,256,128]{2,1,0:T(8,128)S(1)}, f32[3,256,128]{2,1,0:T(8,128)}, u32[]{:S(2)}) copy-start(f32[3,256,128]{2,1,0:T(8,128)} %fusion.16) | copy-start | bytes 1179652
  165.8 8.6 %collective-permute-start.7 = (bf16[256,1280]{1,0:T(8,128)(2,1)S(1)}, bf16[256,1280]{1,0:T(8,128)(2,1)}, u32[]{:S(2)}, u32[]{:S(2)}) collective-permute-start(bf16[256,1280]{1,0:T(8,128)(2,1)S(1)} %slice.71), channel_id=1, source_target_pairs={{0,1},{1,0},{2,3},{3,2},{4,5},{5,4},{6,7},{7,6},{8,9},{9,8},{10,11... | collective-permute-start | bytes 1966088 | tf_op jit(solution)/shard_map/ppermute | solution.py:25
  182.4 21.4 %copy-start.16 = (bf16[3,128,2560]{2,1,0:T(8,128)(2,1)S(1)}, bf16[3,128,2560]{2,1,0:T(8,128)(2,1)}, u32[]{:S(2)}) copy-start(bf16[3,128,2560]{2,1,0:T(8,128)(2,1)} %get-tuple-element.77) | copy-start | bytes 5898244
  203.8 1.1 copy-start.4
  204.9 13.9 %copy-start.11 = (f32[5,64,128]{2,1,0:T(8,128)S(1)}, f32[5,64,128]{2,1,0:T(8,128)}, u32[]{:S(2)}) copy-start(f32[5,64,128]{2,1,0:T(8,128)} %constant_dynamic-slice_fusion.1) | copy-start | bytes 491524
  204.9 13.9 %copy-start.12 = (f32[5,64,128]{2,1,0:T(8,128)S(1)}, f32[5,64,128]{2,1,0:T(8,128)}, u32[]{:S(2)}) copy-start(f32[5,64,128]{2,1,0:T(8,128)} %constant_dynamic-slice_fusion) | copy-start | bytes 491524
  204.9 7.5 %collective-permute-start.8 = (bf16[256,2560]{1,0:T(8,128)(2,1)S(1)}, bf16[256,2560]{1,0:T(8,128)(2,1)S(1)}, u32[]{:S(2)}, u32[]{:S(2)}) collective-permute-start(bf16[256,2560]{1,0:T(8,128)(2,1)S(1)} %bitcast.112), channel_id=1, source_target_pairs={{0,1},{1,0},{2,3},{3,2},{4,5},{5,4},{6,7},{7,6},{8,9},{9,8},{10,11... | collective-permute-start | bytes 3932168 | tf_op jit(solution)/shard_map/ppermute | solution.py:25
  208.8 9.0 %collective-permute-start.10 = (bf16[3,64,128]{2,1,0:T(8,128)(2,1)S(1)}, bf16[3,64,128]{2,1,0:T(8,128)(2,1)S(1)}, u32[]{:S(2)}, u32[]{:S(2)}) collective-permute-start(bf16[3,64,128]{2,1,0:T(8,128)(2,1)S(1)} %get-tuple-element.85), channel_id=1, source_target_pairs={{0,4},{1,5},{2,6},{3,7},{4,0},{5,1},{6,2},{7,3},{8,12},{9,13},{10,... | collective-permute-start | bytes 147464 | tf_op jit(solution)/shard_map/ppermute | solution.py:22
  210.5 7.2 %collective-permute-start.11 = (bf16[3,64,128]{2,1,0:T(8,128)(2,1)S(1)}, bf16[3,64,128]{2,1,0:T(8,128)(2,1)}, u32[]{:S(2)}, u32[]{:S(2)}) collective-permute-start(bf16[3,64,128]{2,1,0:T(8,128)(2,1)S(1)} %get-tuple-element.86), channel_id=1, source_target_pairs={{0,6},{1,7},{2,0},{3,1},{4,2},{5,3},{6,4},{7,5},{8,14},{9,15},{10,... | collective-permute-start | bytes 147464 | tf_op jit(solution)/shard_map/ppermute | solution.py:22
  212.3 5.4 %collective-permute-start.9 = (bf16[3,64,128]{2,1,0:T(8,128)(2,1)S(1)}, bf16[3,64,128]{2,1,0:T(8,128)(2,1)}, u32[]{:S(2)}, u32[]{:S(2)}) collective-permute-start(bf16[3,64,128]{2,1,0:T(8,128)(2,1)S(1)} %get-tuple-element.84), channel_id=1, source_target_pairs={{0,2},{1,3},{2,4},{3,5},{4,6},{5,7},{6,0},{7,1},{8,10},{9,11},{10,... | collective-permute-start | bytes 147464 | tf_op jit(solution)/shard_map/ppermute | solution.py:22
  212.3 1.1 copy-start.8
